TPU v7x, 32 devices: a whole 2x2x4 slice. The times are simulated.
32 devices in a mesh: band: 4 (over y, x), bl: 8 (over z, core).
Axes of the slice: x: 2, y: 2, z: 4, core: 2. Of those that a mesh axis runs over, the one named last changes fastest.
Arguments:
- visibilities: bfloat16 [4096, 8, 2, 1024], P('bl', None, None, 'band'), may hold values from -400 to 400
- send_order: int32 [8, 512], P('bl'), may hold values from 0 to 511, each once within a row
- channel_flags: int32 [1024], replicated, may hold values 0 or 1
- group_ids: int32 [4096], P(('band', 'bl')), may hold values from 0 to 15, as said below
- pair_list: int32 [8192, 2], P(('band', 'bl')), may hold values from 0 to 255, as said below
Outputs:
- group_power: float32 [512, 1024], P(('band', 'bl'))
Inputs may be any that keep to these rules, and one draw needn't show every extreme that they name: `send_order`: row j lists each of the 512 baselines of bl block j once; positions d * 16 to (d + 1) * 16 - 1 name those that owner d receives. `group_ids`: among the 128 baselines of one owner, each group id is held by exactly 8 of them. `pair_list`: in each row (i, j) of an owner's 256 pairs, i is a local baseline; j below 128 is a local baseline, j of 128 or more is baseline j - 128 of the owner one step lower along band (cyclically); j != i; every group of the owner has at least one pair whose i lies in it.
All inputs are finite; a program needn't handle non-finite values.
Results may differ from a plain program's by a relative error of at most 0.0065.
Values may be sent and summed in bfloat16 or wider, within the bound.
No kernel may reach another device: no remote copies, remote signals or barrier semaphores. Data moves between devices by JAX's collectives and lax.ppermute only.
A program may use at most 128 MiB of HBM per device.

v0:
```python
import math

import jax
import jax.numpy as jnp
from jax import lax
from jax.sharding import PartitionSpec as P

GRP_DEV = 16


def shifted(value, axis, steps):
    count = lax.axis_size(axis)
    pairs = [(source, (source + steps) % count) for source in range(count)]
    return lax.ppermute(value, axis, pairs)


def delay_matrix(full_width):
    index = jnp.arange(full_width, dtype=jnp.int32)
    phase = index[:, None] * index[None, :] % full_width
    angle = phase.astype(jnp.float32) * (2.0 * math.pi / full_width)
    cosine = jnp.cos(angle)
    sine = jnp.sin(angle)
    upper = jnp.concatenate([cosine, -sine], axis=1)
    lower = jnp.concatenate([sine, cosine], axis=1)
    return jnp.concatenate([upper, lower], axis=0).astype(jnp.bfloat16)


def channel_weights(channel_flags):
    width = channel_flags.shape[0]
    angle = jnp.arange(width, dtype=jnp.float32) * (2.0 * math.pi / width)
    taper = (
        0.35875
        - 0.48829 * jnp.cos(angle)
        + 0.14128 * jnp.cos(2.0 * angle)
        - 0.01168 * jnp.cos(3.0 * angle)
    )
    weights = taper * channel_flags.astype(jnp.float32)
    return jnp.concatenate([weights, weights], axis=0)


def group_spectra(own_rows, previous, pair_list, group_ids):
    window = jnp.concatenate([own_rows, previous], axis=0)
    slots = window.shape[1] * window.shape[2]
    energy = (
        jnp.einsum("btc,btc->b", window, window, preferred_element_type=jnp.float32) / slots + 1e-06
    )
    first = pair_list[:, 0]
    second = pair_list[:, 1]
    left = jnp.take(window, first, axis=0)
    right = jnp.take(window, second, axis=0)
    product = jnp.einsum("ptc,ptc->pc", left, right, preferred_element_type=jnp.float32)
    half = product.shape[1] // 2
    cross = product[:, :half] + product[:, half:]
    scale = energy[first] * energy[second]
    power = cross / jnp.sqrt(scale)[:, None]
    weight = 1.0 / scale
    member = (group_ids[first][None, :] == jnp.arange(GRP_DEV, dtype=jnp.int32)[:, None]).astype(
        jnp.float32
    )
    numer = jnp.dot(member, weight[:, None] * power, precision=lax.Precision.HIGHEST)
    denom = jnp.dot(member, weight, precision=lax.Precision.HIGHEST)
    return numer / denom[:, None]


def on_device(visibilities, send_order, channel_flags, group_ids, pair_list):
    band_count = lax.axis_size("band")
    block_count = lax.axis_size("bl")
    device_count = band_count * block_count
    block_rows, time_count, part_count, sub_width = visibilities.shape
    full_width = sub_width * band_count
    owned_rows = block_rows // band_count
    peer_rows = owned_rows // block_count
    matrix = delay_matrix(full_width)
    weights = channel_weights(channel_flags)
    chosen = jnp.take(visibilities, send_order[0], axis=0)
    chosen = chosen.reshape(device_count, peer_rows, time_count, part_count, sub_width)
    received = lax.all_to_all(chosen, ("band", "bl"), split_axis=0, concat_axis=0, tiled=True)
    time_slots = received.shape[2]
    ordered = received.reshape(
        band_count, block_count, peer_rows, time_slots, part_count, sub_width
    )
    ordered = ordered.transpose(1, 2, 3, 4, 0, 5).reshape(
        owned_rows * time_slots, part_count * full_width
    )
    tapered = (ordered.astype(jnp.float32) * weights[None, :]).astype(jnp.bfloat16)
    spectra = jnp.dot(tapered, matrix, preferred_element_type=jnp.float32).astype(jnp.bfloat16)
    spectra = spectra.reshape(owned_rows, time_slots, part_count * full_width)
    previous = shifted(spectra, "band", 1)
    return group_spectra(spectra, previous, pair_list, group_ids)


def solution(mesh):
    return jax.shard_map(
        on_device,
        mesh=mesh,
        in_specs=(
            P("bl", None, None, "band"),
            P("bl", None),
            P(),
            P(("band", "bl")),
            P(("band", "bl"), None),
        ),
        out_specs=P(("band", "bl"), None),
        check_vma=False,
    )
```

profile of v0, /device:TPU:0, one launch (start us, length us, event | category | flops | bytes accessed | tf_op | source)
XLA Modules:
  0.0 334.2 jit_solution(13439338997021286694)
XLA Ops:
  0.0 0.0 copy-start
  0.0 0.7 compare_select_fusion.1
  0.7 0.5 broadcast.105
  1.2 1.3 reduce.7
  2.6 0.1 squeeze.11
  2.7 20.9 %gather_fusion.1 = bf16[512,8,2,256]{3,2,1,0:T(2,128)(2,1)} fusion(bf16[512,8,2,256]{3,2,1,0:T(2,128)(2,1)} %param.7, s32[1024]{0:T(1024)S(1)} %pad_clamp_fusion.4), kind=kCustom, calls=%fused_computation.3 | custom fusion | bytes 8390656 | tf_op jit(solution)/shard_map/jit(_take)/gather | solution.py:75
  23.5 2.9 copy.6
  26.5 2.3 broadcast_select_fusion
  28.8 0.0 copy-start.1
  28.8 7.6 %all-to-all-start = ((bf16[32,16,8,2,256]{4,2,3,1,0:T(8,128)(2,1)}), bf16[32,16,8,2,256]{4,2,3,1,0:T(8,128)(2,1)}, u32[]{:S(2)}, u32[]{:S(2)}) async-start(bf16[32,16,8,2,256]{4,2,3,1,0:T(8,128)(2,1)} %broadcast_select_fusion), calls=%async_computation | async-start | bytes 8388608 | tf_op jit(solution)/shard_map/all_to_all | solution.py:77
  36.4 0.0 copy-done.1
  36.4 0.1 fusion.33
  36.4 15.7 %fusion.20 = bf16[1024,1024]{1,0:T(8,128)(2,1)S(1)} fusion(), kind=kLoop, calls=%fused_computation.36 | loop fusion | flops 15728640 | bytes 2097152 | tf_op jit(solution)/shard_map/convert.5
  52.1 17.8 %negate_convert_fusion = (bf16[1024,1024]{1,0:T(8,128)(2,1)}, bf16[1024,1024]{1,0:T(8,128)(2,1)}) fusion(), kind=kLoop, calls=%fused_computation.28 | loop fusion | flops 17825792 | bytes 4194304 | tf_op jit(solution)/shard_map/convert.8
  70.0 61.5 %all-to-all-done = bf16[32,16,8,2,256]{4,2,3,1,0:T(8,128)(2,1)} async-done(((bf16[32,16,8,2,256]{4,2,3,1,0:T(8,128)(2,1)}), bf16[32,16,8,2,256]{4,2,3,1,0:T(8,128)(2,1)}, u32[]{:S(2)}, u32[]{:S(2)}) %all-to-all-start) | async-done | bytes 4194336 | tf_op jit(solution)/shard_map/all_to_all | solution.py:77
  131.4 6.6 %convert_bitcast_fusion = f32[8,16,8,2,4,256]{5,2,3,1,0,4:T(8,128)} fusion(bf16[4,8,16,8,2,256]{5,3,4,2,1,0:T(8,128)(2,1)} %bitcast.17), kind=kLoop, calls=%fused_computation.19 | loop fusion | flops 2097152 | bytes 12582912 | tf_op jit(solution)/shard_map/convert_element_type | solution.py:85
  138.0 14.9 %copy.7 = f32[8,16,8,2,4,256]{5,4,3,2,1,0:T(4,128)} copy(f32[8,16,8,2,4,256]{5,2,3,1,0,4:T(8,128)} %convert_bitcast_fusion) | data formatting | bytes 16777216 | tf_op jit(solution)/shard_map/convert_element_type | solution.py:85
  152.8 10.9 %reshape.67 = f32[1024,2048]{1,0:T(8,128)} reshape(f32[8,16,8,2,4,256]{5,4,3,2,1,0:T(4,128)} %copy.7) | data formatting | bytes 16777216 | tf_op jit(solution)/shard_map/convert_element_type | solution.py:85
  163.8 0.0 copy-start.2
  163.8 20.4 %convert_bitcast_fusion.1 = bf16[128,8,2048]{2,1,0:T(8,128)(2,1)} fusion(bf16[1024,1024]{1,0:T(8,128)(2,1)} %get-tuple-element.14, bf16[1024,1024]{1,0:T(8,128)(2,1)S(1)} %fusion.20, bf16[1024,1024]{1,0:T(8,128)(2,1)} %get-tuple-element.13, f32[1024,2048]{1,0:T(8,128)} %reshape.67, f32[2048]{0:T(1024)S(1)} %pad_maximum_fusion.1), kind=kOutput, calls=%fused_computation.27 | convolution fusion | flops 8629780480 | bytes 18882560 | tf_op jit(solution)/shard_map/dot_general | solution.py:86
  184.2 0.0 collective-permute-start
  184.2 0.0 copy-done.2
  184.2 0.0 copy-done
  184.3 2.1 gather_fusion
  186.5 91.1 %collective-permute-done = bf16[128,8,2048]{2,1,0:T(8,128)(2,1)} collective-permute-done((bf16[128,8,2048]{2,1,0:T(8,128)(2,1)}, bf16[128,8,2048]{2,1,0:T(8,128)(2,1)}, u32[]{:S(2)}, u32[]{:S(2)}) %collective-permute-start) | collective-permute-done | bytes 4194336 | tf_op jit(solution)/shard_map/ppermute | solution.py:14
  277.5 6.3 %fusion.1 = f32[256]{0:T(256)S(1)} fusion(bf16[128,8,2048]{2,1,0:T(8,128)(2,1)} %collective-permute-done, bf16[128,8,2048]{2,1,0:T(8,128)(2,1)} %convert_bitcast_fusion.1), kind=kLoop, calls=%fused_computation.9 | loop fusion | flops 16776960 | bytes 8389632 | tf_op jit(solution)/shard_map/btc,btc->b/dot_general | solution.py:45
  283.9 1.9 gather_fusion.3
  285.8 1.9 gather_fusion.2
  287.8 7.4 %pad_maximum_fusion = bf16[256,8,2048]{2,1,0:T(8,128)(2,1)} fusion(bf16[128,8,2048]{2,1,0:T(8,128)(2,1)} %collective-permute-done, bf16[128,8,2048]{2,1,0:T(8,128)(2,1)} %convert_bitcast_fusion.1), kind=kLoop, calls=%fused_computation.18 | loop fusion | flops 4194304 | bytes 16777216 | tf_op jit(solution)/shard_map/concatenate | solution.py:42
  295.2 12.0 %gather_fusion.4 = bf16[256,8,2048]{2,1,0:T(8,128)(2,1)} fusion(bf16[256,8,2048]{2,1,0:T(8,128)(2,1)} %pad_maximum_fusion, s32[1024]{0:T(1024)S(1)} %pad_clamp_fusion.1), kind=kCustom, calls=%fused_computation.clone | custom fusion | bytes 16778240 | tf_op jit(solution)/shard_map/jit(_take)/gather | solution.py:49
  307.2 12.0 %gather_fusion.5 = bf16[256,8,2048]{2,1,0:T(8,128)(2,1)} fusion(bf16[256,8,2048]{2,1,0:T(8,128)(2,1)} %pad_maximum_fusion, s32[1024]{0:T(1024)S(1)} %pad_clamp_fusion), kind=kCustom, calls=%fused_computation.1.clone | custom fusion | bytes 16778240 | tf_op jit(solution)/shard_map/jit(_take)/gather | solution.py:50
  319.2 0.1 convolution_bitcast_fusion
  319.3 13.2 %fusion = f32[256,2048]{1,0:T(8,128)S(1)} fusion(bf16[256,8,2048]{2,1,0:T(8,128)(2,1)} %gather_fusion.5, bf16[256,8,2048]{2,1,0:T(8,128)(2,1)} %gather_fusion.4, pred[256]{0:T(512)(128)(4,1)S(1)} %get-tuple-element.15, pred[256]{0:T(512)(128)(4,1)S(1)} %get-tuple-element.16), kind=kLoop, calls=%fused_computation.7 | loop fusion | flops 24641536 | bytes 18874880 | tf_op jit(solution)/shard_map/ptc,ptc->pc/dot_general | solution.py:51
  332.5 1.3 convolution_divide_fusion
  (14 shorter events, 0.1 us)
Async XLA Ops:
  0.0 184.2 %copy-start = (s32[128]{0:T(128)S(1)}, s32[128]{0:T(128)}, u32[]{:S(2)}) copy-start(s32[128]{0:T(128)} %param.10) | copy-start | bytes 1540
  28.8 7.6 %copy-start.1 = (s32[1024]{0:T(1024)S(1)}, s32[1024]{0:T(1024)}, u32[]{:S(2)}) copy-start(s32[1024]{0:T(1024)} %param.9) | copy-start | bytes 12292
  28.8 102.7 %all-to-all-start = ((bf16[32,16,8,2,256]{4,2,3,1,0:T(8,128)(2,1)}), bf16[32,16,8,2,256]{4,2,3,1,0:T(8,128)(2,1)}, u32[]{:S(2)}, u32[]{:S(2)}) async-start(bf16[32,16,8,2,256]{4,2,3,1,0:T(8,128)(2,1)} %broadcast_select_fusion), calls=%async_computation | async-start | bytes 8388608 | tf_op jit(solution)/shard_map/all_to_all | solution.py:77
  163.8 20.5 %copy-start.2 = (s32[256,2]{0,1:T(2,128)S(1)}, s32[256,2]{0,1:T(2,128)}, u32[]{:S(2)}) copy-start(s32[256,2]{0,1:T(2,128)} %param.11) | copy-start | bytes 6148
  184.2 93.3 %collective-permute-start = (bf16[128,8,2048]{2,1,0:T(8,128)(2,1)}, bf16[128,8,2048]{2,1,0:T(8,128)(2,1)}, u32[]{:S(2)}, u32[]{:S(2)}) collective-permute-start(bf16[128,8,2048]{2,1,0:T(8,128)(2,1)} %convert_bitcast_fusion.1), channel_id=1, source_target_pairs={{0,8},{8,16},{16,24},{24,0},{1,9},{9,17},{17,25},{25,1},{2,10},{10... | collective-permute-start | bytes 12582920 | tf_op jit(solution)/shard_map/ppermute | solution.py:14
where the time goes:
time: 339 us; the launch traced here: 334 us
  waiting for transfers between devices  153 us (45%)
  local copies, waits for them, and re-layouts  80.2 us (24%)
  other arithmetic  71.4 us (21%)
  matrix products  21.8 us (6%)
  starting transfers between devices  7.6 us (2%)
    ppermute x1, waiting for transfers between devices, shifted(): return lax.ppermute(value, axis, pairs)  91.1 us
    all_to_all x1, waiting for transfers between devices, on_device(): lax.all_to_all(chosen, ('band', 'bl'), split_axis=0, concat_axis=0, tiled...  61.5 us
    another operation x2, other arithmetic  33.5 us
    convert_element_type x2, local copies, waits for them, and re-layouts, on_device(): ordered.astype(jnp.float32) * weights[None, :]  25.8 us
    gather x2, local copies, waits for them, and re-layouts, on_device(): chosen = jnp.take(visibilities, send_order[0], axis=0)  23.8 us
    dot_general x1, matrix products, on_device(): jnp.dot(tapered, matrix, preferred_element_type=jnp.float32)  20.4 us
    dot_general x1, other arithmetic, group_spectra(): jnp.einsum('ptc,ptc->pc', left, right, preferred_element_type=jnp.float32)  13.2 us
    gather x1, local copies, waits for them, and re-layouts, group_spectra(): left = jnp.take(window, first, axis=0)  12 us
  transfers between devices with their start and end apart: 2, of which 2 were waited for; matrix products, arithmetic and copies ran while one was open for 11% of the time, Pallas kernels for 0%

commit v1 on v0

v1 whole, which is shorter than its diff:
```python
import functools
import math

import jax
import jax.numpy as jnp
import ml_dtypes
import numpy as np
from jax import lax
from jax.experimental import pallas as pl
from jax.experimental.pallas import tpu as pltpu
from jax.sharding import PartitionSpec as P

GRP_DEV = 16
LANES = 128
ENERGY_PARTS = 3
EXTRA_ROWS = 16
HIGHEST = lax.Precision.HIGHEST
VMEM_LIMIT = 20 * 1024 * 1024
F32 = jnp.float32
BF16 = jnp.bfloat16
VMEM = pl.BlockSpec(memory_space=pltpu.VMEM)
SMEM = pl.BlockSpec(memory_space=pltpu.SMEM)


def shifted(value, axis, steps):
    count = lax.axis_size(axis)
    pairs = [(source, (source + steps) % count) for source in range(count)]
    return lax.ppermute(value, axis, pairs)


def spread(pieces):
    return [pieces[0]] + [shifted(pieces[s], "band", s) for s in range(1, len(pieces))]


def cost(flops, bytes_accessed):
    return pl.CostEstimate(flops=flops, bytes_accessed=bytes_accessed, transcendentals=0)


def params():
    return pltpu.CompilerParams(vmem_limit_bytes=VMEM_LIMIT)


def class_matrices(full_width, classes):
    sub = full_width // classes
    channel = np.arange(sub)[None, :, None]
    delay = classes * np.arange(sub)[None, None, :] + np.arange(classes)[:, None, None]
    angle = (channel * delay % full_width) * (2.0 * math.pi / full_width)
    cosine, sine = np.cos(angle), np.sin(angle)
    upper = np.concatenate([cosine, -sine], axis=2)
    lower = np.concatenate([sine, cosine], axis=2)
    return np.concatenate([upper, lower], axis=1).astype(ml_dtypes.bfloat16)


def channel_weights(channel_flags):
    width = channel_flags.shape[0]
    angle = jnp.arange(width, dtype=F32) * (2.0 * math.pi / width)
    taper = (
        0.35875
        - 0.48829 * jnp.cos(angle)
        + 0.14128 * jnp.cos(2.0 * angle)
        - 0.01168 * jnp.cos(3.0 * angle)
    )
    return taper * channel_flags.astype(F32)


def taper_kernel(split, first_time, me_ref, order_ref, weight_ref, vis_ref, *refs):
    out_refs, energy_ref, wide_ref = refs[:-2], refs[-2], refs[-1]
    rows, parts, times, sub = vis_ref.shape
    count = times // 2
    me = me_ref[0]
    pick = (lax.broadcasted_iota(jnp.int32, (rows, rows), 1) == order_ref[...]).astype(BF16)
    total = jnp.zeros((rows, sub), F32)
    for part in range(parts):
        lanes = slice(part * sub, (part + 1) * sub)
        wide = vis_ref[:, part].astype(F32).reshape(rows * times, sub)
        for c in range(wide_ref.shape[0]):
            wide_ref[c] = wide[:, c * LANES : (c + 1) * LANES]
        for s in range(count):
            time = first_time + lax.rem(me + s, count)
            here = [wide_ref[c, pl.ds(time, rows, stride=times), :] for c in range(wide_ref.shape[0])]
            here = jnp.concatenate(here, axis=1).astype(BF16)
            moved = jnp.dot(pick, here, preferred_element_type=F32)
            tapered = (moved * weight_ref[...]).astype(BF16)
            if split:
                out_refs[s][:, lanes] = tapered
            else:
                blocks = out_refs[0].shape[0]
                out_refs[0][:, s, :, lanes] = tapered.reshape(blocks, rows // blocks, sub)
            square = tapered.astype(F32)
            total = total + square * square
    energy_ref[...] = lax.dot_general(
        jnp.ones((8, sub), F32),
        total,
        (((1,), (1,)), ((), ())),
        precision=HIGHEST,
        preferred_element_type=F32,
    )


def taper(split, first_time, blocks, me, order, weight, vis):
    rows, parts, times, sub = vis.shape
    count, lanes = times // 2, parts * sub
    if split:
        outs = [jax.ShapeDtypeStruct((rows, lanes), BF16)] * count
    else:
        outs = [jax.ShapeDtypeStruct((blocks, count, rows // blocks, lanes), BF16)]
    outs = outs + [jax.ShapeDtypeStruct((8, rows), F32)]
    return pl.pallas_call(
        functools.partial(taper_kernel, split, first_time),
        out_shape=outs,
        in_specs=[SMEM, VMEM, VMEM, VMEM],
        out_specs=[VMEM] * len(outs),
        scratch_shapes=[pltpu.VMEM((sub // LANES, rows * times, LANES), F32)],
        compiler_params=params(),
        cost_estimate=cost(2 * count * rows * rows * lanes, 4 * count * rows * lanes),
        name="taper_rows",
    )(me, order, weight, vis)


def delay_kernel(me_ref, matrix_ref, *refs):
    x_refs, out_refs, mixed = refs[:4], refs[4:8], refs[8]
    half = x_refs[0].shape[1] // 2
    me = me_ref[0]
    x = [ref[...].astype(F32) for ref in x_refs]
    a, b, c, d = x[0] + x[2], x[0] - x[2], x[1] + x[3], x[1] - x[3]
    turned = jnp.concatenate([-d[:, half:], d[:, :half]], axis=1)
    for r, value in enumerate((a + c, b + turned, a - c, b - turned)):
        if r:
            turns = lax.rem(r * me, 4)
            real = jnp.where(turns == 0, 1.0, jnp.where(turns == 2, -1.0, 0.0)).astype(F32)
            imag = jnp.where(turns == 3, 1.0, jnp.where(turns == 1, -1.0, 0.0)).astype(F32)
            if r == 2:
                value = value * real
            else:
                other = jnp.concatenate([-value[:, half:], value[:, :half]], axis=1)
                value = value * real + other * imag
        mixed[r] = value.astype(BF16)
    for s in range(4):
        r = lax.rem(me + s, 4)
        out_refs[s][...] = jnp.dot(mixed[r], matrix_ref[r], preferred_element_type=F32).astype(BF16)


def delay_transform(me, matrices, pieces):
    rows, lanes = pieces[0].shape
    block = min(rows, 256)
    tile = pl.BlockSpec((block, lanes), lambda i: (i, 0))
    return pl.pallas_call(
        delay_kernel,
        grid=(rows // block,),
        out_shape=[jax.ShapeDtypeStruct((rows, lanes), BF16)] * 4,
        in_specs=[SMEM, pl.BlockSpec(matrices.shape, lambda i: (0, 0, 0))] + [tile] * 4,
        out_specs=[tile] * 4,
        scratch_shapes=[pltpu.VMEM((4, block, lanes), BF16)],
        compiler_params=params(),
        cost_estimate=cost(8 * rows * lanes * lanes, 16 * rows * lanes + matrices.size * 2),
        name="delay_transform",
    )(me, matrices, *pieces)


def pair_weights_kernel(first_ref, second_ref, energy_ref, slot_ref, high_ref, low_ref, group_ref):
    rows = energy_ref.shape[1]
    pairs = first_ref.shape[1]
    place = lax.broadcasted_iota(jnp.int32, (rows, pairs), 0)
    contract_last = (((1,), (1,)), ((), ()))
    counts = lax.dot_general(
        (place == first_ref[...]).astype(BF16),
        (place == second_ref[...]).astype(BF16),
        contract_last,
        preferred_element_type=F32,
    )
    inverse = 1.0 / energy_ref[...]
    scale = inverse * jnp.sqrt(inverse)
    weighted = counts * scale
    high = weighted.astype(BF16)
    high_ref[...] = high
    low_ref[...] = (weighted - high.astype(F32)).astype(BF16)
    partner = lax.dot_general(
        jnp.broadcast_to(inverse, (8, rows)),
        counts,
        contract_last,
        precision=HIGHEST,
        preferred_element_type=F32,
    )[0:1]
    slots = group_ref.shape[0]
    member = lax.broadcasted_iota(jnp.int32, (slots, rows), 0) == slot_ref[...]
    denom = jnp.sum(jnp.where(member, inverse * partner, 0.0), axis=1, keepdims=True)
    group_ref[...] = jnp.where(member, scale, 0.0) / denom


def pair_weights(first, second, energy, slot, slots):
    rows = energy.shape[1]
    return pl.pallas_call(
        pair_weights_kernel,
        out_shape=[
            jax.ShapeDtypeStruct((rows, rows), BF16),
            jax.ShapeDtypeStruct((rows, rows), BF16),
            jax.ShapeDtypeStruct((slots, rows), F32),
        ],
        in_specs=[VMEM] * 4,
        out_specs=[VMEM] * 3,
        compiler_params=params(),
        cost_estimate=cost(2 * rows * rows * first.shape[1], 4 * rows * rows),
        name="pair_weights",
    )(first, second, energy, slot)


def pair_kernel(packed, count, high_ref, low_ref, group_ref, *refs):
    z_refs, out_ref = refs[:-1], refs[-1]
    block = high_ref.shape[0]
    rows = high_ref.shape[1]
    lanes = z_refs[0].shape[-1]
    step = pl.program_id(0)
    start = pl.multiple_of(step * block, block)
    total = jnp.zeros((block, lanes), F32)
    for t in range(count):
        if packed:
            per = rows // z_refs[0].shape[0]
            here = slice(t * per, (t + 1) * per)
            window = z_refs[0][:, here].reshape(rows, lanes)
            own = z_refs[0][pl.ds(step * (block // per), block // per), here].reshape(block, lanes)
        else:
            window = z_refs[t][...]
            own = z_refs[t][pl.ds(start, block), :]
        mixed = jnp.dot(high_ref[...], window, preferred_element_type=F32)
        mixed = mixed + jnp.dot(low_ref[...], window, preferred_element_type=F32)
        total = total + own.astype(F32) * mixed
    half = lanes // 2
    cross = total[:, :half] + total[:, half:]
    part = jnp.dot(group_ref[...], cross, precision=HIGHEST, preferred_element_type=F32)

    @pl.when(step == 0)
    def _():
        out_ref[...] = part

    @pl.when(step > 0)
    def _():
        out_ref[...] += part


def pair_sums(packed, count, high, low, group, pieces):
    rows = high.shape[1]
    slots = group.shape[0]
    lanes = pieces[0].shape[-1]
    block = min(rows, 256)
    whole = [pl.BlockSpec(p.shape, lambda i, n=p.ndim: (0,) * n) for p in pieces]
    return pl.pallas_call(
        functools.partial(pair_kernel, packed, count),
        grid=(rows // block,),
        out_shape=jax.ShapeDtypeStruct((slots, lanes // 2), F32),
        in_specs=[
            pl.BlockSpec((block, rows), lambda i: (i, 0)),
            pl.BlockSpec((block, rows), lambda i: (i, 0)),
            pl.BlockSpec((slots, block), lambda i: (0, i)),
        ]
        + whole,
        out_specs=pl.BlockSpec((slots, lanes // 2), lambda i: (0, 0)),
        compiler_params=params(),
        cost_estimate=cost(4 * count * rows * rows * lanes, 2 * count * rows * lanes),
        name="pair_sums",
    )(high, low, group, *pieces)


def interleave_kernel(me_ref, *refs):
    pieces, out_ref = refs[:-1], refs[-1]
    count = len(pieces)
    width = pieces[0].shape[1]
    me = me_ref[0]
    row = lax.broadcasted_iota(jnp.int32, (width, count * width), 0)
    column = lax.broadcasted_iota(jnp.int32, (width, count * width), 1)
    total = jnp.zeros(out_ref.shape, F32)
    for s in range(count):
        r = lax.rem(me + count - s, count)
        pick = (column == row * count + r).astype(F32)
        total = total + jnp.dot(pieces[s][...], pick, precision=HIGHEST, preferred_element_type=F32)
    out_ref[...] = total


def interleave(me, pieces):
    groups, width = pieces[0].shape
    return pl.pallas_call(
        interleave_kernel,
        out_shape=jax.ShapeDtypeStruct((groups, width * len(pieces)), F32),
        in_specs=[SMEM] + [VMEM] * len(pieces),
        out_specs=VMEM,
        compiler_params=params(),
        name="interleave_delays",
    )(me, *pieces)


def window_places(pair_list, owner, block_count, peer, band_count):
    owned = block_count * peer
    local = pair_list % owned
    source = jnp.where(pair_list < owned, owner, (owner + band_count - 1) % band_count)
    return (local // peer) * (band_count * peer) + source * peer + local % peer


def assemble_kernel(energy_ref, *refs):
    pieces, out_ref = refs[:-1], refs[-1]
    blocks, height, lanes = out_ref.shape
    per = pieces[0].shape[0] // blocks
    for t, piece in enumerate(pieces):
        out_ref[:, t * per : (t + 1) * per] = piece[...].reshape(blocks, per, lanes)
    extra = height - per * len(pieces)
    row = lax.broadcasted_iota(jnp.int32, (blocks, extra, lanes), 1)
    rest = jnp.broadcast_to(energy_ref[...], (blocks, extra, lanes))
    block = jnp.zeros((blocks, extra, lanes), F32)
    for k in range(ENERGY_PARTS):
        part = rest.astype(BF16).astype(F32)
        block = jnp.where(row == k, part, block)
        rest = rest - part
    out_ref[:, per * len(pieces) :] = block.astype(BF16)


def assemble(energy, blocks, pieces):
    rows, lanes = pieces[0].shape
    energy = energy.reshape(blocks, 1, rows // blocks)
    energy = jnp.pad(energy, ((0, 0), (0, 0), (0, lanes - rows // blocks)))
    height = len(pieces) * (rows // blocks) + EXTRA_ROWS
    return pl.pallas_call(
        assemble_kernel,
        out_shape=jax.ShapeDtypeStruct((blocks, height, lanes), BF16),
        in_specs=[VMEM] * (1 + len(pieces)),
        out_specs=VMEM,
        compiler_params=params(),
        cost_estimate=cost(rows * lanes, 4 * len(pieces) * rows * lanes),
        name="assemble",
    )(energy, *pieces)


def on_device(matrices, visibilities, send_order, channel_flags, group_ids, pair_list):
    band_count = lax.axis_size("band")
    block_count = lax.axis_size("bl")
    rows, times, parts, sub = visibilities.shape
    peer = rows // (band_count * block_count)
    column = band_count * peer
    lanes = parts * sub
    band = lax.axis_index("band").astype(jnp.int32)
    me = band.reshape(1)

    order = send_order[0].reshape(band_count, block_count, peer).transpose(1, 0, 2).reshape(rows, 1)
    weight = lax.dynamic_slice(channel_weights(channel_flags), (band * sub,), (sub,))
    weight = weight.reshape(1, sub)
    vis = visibilities.transpose(0, 2, 1, 3)

    *late, energy_late = taper(True, times // 2, block_count, me, order, weight, vis)
    late, vis = lax.optimization_barrier((late, vis))
    first_half, energy_first = taper(False, 0, block_count, me, order, weight, vis)

    energy = sum(spread([energy_first[0] + energy_late[0]] * band_count))

    tables = spread([jnp.concatenate([pair_list.reshape(-1), group_ids])] * band_count)
    owners = [(band + band_count - s) % band_count for s in range(band_count)]
    place = jnp.concatenate(
        [
            window_places(table[: pair_list.size].reshape(-1, 2), owner, block_count, peer, band_count)
            for table, owner in zip(tables, owners)
        ]
    ).T
    slot = jnp.zeros((block_count, band_count, peer), jnp.int32)
    for s, (table, owner) in enumerate(zip(tables, owners)):
        groups = table[pair_list.size :].reshape(block_count, 1, peer)
        groups = groups + GRP_DEV * ((band_count - s) % band_count)
        slot = jnp.where(jnp.arange(band_count)[None, :, None] == owner, groups, slot)

    early = lax.all_to_all(first_half, "bl", split_axis=0, concat_axis=0, tiled=True)
    late = spread(delay_transform(me, matrices, spread(late)))
    late = assemble(energy, block_count, late)
    late = lax.all_to_all(late, "bl", split_axis=0, concat_axis=0, tiled=True)

    early = [early[:, s].reshape(rows, lanes) for s in range(band_count)]
    early = spread(delay_transform(me, matrices, spread(early)))

    energy = late[:, band_count * column :][:, :ENERGY_PARTS, :column].astype(F32).sum(axis=1)
    energy = energy.reshape(1, rows) / (parts * times) + 1e-06
    high, low, group = pair_weights(
        place[0:1], place[1:2], energy, slot.reshape(1, rows), GRP_DEV * band_count
    )
    sums = pair_sums(True, band_count, high, low, group, [late])
    sums = sums + pair_sums(False, band_count, high, low, group, early)
    sums = sums.reshape(band_count, GRP_DEV, sub)
    return interleave(me, spread([sums[s] for s in range(band_count)]))


def solution(mesh):
    band_count = mesh.shape["band"]

    def whole(visibilities, send_order, channel_flags, group_ids, pair_list):
        full_width = visibilities.shape[3]
        matrices = jnp.asarray(class_matrices(full_width, band_count))
        mapped = jax.shard_map(
            on_device,
            mesh=mesh,
            in_specs=(
                P(),
                P("bl", None, None, "band"),
                P("bl", None),
                P(),
                P(("band", "bl")),
                P(("band", "bl"), None),
            ),
            out_specs=P(("band", "bl"), None),
            check_vma=False,
        )
        return mapped(matrices, visibilities, send_order, channel_flags, group_ids, pair_list)

    return whole
```

time: 339 us -> 171 us (0.50); the launches traced: 334 us -> 171 us
  other arithmetic: 71.4 us -> 2.35 us
  waiting for transfers between devices: 153 us -> 84.5 us
  local copies, waits for them, and re-layouts: 80.2 us -> 14.2 us
  starting transfers between devices: 7.6 us -> 39.7 us
  Pallas kernels: 0 us -> 29.7 us
  matrix products: 21.8 us -> 0 us
    gather x7 -> x0, local copies, waits for them, and re-layouts: 53.8 us -> none  [the longest x2 23.8 us: on_device(): chosen = jnp.take(visibilities, send_order[0], axis=0)]
    all_to_all x1 -> x2, waiting for transfers between devices: 61.5 us -> 9.78 us  [the longest x1 9.78 us: on_device(): late = lax.all_to_all(late, 'bl', split_axis=0, concat_axis=0, tiled=True)]
    another operation x2 -> x0, other arithmetic: 33.5 us -> none
    pallas_call x0 -> x9, Pallas kernels: none -> 29.7 us  [the longest x2 9.5 us: pair_sums(): pl.pallas_call(functools.partial(pair_kernel, packed, count), grid=(rows...]
    ppermute x1 -> x21, starting transfers between devices: 0.01 us -> 28.3 us  [shifted(): return lax.ppermute(value, axis, pairs)]
    convert_element_type x2 -> x0, local copies, waits for them, and re-layouts: 25.8 us -> none  [on_device(): ordered.astype(jnp.float32) * weights[None, :]]
    dot_general x3 -> x0, matrix products: 21.8 us -> none  [the longest x1 20.4 us: on_device(): jnp.dot(tapered, matrix, preferred_element_type=jnp.float32)]
    dot_general x2 -> x0, other arithmetic: 19.5 us -> none  [the longest x1 13.2 us: group_spectra(): jnp.einsum('ptc,ptc->pc', left, right, preferred_element_type=jnp.float32)]
  transfers between devices with their start and end apart: 2 -> 23, of which waited for: 2 -> 14; matrix products, arithmetic and copies ran while one was open for 11% -> 2% of each run, Pallas kernels for 0% -> 9%
where the time goes in v1:
time: 171 us
  waiting for transfers between devices  84.5 us (49%)
  starting transfers between devices  39.7 us (23%)
  Pallas kernels  29.7 us (17%)
  local copies, waits for them, and re-layouts  14.2 us (8%)
  other arithmetic  2.35 us (1%)
    ppermute x21, waiting for transfers between devices, shifted(): return lax.ppermute(value, axis, pairs)  74.7 us
    ppermute x21, starting transfers between devices, shifted(): return lax.ppermute(value, axis, pairs)  28.3 us
    unnamed x20, local copies, waits for them, and re-layouts  10.8 us
    all_to_all x1, waiting for transfers between devices, on_device(): late = lax.all_to_all(late, 'bl', split_axis=0, concat_axis=0, tiled=True)  9.78 us
    pallas_call x2, Pallas kernels, pair_sums(): pl.pallas_call(functools.partial(pair_kernel, packed, count), grid=(rows...  9.5 us
    pallas_call x2, Pallas kernels, taper(): pl.pallas_call(functools.partial(taper_kernel, split, first_time), out_sh...  7.06 us
    all_to_all x1, starting transfers between devices, on_device(): lax.all_to_all(first_half, 'bl', split_axis=0, concat_axis=0, tiled=True)  6.46 us
    pallas_call x2, Pallas kernels, delay_transform(): pl.pallas_call(delay_kernel, grid=(rows // block,), out_shape=[jax.ShapeD...  5.45 us
  transfers between devices with their start and end apart: 23, of which 14 were waited for; matrix products, arithmetic and copies ran while one was open for 2% of the time, Pallas kernels for 9%

profile of v1, /device:TPU:0, one launch (start us, length us, event | category | flops | bytes accessed | tf_op | source)
XLA Modules:
  0.0 170.7 jit_solution(1406076335588389953)
XLA Ops:
  0.0 0.7 fusion.5
  0.8 4.9 %copy.28 = bf16[512,8,2,256]{3,1,2,0:T(8,128)(2,1)} copy(bf16[512,8,2,256]{3,2,1,0:T(2,128)(2,1)} %param.6) | data formatting | bytes 8388608 | tf_op args[0]
  5.7 0.5 broadcast.171
  6.2 0.7 reduce.3
  6.8 0.1 reshape_squeeze.15
  6.9 0.2 reshape.253.order_ref
  7.2 2.2 %copy-done = bf16[512,8,2,256]{3,1,2,0:T(8,128)(2,1)S(1)} copy-done((bf16[512,8,2,256]{3,1,2,0:T(8,128)(2,1)S(1)}, bf16[512,8,2,256]{3,1,2,0:T(8,128)(2,1)}, u32[]{:S(2)}) %copy-start) | copy-done | bytes 4194328
  9.4 3.5 %taper_rows.2 = (bf16[512,512]{1,0:T(8,128)(2,1)S(1)}, bf16[512,512]{1,0:T(8,128)(2,1)S(1)}, bf16[512,512]{1,0:T(8,128)(2,1)S(1)}, bf16[512,512]{1,0:T(8,128)(2,1)S(1)}, f32[8,512]{1,0:T(8,128)S(1)}) custom-call(s32[1]{0:T(128)} %bitcast.me_ref, s32[512,1]{1,0:T(8,128)S(1)} %reshape.253.order_ref, f32[1,256]{1,0:T(1,128)S(1)} %bitcast.18, ...), custom_call_target="tpu_custom_call" | custom-call | flops 1073741824 | bytes 4194304 | tf_op jit(solution)/shard_map/taper_rows/pallas_call | solution.py:108
  12.8 0.8 copy-done.3
  13.7 0.8 copy-done.4
  14.5 3.6 %taper_rows.3 = (bf16[8,4,64,512]{3,2,1,0:T(8,128)(2,1)S(1)}, f32[8,512]{1,0:T(8,128)S(1)}) custom-call(s32[1]{0:T(128)} %bitcast.me_ref, s32[512,1]{1,0:T(8,128)S(1)} %reshape.253.order_ref, f32[1,256]{1,0:T(1,128)S(1)} %bitcast.19, bf16[512,2,8,256]{3,2,1,0:T(8,128)(2,1)S(1)} %bitcast.16), custom_call_target="tpu_custom_call" | custom-call | flops 1073741824 | bytes 4194304 | tf_op jit(solution)/shard_map/taper_rows/pallas_call | solution.py:108
  18.1 1.4 copy-done.2
  19.5 6.5 %all-to-all-start.1 = ((bf16[8,4,64,512]{3,2,1,0:T(8,128)(2,1)}), bf16[8,4,64,512]{3,2,1,0:T(8,128)(2,1)}, u32[]{:S(2)}, u32[]{:S(2)}) async-start(bf16[8,4,64,512]{3,2,1,0:T(8,128)(2,1)} %copy-done.2), calls=%async_computation.1 | async-start | bytes 4194304 | tf_op jit(solution)/shard_map/all_to_all | solution.py:365
  25.9 1.5 collective-permute-start.6
  27.4 1.5 collective-permute-start.7
  28.9 1.4 collective-permute-start.8
  30.4 11.4 %collective-permute-done.6.refs_1_ = bf16[512,512]{1,0:T(8,128)(2,1)S(1)} collective-permute-done((bf16[512,512]{1,0:T(8,128)(2,1)}, bf16[512,512]{1,0:T(8,128)(2,1)S(1)}, u32[]{:S(2)}, u32[]{:S(2)}) %collective-permute-start.6) | collective-permute-done | bytes 524320 | tf_op jit(solution)/shard_map/ppermute | solution.py:28
  41.8 10.8 %collective-permute-done.7.refs_2_ = bf16[512,512]{1,0:T(8,128)(2,1)S(1)} collective-permute-done((bf16[512,512]{1,0:T(8,128)(2,1)}, bf16[512,512]{1,0:T(8,128)(2,1)S(1)}, u32[]{:S(2)}, u32[]{:S(2)}) %collective-permute-start.7) | collective-permute-done | bytes 524320 | tf_op jit(solution)/shard_map/ppermute | solution.py:28
  52.6 0.1 collective-permute-done.8.refs_3_
  52.7 2.8 %delay_transform.2 = (bf16[512,512]{1,0:T(8,128)(2,1)S(1)}, bf16[512,512]{1,0:T(8,128)(2,1)}, bf16[512,512]{1,0:T(8,128)(2,1)}, bf16[512,512]{1,0:T(8,128)(2,1)}) custom-call(s32[1]{0:T(128)} %bitcast.me_ref, bf16[4,512,512]{2,1,0:T(8,128)(2,1)S(1)} %copy-done.1, bf16[512,512]{1,0:T(8,128)(2,1)S(1)} %get-tuple-element.35.refs_0_, ...), custom_call_target="tpu_custom_call" | custom-call | flops 1073741824 | bytes 6291456 | tf_op jit(solution)/shard_map/delay_transform/pallas_call | solution.py:147
  55.5 1.4 collective-permute-start.10
  56.9 1.7 %collective-permute-start.11 = (bf16[512,512]{1,0:T(8,128)(2,1)}, bf16[512,512]{1,0:T(8,128)(2,1)}, u32[]{:S(2)}, u32[]{:S(2)}) collective-permute-start(bf16[512,512]{1,0:T(8,128)(2,1)} %get-tuple-element.42), channel_id=1, source_target_pairs={{0,24},{8,0},{16,8},{24,16},{1,25},{9,1},{17,9},{25,17},{2,26},{10... | collective-permute-start | bytes 1572872 | tf_op jit(solution)/shard_map/ppermute | solution.py:28
  58.7 0.3 collective-permute-start.9
  59.0 1.7 %collective-permute-start.3 = (f32[512]{0:T(512)S(1)}, f32[512]{0:T(512)S(1)}, u32[]{:S(2)}, u32[]{:S(2)}) collective-permute-start(f32[512]{0:T(512)S(1)} %bitcast.24), channel_id=1, source_target_pairs={{0,8},{8,16},{16,24},{24,0},{1,9},{9,17},{17,25},{25,1},{2,10},{10... | collective-permute-start | bytes 6152 | tf_op jit(solution)/shard_map/ppermute | solution.py:28
  60.7 1.5 collective-permute-start.4
  62.2 20.0 %collective-permute-done.3 = f32[512]{0:T(512)S(1)} collective-permute-done((f32[512]{0:T(512)S(1)}, f32[512]{0:T(512)S(1)}, u32[]{:S(2)}, u32[]{:S(2)}) %collective-permute-start.3) | collective-permute-done | bytes 2080 | tf_op jit(solution)/shard_map/ppermute | solution.py:28
  82.1 1.3 collective-permute-start.5
  83.4 2.3 %collective-permute-done.5 = f32[512]{0:T(512)S(1)} collective-permute-done((f32[512]{0:T(512)S(1)}, f32[512]{0:T(512)S(1)}, u32[]{:S(2)}, u32[]{:S(2)}) %collective-permute-start.5) | collective-permute-done | bytes 2080 | tf_op jit(solution)/shard_map/ppermute | solution.py:28
  85.7 0.1 reshape.252
  85.9 2.8 %assemble.1 = bf16[8,272,512]{2,1,0:T(8,128)(2,1)} custom-call(f32[8,1,512]{2,1,0:T(1,128)S(1)} %pad.4.energy_ref, bf16[512,512]{1,0:T(8,128)(2,1)S(1)} %get-tuple-element.39.refs_0_, bf16[512,512]{1,0:T(8,128)(2,1)} %collective-permute-done.9.refs_1_, bf16[512,512]{1,0:T(8,128)(2,1)S(1)} %collective-permute-done.10.refs_2_, ...), custom_call_target="tpu_custom_call" | custom-call | flops 262144 | bytes 4194304 | tf_op jit(solution)/shard_map/assemble/pallas_call | solution.py:319
  88.6 4.9 %all-to-all-start = ((bf16[8,272,512]{2,1,0:T(8,128)(2,1)}), bf16[8,272,512]{2,1,0:T(8,128)(2,1)}, u32[]{:S(2)}, u32[]{:S(2)}) async-start(bf16[8,272,512]{2,1,0:T(8,128)(2,1)} %assemble.1), calls=%async_computation | async-start | bytes 4456448 | tf_op jit(solution)/shard_map/all_to_all | solution.py:368
  93.5 0.1 copy.9
  93.6 0.1 reshape.246
  93.8 1.9 %collective-permute-start.2 = (s32[640]{0:T(1024)S(1)}, s32[640]{0:T(1024)S(1)}, u32[]{:S(2)}, u32[]{:S(2)}) collective-permute-start(s32[640]{0:T(1024)S(1)} %constant_dynamic-update-slice_fusion), channel_id=1, source_target_pairs={{0,24},{8,0},{16,8},{24,16},{1,25},{9,1},{17,9},{25,17},{2,26},{10... | collective-permute-start | bytes 7688 | tf_op jit(solution)/shard_map/ppermute | solution.py:28
  95.8 1.5 collective-permute-start.1
  97.2 0.2 collective-permute-start
  97.5 1.9 %collective-permute-done.1 = s32[640]{0:T(1024)S(1)} collective-permute-done((s32[640]{0:T(1024)S(1)}, s32[640]{0:T(1024)S(1)}, u32[]{:S(2)}, u32[]{:S(2)}) %collective-permute-start.1) | collective-permute-done | bytes 2592 | tf_op jit(solution)/shard_map/ppermute | solution.py:28
  99.5 2.2 %collective-permute-done = s32[640]{0:T(1024)S(1)} collective-permute-done((s32[640]{0:T(1024)S(1)}, s32[640]{0:T(1024)S(1)}, u32[]{:S(2)}, u32[]{:S(2)}) %collective-permute-start) | collective-permute-done | bytes 2592 | tf_op jit(solution)/shard_map/ppermute | solution.py:28
  101.9 0.1 select_n.175.slot_ref
  102.0 0.1 reshape.247
  102.2 0.2 reshape.248
  102.5 0.2 reshape.249
  102.8 1.7 fusion.26
  104.5 0.6 collective-permute-start.13
  105.1 2.8 %collective-permute-start.14 = (bf16[512,512]{1,0:T(8,128)(2,1)S(1)}, bf16[512,512]{1,0:T(8,128)(2,1)S(1)}, u32[]{:S(2)}, u32[]{:S(2)}) collective-permute-start(bf16[512,512]{1,0:T(8,128)(2,1)S(1)} %bitcast.20), channel_id=1, source_target_pairs={{0,24},{8,0},{16,8},{24,16},{1,25},{9,1},{17,9},{25,17},{2,26},{10... | collective-permute-start | bytes 1572872 | tf_op jit(solution)/shard_map/ppermute | solution.py:28
  108.0 12.2 %collective-permute-done.12.refs_1_ = bf16[512,512]{1,0:T(8,128)(2,1)S(1)} collective-permute-done((bf16[512,512]{1,0:T(8,128)(2,1)S(1)}, bf16[512,512]{1,0:T(8,128)(2,1)S(1)}, u32[]{:S(2)}, u32[]{:S(2)}) %collective-permute-start.12) | collective-permute-done | bytes 524320 | tf_op jit(solution)/shard_map/ppermute | solution.py:28
  120.2 8.4 %collective-permute-done.13.refs_2_ = bf16[512,512]{1,0:T(8,128)(2,1)S(1)} collective-permute-done((bf16[512,512]{1,0:T(8,128)(2,1)S(1)}, bf16[512,512]{1,0:T(8,128)(2,1)S(1)}, u32[]{:S(2)}, u32[]{:S(2)}) %collective-permute-start.13) | collective-permute-done | bytes 524320 | tf_op jit(solution)/shard_map/ppermute | solution.py:28
  128.7 2.7 %delay_transform.3 = (bf16[512,512]{1,0:T(8,128)(2,1)S(1)}, bf16[512,512]{1,0:T(8,128)(2,1)}, bf16[512,512]{1,0:T(8,128)(2,1)}, bf16[512,512]{1,0:T(8,128)(2,1)S(1)}) custom-call(s32[1]{0:T(128)} %bitcast.me_ref, bf16[4,512,512]{2,1,0:T(8,128)(2,1)S(1)} %copy-done.1, bf16[512,512]{1,0:T(8,128)(2,1)S(1)} %bitcast.17, ...), custom_call_target="tpu_custom_call" | custom-call | flops 1073741824 | bytes 6291456 | tf_op jit(solution)/shard_map/delay_transform/pallas_call | solution.py:147
  131.3 1.7 collective-permute-start.15
  133.0 1.5 collective-permute-start.16
  134.5 1.2 collective-permute-start.17
  135.7 9.8 %all-to-all-done.refs_0_ = bf16[8,272,512]{2,1,0:T(8,128)(2,1)} async-done(((bf16[8,272,512]{2,1,0:T(8,128)(2,1)}), bf16[8,272,512]{2,1,0:T(8,128)(2,1)}, u32[]{:S(2)}, u32[]{:S(2)}) %all-to-all-start) | async-done | bytes 2228256 | tf_op jit(solution)/shard_map/all_to_all | solution.py:368
  145.5 0.7 convert_reduce_fusion
  146.3 1.9 %pair_weights.1 = (bf16[512,512]{1,0:T(8,128)(2,1)S(1)}, bf16[512,512]{1,0:T(8,128)(2,1)S(1)}, f32[64,512]{1,0:T(8,128)S(1)}) custom-call(s32[1,1024]{1,0:T(1,128)S(1)} %get-tuple-element.60.first_ref, s32[1,1024]{1,0:T(1,128)S(1)} %get-tuple-element.59.second_ref, f32[1,512]{1,0:T(1,128)S(1)} %add.228.energy_ref, s32[1,512]{1,0:T(1,128)S(1)} %select_n.175.slot_ref), custom_call_target="tpu_custom_call" | custom-call | flops 536870912 | bytes 1048576 | tf_op jit(solution)/shard_map/pair_weights/pallas_call | solution.py:192
  148.2 5.0 %pair_sums.2 = f32[64,256]{1,0:T(8,128)S(1)} custom-call(bf16[512,512]{1,0:T(8,128)(2,1)S(1)} %get-tuple-element.43.high_ref, bf16[512,512]{1,0:T(8,128)(2,1)S(1)} %get-tuple-element.44.low_ref, f32[64,512]{1,0:T(8,128)S(1)} %get-tuple-element.45.group_ref, bf16[8,272,512]{2,1,0:T(8,128)(2,1)} %all-to-all-done.refs_0_), custom_call_target="tpu_custom_call" | custom-call | flops 2147483648 | bytes 2097152 | tf_op jit(solution)/shard_map/pair_sums/pallas_call | solution.py:246
  153.1 2.8 %collective-permute-done.16.refs_2_ = bf16[512,512]{1,0:T(8,128)(2,1)} collective-permute-done((bf16[512,512]{1,0:T(8,128)(2,1)}, bf16[512,512]{1,0:T(8,128)(2,1)}, u32[]{:S(2)}, u32[]{:S(2)}) %collective-permute-start.16) | collective-permute-done | bytes 524320 | tf_op jit(solution)/shard_map/ppermute | solution.py:28
  156.0 4.5 %pair_sums.3 = f32[64,256]{1,0:T(8,128)S(1)} custom-call(bf16[512,512]{1,0:T(8,128)(2,1)S(1)} %get-tuple-element.43.high_ref, bf16[512,512]{1,0:T(8,128)(2,1)S(1)} %get-tuple-element.44.low_ref, f32[64,512]{1,0:T(8,128)S(1)} %get-tuple-element.45.group_ref, bf16[512,512]{1,0:T(8,128)(2,1)S(1)} %get-tuple-element.47.refs_0_, ...), custom_call_target="tpu_custom_call" | custom-call | flops 2147483648 | bytes 2097152 | tf_op jit(solution)/shard_map/pair_sums/pallas_call | solution.py:246
  160.6 1.8 %collective-permute-start.18 = (f32[16,256]{1,0:T(8,128)S(1)}, f32[16,256]{1,0:T(8,128)S(1)}, u32[]{:S(2)}, u32[]{:S(2)}) collective-permute-start(f32[16,256]{1,0:T(8,128)S(1)} %get-tuple-element.57), channel_id=1, source_target_pairs={{0,8},{8,16},{16,24},{24,0},{1,9},{9,17},{17,25},{25,1},{2,10},{10... | collective-permute-start | bytes 49160 | tf_op jit(solution)/shard_map/ppermute | solution.py:28
  162.4 1.5 collective-permute-start.19
  163.8 1.2 collective-permute-start.20
  165.0 0.2 collective-permute-done.18.refs_1_
  165.3 0.8 collective-permute-done.19.refs_2_
  166.1 1.5 collective-permute-done.20.refs_3_
  167.6 3.1 %interleave_delays.1 = f32[16,1024]{1,0:T(8,128)} custom-call(s32[1]{0:T(128)} %bitcast.me_ref, f32[16,256]{1,0:T(8,128)S(1)} %get-tuple-element.58.refs_0_, f32[16,256]{1,0:T(8,128)S(1)} %collective-permute-done.18.refs_1_, f32[16,256]{1,0:T(8,128)S(1)} %collective-permute-done.19.refs_2_, f32[16,256]{1,0:T(8,128)S(1)} %collective-permute-done.20.refs_3_), custom_call_target="tpu_custom_call" | custom-call | tf_op jit(solution)/shard_map/interleave_delays/pallas_call | solution.py:280
  (54 shorter events, 1.1 us)
Async XLA Ops:
  0.8 5.4 %copy-start.6 = (s32[1,512]{1,0:T(1,128)S(1)}, s32[1,512]{1,0:T(1,128)}, u32[]{:S(2)}) copy-start(s32[1,512]{1,0:T(1,128)} %param.7) | copy-start | bytes 6148
  7.2 2.2 %copy-start = (bf16[512,8,2,256]{3,1,2,0:T(8,128)(2,1)S(1)}, bf16[512,8,2,256]{3,1,2,0:T(8,128)(2,1)}, u32[]{:S(2)}) copy-start(bf16[512,8,2,256]{3,1,2,0:T(8,128)(2,1)} %copy.28) | copy-start | bytes 12582916
  12.8 0.8 copy-start.3
  13.7 0.8 copy-start.4
  18.1 1.4 copy-start.2
  19.5 33.2 %copy-start.1 = (bf16[4,512,512]{2,1,0:T(8,128)(2,1)S(1)}, bf16[4,512,512]{2,1,0:T(8,128)(2,1)}, u32[]{:S(2)}) copy-start(bf16[4,512,512]{2,1,0:T(8,128)(2,1)} %constant.193.clone.matrix_ref) | copy-start | bytes 6291460
  19.5 69.2 %all-to-all-start.1 = ((bf16[8,4,64,512]{3,2,1,0:T(8,128)(2,1)}), bf16[8,4,64,512]{3,2,1,0:T(8,128)(2,1)}, u32[]{:S(2)}, u32[]{:S(2)}) async-start(bf16[8,4,64,512]{3,2,1,0:T(8,128)(2,1)} %copy-done.2), calls=%async_computation.1 | async-start | bytes 4194304 | tf_op jit(solution)/shard_map/all_to_all | solution.py:365
  25.9 15.9 %collective-permute-start.6 = (bf16[512,512]{1,0:T(8,128)(2,1)}, bf16[512,512]{1,0:T(8,128)(2,1)S(1)}, u32[]{:S(2)}, u32[]{:S(2)}) collective-permute-start(bf16[512,512]{1,0:T(8,128)(2,1)} %copy-done.4), channel_id=1, source_target_pairs={{0,8},{8,16},{16,24},{24,0},{1,9},{9,17},{17,25},{25,1},{2,10},{10... | collective-permute-start | bytes 1572872 | tf_op jit(solution)/shard_map/ppermute | solution.py:28
  27.4 25.2 %collective-permute-start.7 = (bf16[512,512]{1,0:T(8,128)(2,1)}, bf16[512,512]{1,0:T(8,128)(2,1)S(1)}, u32[]{:S(2)}, u32[]{:S(2)}) collective-permute-start(bf16[512,512]{1,0:T(8,128)(2,1)} %copy-done.3), channel_id=1, source_target_pairs={{0,16},{8,24},{16,0},{24,8},{1,17},{9,25},{17,1},{25,9},{2,18},{10... | collective-permute-start | bytes 1572872 | tf_op jit(solution)/shard_map/ppermute | solution.py:28
  28.9 23.8 %collective-permute-start.8 = (bf16[512,512]{1,0:T(8,128)(2,1)S(1)}, bf16[512,512]{1,0:T(8,128)(2,1)S(1)}, u32[]{:S(2)}, u32[]{:S(2)}) collective-permute-start(bf16[512,512]{1,0:T(8,128)(2,1)S(1)} %get-tuple-element.38), channel_id=1, source_target_pairs={{0,24},{8,0},{16,8},{24,16},{1,25},{9,1},{17,9},{25,17},{2,26},{10... | collective-permute-start | bytes 1572872 | tf_op jit(solution)/shard_map/ppermute | solution.py:28
  55.5 30.4 %collective-permute-start.10 = (bf16[512,512]{1,0:T(8,128)(2,1)}, bf16[512,512]{1,0:T(8,128)(2,1)S(1)}, u32[]{:S(2)}, u32[]{:S(2)}) collective-permute-start(bf16[512,512]{1,0:T(8,128)(2,1)} %get-tuple-element.41), channel_id=1, source_target_pairs={{0,16},{8,24},{16,0},{24,8},{1,17},{9,25},{17,1},{25,9},{2,18},{10... | collective-permute-start | bytes 1572872 | tf_op jit(solution)/shard_map/ppermute | solution.py:28
  56.9 28.9 %collective-permute-start.11 = (bf16[512,512]{1,0:T(8,128)(2,1)}, bf16[512,512]{1,0:T(8,128)(2,1)}, u32[]{:S(2)}, u32[]{:S(2)}) collective-permute-start(bf16[512,512]{1,0:T(8,128)(2,1)} %get-tuple-element.42), channel_id=1, source_target_pairs={{0,24},{8,0},{16,8},{24,16},{1,25},{9,1},{17,9},{25,17},{2,26},{10... | collective-permute-start | bytes 1572872 | tf_op jit(solution)/shard_map/ppermute | solution.py:28
  58.7 27.2 %collective-permute-start.9 = (bf16[512,512]{1,0:T(8,128)(2,1)}, bf16[512,512]{1,0:T(8,128)(2,1)}, u32[]{:S(2)}, u32[]{:S(2)}) collective-permute-start(bf16[512,512]{1,0:T(8,128)(2,1)} %get-tuple-element.40), channel_id=1, source_target_pairs={{0,8},{8,16},{16,24},{24,0},{1,9},{9,17},{17,25},{25,1},{2,10},{10... | collective-permute-start | bytes 1572872 | tf_op jit(solution)/shard_map/ppermute | solution.py:28
  59.0 23.2 %collective-permute-start.3 = (f32[512]{0:T(512)S(1)}, f32[512]{0:T(512)S(1)}, u32[]{:S(2)}, u32[]{:S(2)}) collective-permute-start(f32[512]{0:T(512)S(1)} %bitcast.24), channel_id=1, source_target_pairs={{0,8},{8,16},{16,24},{24,0},{1,9},{9,17},{17,25},{25,1},{2,10},{10... | collective-permute-start | bytes 6152 | tf_op jit(solution)/shard_map/ppermute | solution.py:28
  60.7 22.7 %collective-permute-start.4 = (f32[512]{0:T(512)S(1)}, f32[512]{0:T(512)S(1)}, u32[]{:S(2)}, u32[]{:S(2)}) collective-permute-start(f32[512]{0:T(512)S(1)} %bitcast.25), channel_id=1, source_target_pairs={{0,16},{8,24},{16,0},{24,8},{1,17},{9,25},{17,1},{25,9},{2,18},{10... | collective-permute-start | bytes 6152 | tf_op jit(solution)/shard_map/ppermute | solution.py:28
  82.1 3.6 %collective-permute-start.5 = (f32[512]{0:T(512)S(1)}, f32[512]{0:T(512)S(1)}, u32[]{:S(2)}, u32[]{:S(2)}) collective-permute-start(f32[512]{0:T(512)S(1)} %bitcast.26), channel_id=1, source_target_pairs={{0,24},{8,0},{16,8},{24,16},{1,25},{9,1},{17,9},{25,17},{2,26},{10... | collective-permute-start | bytes 6152 | tf_op jit(solution)/shard_map/ppermute | solution.py:28
  88.6 4.9 %copy-start.5 = (s32[256,2]{0,1:T(2,128)S(1)}, s32[256,2]{0,1:T(2,128)}, u32[]{:S(2)}) copy-start(s32[256,2]{0,1:T(2,128)} %param.10) | copy-start | bytes 6148
  88.6 5.2 %copy-start.7 = (s32[128]{0:T(128)S(1)}, s32[128]{0:T(128)}, u32[]{:S(2)}) copy-start(s32[128]{0:T(128)} %param.9) | copy-start | bytes 1540
  88.6 56.8 %all-to-all-start = ((bf16[8,272,512]{2,1,0:T(8,128)(2,1)}), bf16[8,272,512]{2,1,0:T(8,128)(2,1)}, u32[]{:S(2)}, u32[]{:S(2)}) async-start(bf16[8,272,512]{2,1,0:T(8,128)(2,1)} %assemble.1), calls=%async_computation | async-start | bytes 4456448 | tf_op jit(solution)/shard_map/all_to_all | solution.py:368
  93.8 3.7 %collective-permute-start.2 = (s32[640]{0:T(1024)S(1)}, s32[640]{0:T(1024)S(1)}, u32[]{:S(2)}, u32[]{:S(2)}) collective-permute-start(s32[640]{0:T(1024)S(1)} %constant_dynamic-update-slice_fusion), channel_id=1, source_target_pairs={{0,24},{8,0},{16,8},{24,16},{1,25},{9,1},{17,9},{25,17},{2,26},{10... | collective-permute-start | bytes 7688 | tf_op jit(solution)/shard_map/ppermute | solution.py:28
  95.8 3.6 %collective-permute-start.1 = (s32[640]{0:T(1024)S(1)}, s32[640]{0:T(1024)S(1)}, u32[]{:S(2)}, u32[]{:S(2)}) collective-permute-start(s32[640]{0:T(1024)S(1)} %constant_dynamic-update-slice_fusion), channel_id=1, source_target_pairs={{0,16},{8,24},{16,0},{24,8},{1,17},{9,25},{17,1},{25,9},{2,18},{10... | collective-permute-start | bytes 7688 | tf_op jit(solution)/shard_map/ppermute | solution.py:28
  97.2 4.5 %collective-permute-start = (s32[640]{0:T(1024)S(1)}, s32[640]{0:T(1024)S(1)}, u32[]{:S(2)}, u32[]{:S(2)}) collective-permute-start(s32[640]{0:T(1024)S(1)} %constant_dynamic-update-slice_fusion), channel_id=1, source_target_pairs={{0,8},{8,16},{16,24},{24,0},{1,9},{9,17},{17,25},{25,1},{2,10},{10... | collective-permute-start | bytes 7688 | tf_op jit(solution)/shard_map/ppermute | solution.py:28
  104.4 15.8 %collective-permute-start.12 = (bf16[512,512]{1,0:T(8,128)(2,1)S(1)}, bf16[512,512]{1,0:T(8,128)(2,1)S(1)}, u32[]{:S(2)}, u32[]{:S(2)}) collective-permute-start(bf16[512,512]{1,0:T(8,128)(2,1)S(1)} %bitcast.22), channel_id=1, source_target_pairs={{0,8},{8,16},{16,24},{24,0},{1,9},{9,17},{17,25},{25,1},{2,10},{10... | collective-permute-start | bytes 1572872 | tf_op jit(solution)/shard_map/ppermute | solution.py:28
  104.5 24.2 %collective-permute-start.13 = (bf16[512,512]{1,0:T(8,128)(2,1)S(1)}, bf16[512,512]{1,0:T(8,128)(2,1)S(1)}, u32[]{:S(2)}, u32[]{:S(2)}) collective-permute-start(bf16[512,512]{1,0:T(8,128)(2,1)S(1)} %bitcast.21), channel_id=1, source_target_pairs={{0,16},{8,24},{16,0},{24,8},{1,17},{9,25},{17,1},{25,9},{2,18},{10... | collective-permute-start | bytes 1572872 | tf_op jit(solution)/shard_map/ppermute | solution.py:28
  105.1 23.5 %collective-permute-start.14 = (bf16[512,512]{1,0:T(8,128)(2,1)S(1)}, bf16[512,512]{1,0:T(8,128)(2,1)S(1)}, u32[]{:S(2)}, u32[]{:S(2)}) collective-permute-start(bf16[512,512]{1,0:T(8,128)(2,1)S(1)} %bitcast.20), channel_id=1, source_target_pairs={{0,24},{8,0},{16,8},{24,16},{1,25},{9,1},{17,9},{25,17},{2,26},{10... | collective-permute-start | bytes 1572872 | tf_op jit(solution)/shard_map/ppermute | solution.py:28
  131.3 21.8 %collective-permute-start.15 = (bf16[512,512]{1,0:T(8,128)(2,1)}, bf16[512,512]{1,0:T(8,128)(2,1)S(1)}, u32[]{:S(2)}, u32[]{:S(2)}) collective-permute-start(bf16[512,512]{1,0:T(8,128)(2,1)} %get-tuple-element.48), channel_id=1, source_target_pairs={{0,8},{8,16},{16,24},{24,0},{1,9},{9,17},{17,25},{25,1},{2,10},{10... | collective-permute-start | bytes 1572872 | tf_op jit(solution)/shard_map/ppermute | solution.py:28
  133.0 22.9 %collective-permute-start.16 = (bf16[512,512]{1,0:T(8,128)(2,1)}, bf16[512,512]{1,0:T(8,128)(2,1)}, u32[]{:S(2)}, u32[]{:S(2)}) collective-permute-start(bf16[512,512]{1,0:T(8,128)(2,1)} %get-tuple-element.49), channel_id=1, source_target_pairs={{0,16},{8,24},{16,0},{24,8},{1,17},{9,25},{17,1},{25,9},{2,18},{10... | collective-permute-start | bytes 1572872 | tf_op jit(solution)/shard_map/ppermute | solution.py:28
  134.5 21.5 %collective-permute-start.17 = (bf16[512,512]{1,0:T(8,128)(2,1)S(1)}, bf16[512,512]{1,0:T(8,128)(2,1)}, u32[]{:S(2)}, u32[]{:S(2)}) collective-permute-start(bf16[512,512]{1,0:T(8,128)(2,1)S(1)} %get-tuple-element.50), channel_id=1, source_target_pairs={{0,24},{8,0},{16,8},{24,16},{1,25},{9,1},{17,9},{25,17},{2,26},{10... | collective-permute-start | bytes 1572872 | tf_op jit(solution)/shard_map/ppermute | solution.py:28
  160.6 4.7 %collective-permute-start.18 = (f32[16,256]{1,0:T(8,128)S(1)}, f32[16,256]{1,0:T(8,128)S(1)}, u32[]{:S(2)}, u32[]{:S(2)}) collective-permute-start(f32[16,256]{1,0:T(8,128)S(1)} %get-tuple-element.57), channel_id=1, source_target_pairs={{0,8},{8,16},{16,24},{24,0},{1,9},{9,17},{17,25},{25,1},{2,10},{10... | collective-permute-start | bytes 49160 | tf_op jit(solution)/shard_map/ppermute | solution.py:28
  162.4 3.7 %collective-permute-start.19 = (f32[16,256]{1,0:T(8,128)S(1)}, f32[16,256]{1,0:T(8,128)S(1)}, u32[]{:S(2)}, u32[]{:S(2)}) collective-permute-start(f32[16,256]{1,0:T(8,128)S(1)} %get-tuple-element.56), channel_id=1, source_target_pairs={{0,16},{8,24},{16,0},{24,8},{1,17},{9,25},{17,1},{25,9},{2,18},{10... | collective-permute-start | bytes 49160 | tf_op jit(solution)/shard_map/ppermute | solution.py:28
  163.8 3.7 %collective-permute-start.20 = (f32[16,256]{1,0:T(8,128)S(1)}, f32[16,256]{1,0:T(8,128)S(1)}, u32[]{:S(2)}, u32[]{:S(2)}) collective-permute-start(f32[16,256]{1,0:T(8,128)S(1)} %get-tuple-element.55), channel_id=1, source_target_pairs={{0,24},{8,0},{16,8},{24,16},{1,25},{9,1},{17,9},{25,17},{2,26},{10... | collective-permute-start | bytes 49160 | tf_op jit(solution)/shard_map/ppermute | solution.py:28

commit v2 on v1

v2 whole, which is shorter than its diff:
```python
import functools
import math

import jax
import jax.numpy as jnp
import ml_dtypes
import numpy as np
from jax import lax
from jax.experimental import pallas as pl
from jax.experimental.pallas import tpu as pltpu
from jax.sharding import PartitionSpec as P

GRP_DEV = 16
LANES = 128
DELAY_COST = 800
BF16_PARTS = 3
EXTRA_ROWS = 16
HIGHEST = lax.Precision.HIGHEST
VMEM_LIMIT = 28 * 1024 * 1024
F32 = jnp.float32
BF16 = jnp.bfloat16
VMEM = pl.BlockSpec(memory_space=pltpu.VMEM)
SMEM = pl.BlockSpec(memory_space=pltpu.SMEM)


def shifted(value, axis, steps):
    count = lax.axis_size(axis)
    pairs = [(source, (source + steps) % count) for source in range(count)]
    return lax.ppermute(value, axis, pairs)


def spread(pieces):
    return [pieces[0]] + [shifted(pieces[s], "band", s) for s in range(1, len(pieces))]


def cost(flops, bytes_accessed):
    return pl.CostEstimate(flops=flops, bytes_accessed=bytes_accessed, transcendentals=0)


def params(limit=VMEM_LIMIT):
    return pltpu.CompilerParams(vmem_limit_bytes=limit)


def class_matrices(full_width, classes):
    sub = full_width // classes
    channel = np.arange(sub)[None, :, None]
    delay = classes * np.arange(sub)[None, None, :] + np.arange(classes)[:, None, None]
    angle = (channel * delay % full_width) * (2.0 * math.pi / full_width)
    cosine, sine = np.cos(angle), np.sin(angle)
    upper = np.concatenate([cosine, -sine], axis=2)
    lower = np.concatenate([sine, cosine], axis=2)
    return np.concatenate([upper, lower], axis=1).astype(ml_dtypes.bfloat16)


def taper_window(full_width):
    angle = np.arange(full_width) * (2.0 * math.pi / full_width)
    window = (
        0.35875
        - 0.48829 * np.cos(angle)
        + 0.14128 * np.cos(2.0 * angle)
        - 0.01168 * np.cos(3.0 * angle)
    )
    return window.reshape(1, -1).astype(np.float32)


def tiles_of(ref, where, start, count, column):
    tiles = [ref[where, pl.ds((start + c) * column, column), :] for c in range(count)]
    return jnp.concatenate([t.reshape(-1, LANES) for t in tiles], axis=1)


def taper_kernel(times, parts, band_count, me_ref, order_ref, window_ref, flags_ref, vis_ref, *refs):
    early_ref, late_refs = refs[0], refs[1:-4]
    slab_ref, early_buf, late_buf, sems = refs[-4:]
    step = pl.program_id(0)
    slabs, rows, _ = slab_ref.shape
    height = vis_ref.shape[0] // slabs
    block = jnp.transpose(vis_ref[...].reshape(height, slabs, LANES), (1, 0, 2))
    slab_ref[:, pl.ds(pl.multiple_of(step * height, height), height), :] = block

    @pl.when(step == pl.num_programs(0) - 1)
    def _():
        blocks = early_buf.shape[0]
        count = len(late_refs)
        column = rows // blocks
        peer = column // band_count
        tiles = slabs // times
        sub = tiles // parts * LANES
        me = me_ref[0]
        here = pl.ds(pl.multiple_of(me * sub, sub), sub)
        weight = window_ref[:, here] * flags_ref[:, here].astype(F32)
        weight = jnp.concatenate([weight] * parts, axis=1)
        order = jnp.transpose(jnp.broadcast_to(order_ref[...].astype(F32), (LANES, rows)))
        if peer % 8 == 0:
            order = order.reshape(band_count, blocks, peer, LANES).transpose(1, 0, 2, 3)
            order = order.reshape(rows, LANES)
        lane = lax.broadcasted_iota(jnp.int32, (rows, LANES), 1)
        pick = [(lane + c == order.astype(jnp.int32)).astype(BF16) for c in range(0, rows, LANES)]
        pick = jnp.concatenate(pick, axis=1)
        total = jnp.zeros((rows, LANES), F32)
        copies = []
        for half in (1, 0):
            for s in range(count):
                time = half * count + lax.rem(me + s, count)
                source = [
                    slab_ref[(time * (tiles // parts) + tile) * parts + part]
                    for part in range(parts)
                    for tile in range(tiles // parts)
                ]
                moved = jnp.dot(pick, jnp.concatenate(source, axis=1), preferred_element_type=F32)
                tapered = (moved * weight).astype(BF16)
                for c in range(tiles):
                    tile = tapered[:, c * LANES : (c + 1) * LANES]
                    wide = tile.astype(F32)
                    total = total + wide * wide
                    tile = tile.reshape(blocks, column, LANES)
                    if half:
                        late_buf[s, :, c * column : (c + 1) * column] = tile
                    else:
                        start = (s * tiles + c) * column
                        early_buf[:, start : start + column] = tile
                if half:
                    copy = pltpu.make_async_copy(late_buf.at[s], late_refs[s], sems.at[s])
                else:
                    where = pl.ds(s * tiles * column, tiles * column)
                    copy = pltpu.make_async_copy(
                        early_buf.at[:, where], early_ref.at[:, where], sems.at[count + s]
                    )
                copy.start()
                copies.append(copy)
        energy = lax.dot_general(
            jnp.ones((EXTRA_ROWS, LANES), F32),
            total,
            (((1,), (1,)), ((), ())),
            precision=HIGHEST,
            preferred_element_type=F32,
        )
        row = lax.broadcasted_iota(jnp.int32, energy.shape, 0)
        rest, extra = energy, jnp.zeros_like(energy)
        for k in range(BF16_PARTS):
            part = rest.astype(BF16).astype(F32)
            extra = jnp.where(row == k, part, extra)
            rest = rest - part
        start = count * tiles * column
        for j in range(blocks):
            mine = extra[:, j * column : (j + 1) * column]
            mine = jnp.concatenate([mine, jnp.zeros((EXTRA_ROWS, LANES - column), F32)], axis=1)
            early_buf[j, start:] = mine.astype(BF16)
        where = pl.ds(start, EXTRA_ROWS)
        copy = pltpu.make_async_copy(
            early_buf.at[:, where], early_ref.at[:, where], sems.at[2 * count]
        )
        copy.start()
        for copy in copies + [copy]:
            copy.wait()


def taper(band_count, blocks, me, order, window, flags, visibilities):
    rows, times, parts, sub = visibilities.shape
    count, lanes, tiles, steps = times // 2, parts * sub, sub // LANES, 4
    column = rows // blocks
    vis = visibilities.reshape(rows, times, parts, tiles, LANES).transpose(0, 1, 3, 2, 4)
    vis = vis.reshape(rows * times * tiles * parts, LANES)
    piece = (blocks, parts * tiles * column, LANES)
    early = (blocks, count * parts * tiles * column + EXTRA_ROWS, LANES)
    return pl.pallas_call(
        functools.partial(taper_kernel, times, parts, band_count),
        grid=(steps,),
        out_shape=[jax.ShapeDtypeStruct(shape, BF16) for shape in [early] + [piece] * count],
        in_specs=[
            SMEM,
            pl.BlockSpec(order.shape, lambda i: (0, 0)),
            pl.BlockSpec(window.shape, lambda i: (0, 0)),
            pl.BlockSpec(flags.shape, lambda i: (0, 0)),
            pl.BlockSpec((vis.shape[0] // steps, LANES), lambda i: (i, 0)),
        ],
        out_specs=[pl.BlockSpec(memory_space=pl.ANY)] * (1 + count),
        scratch_shapes=[
            pltpu.VMEM((vis.shape[0] // rows, rows, LANES), BF16),
            pltpu.VMEM(early, BF16),
            pltpu.VMEM((count,) + piece, BF16),
            pltpu.SemaphoreType.DMA((2 * count + 1,)),
        ],
        compiler_params=params(60 * 1024 * 1024),
        cost_estimate=cost(2 * times * rows * rows * lanes, 4 * times * rows * lanes),
        name="taper_rows",
    )(me, order, window, flags, vis)


def delay_kernel(me_ref, matrix_ref, *refs):
    x_refs, out_refs, mixed = refs[:4], refs[4:8], refs[8]
    blocks, height, _ = x_refs[0].shape
    tiles = mixed.shape[2] // LANES
    column = height // tiles
    half = mixed.shape[2] // 2
    me = me_ref[0]
    x = [tiles_of(ref, slice(None), 0, tiles, column).astype(F32) for ref in x_refs]
    a, b, c, d = x[0] + x[2], x[0] - x[2], x[1] + x[3], x[1] - x[3]
    turned = jnp.concatenate([-d[:, half:], d[:, :half]], axis=1)
    for r, value in enumerate((a + c, b + turned, a - c, b - turned)):
        if r:
            turns = lax.rem(r * me, 4)
            real = jnp.where(turns == 0, 1.0, jnp.where(turns == 2, -1.0, 0.0)).astype(F32)
            imag = jnp.where(turns == 3, 1.0, jnp.where(turns == 1, -1.0, 0.0)).astype(F32)
            if r == 2:
                value = value * real
            else:
                other = jnp.concatenate([-value[:, half:], value[:, :half]], axis=1)
                value = value * real + other * imag
        mixed[r] = value.astype(BF16)
    for s in range(4):
        r = lax.rem(me + s, 4)
        out = jnp.dot(mixed[r], matrix_ref[r], preferred_element_type=F32).astype(BF16)
        for c in range(tiles):
            tile = out[:, c * LANES : (c + 1) * LANES].reshape(blocks, column, LANES)
            out_refs[s][:, c * column : (c + 1) * column] = tile


def delay_transform(me, matrices, pieces):
    _, lanes, _ = matrices.shape
    blocks, height, _ = pieces[-1].shape
    column = height // (lanes // LANES)
    group = max(1, 256 // column)
    tile = pl.BlockSpec((group, height, LANES), lambda i: (i, 0, 0))
    return pl.pallas_call(
        delay_kernel,
        grid=(blocks // group,),
        out_shape=[jax.ShapeDtypeStruct((blocks, height, LANES), BF16)] * 4,
        in_specs=[SMEM, pl.BlockSpec(matrices.shape, lambda i: (0, 0, 0))] + [tile] * 4,
        out_specs=[tile] * 4,
        scratch_shapes=[pltpu.VMEM((4, group * column, lanes), BF16)],
        compiler_params=params(),
        cost_estimate=cost(DELAY_COST * blocks * column * lanes * lanes, 16 * blocks * height * LANES),
        name="delay_transform",
    )(me, matrices, *pieces)


def pair_weights_kernel(first_ref, second_ref, energy_ref, slot_ref, mix_ref, group_ref):
    rows = energy_ref.shape[1]
    pairs = first_ref.shape[1]
    place = lax.broadcasted_iota(jnp.int32, (rows, pairs), 0)
    contract_last = (((1,), (1,)), ((), ()))
    counts = lax.dot_general(
        (place == first_ref[...]).astype(BF16),
        (place == second_ref[...]).astype(BF16),
        contract_last,
        preferred_element_type=F32,
    )
    inverse = 1.0 / energy_ref[...]
    scale = inverse * jnp.sqrt(inverse)
    weighted = counts * scale
    mix_ref[...] = weighted.astype(BF16)
    partner = lax.dot_general(
        jnp.broadcast_to(inverse, (8, rows)),
        counts,
        contract_last,
        precision=HIGHEST,
        preferred_element_type=F32,
    )[0:1]
    slots = group_ref.shape[0]
    member = lax.broadcasted_iota(jnp.int32, (slots, rows), 0) == slot_ref[...]
    denom = jnp.sum(jnp.where(member, inverse * partner, 0.0), axis=1, keepdims=True)
    group_ref[...] = jnp.where(member, scale, 0.0) / denom


def pair_weights(first, second, energy, slot, slots):
    rows = energy.shape[1]
    return pl.pallas_call(
        pair_weights_kernel,
        out_shape=[
            jax.ShapeDtypeStruct((rows, rows), BF16),
            jax.ShapeDtypeStruct((slots, rows), F32),
        ],
        in_specs=[VMEM] * 4,
        out_specs=[VMEM] * 2,
        compiler_params=params(),
        cost_estimate=cost(2 * rows * rows * first.shape[1], 4 * rows * rows),
        name="pair_weights",
    )(first, second, energy, slot)


def pair_kernel(count, mix_ref, group_ref, *refs):
    z_refs, out_ref = refs[:-1], refs[-1]
    block, rows = mix_ref.shape
    column = rows // z_refs[0].shape[0]
    lanes = 2 * out_ref.shape[1]
    tiles = lanes // LANES
    step = pl.program_id(0)
    mine = pl.ds(step * (block // column), block // column)
    total = jnp.zeros((block, lanes), F32)
    for t in range(count):
        ref, start = (z_refs[0], t * tiles) if len(z_refs) == 1 else (z_refs[t], 0)
        window = tiles_of(ref, slice(None), start, tiles, column)
        own = tiles_of(ref, mine, start, tiles, column)
        mixed = jnp.dot(mix_ref[...], window, preferred_element_type=F32)
        total = total + own.astype(F32) * mixed
    half = lanes // 2
    cross = total[:, :half] + total[:, half:]
    part = jnp.dot(group_ref[...], cross, precision=HIGHEST, preferred_element_type=F32)

    @pl.when(step == 0)
    def _():
        out_ref[...] = part

    @pl.when(step > 0)
    def _():
        out_ref[...] += part


def pair_sums(count, half, mix, group, pieces):
    rows = mix.shape[1]
    slots = group.shape[0]
    block = min(rows, 256)
    whole = [pl.BlockSpec(p.shape, lambda i: (0, 0, 0)) for p in pieces]
    return pl.pallas_call(
        functools.partial(pair_kernel, count),
        grid=(rows // block,),
        out_shape=jax.ShapeDtypeStruct((slots, half), F32),
        in_specs=[
            pl.BlockSpec((block, rows), lambda i: (i, 0)),
            pl.BlockSpec((slots, block), lambda i: (0, i)),
        ]
        + whole,
        out_specs=pl.BlockSpec((slots, half), lambda i: (0, 0)),
        compiler_params=params(),
        cost_estimate=cost(4 * count * rows * rows * half, 4 * count * rows * half),
        name="pair_sums",
    )(mix, group, *pieces)


def interleave_kernel(me_ref, *refs):
    pieces, out_ref = refs[:-1], refs[-1]
    count = len(pieces)
    width = pieces[0].shape[1]
    me = me_ref[0]
    row = lax.broadcasted_iota(jnp.int32, (width, count * width), 0)
    column = lax.broadcasted_iota(jnp.int32, (width, count * width), 1)
    total = 0.0
    for s in range(count):
        r = lax.rem(me + count - s, count)
        pick = (column == row * count + r).astype(BF16)
        rest, parts = pieces[s][...], []
        for _ in range(BF16_PARTS):
            parts.append(rest.astype(BF16))
            rest = rest - parts[-1].astype(F32)
        parts = jnp.concatenate(parts, axis=0)
        total = total + jnp.dot(parts, pick, preferred_element_type=F32)
    groups = out_ref.shape[0]
    out_ref[...] = sum(total[k * groups : (k + 1) * groups] for k in range(BF16_PARTS))


def interleave(me, pieces):
    groups, width = pieces[0].shape
    return pl.pallas_call(
        interleave_kernel,
        out_shape=jax.ShapeDtypeStruct((groups, width * len(pieces)), F32),
        in_specs=[SMEM] + [VMEM] * len(pieces),
        out_specs=VMEM,
        compiler_params=params(),
        name="interleave_delays",
    )(me, *pieces)


def window_places(pair_list, owner, block_count, peer, band_count):
    owned = block_count * peer
    local = pair_list % owned
    source = jnp.where(pair_list < owned, owner, (owner + band_count - 1) % band_count)
    return (local // peer) * (band_count * peer) + source * peer + local % peer


def on_device(matrices, window, visibilities, send_order, channel_flags, group_ids, pair_list):
    band_count = lax.axis_size("band")
    block_count = lax.axis_size("bl")
    rows, times, parts, sub = visibilities.shape
    peer = rows // (band_count * block_count)
    column = band_count * peer
    height = parts * sub // LANES * column
    band = lax.axis_index("band").astype(jnp.int32)
    me = band.reshape(1)

    order = send_order
    if peer % 8:
        order = order.reshape(band_count, block_count, peer).transpose(1, 0, 2).reshape(1, rows)
    flags = channel_flags.reshape(1, -1)
    early, *late = taper(band_count, block_count, me, order, window, flags, visibilities)

    early = lax.all_to_all(early, "bl", split_axis=0, concat_axis=0, tiled=True)
    late = spread(delay_transform(me, matrices, spread(late)))
    late = jnp.concatenate(late, axis=1)
    late = lax.all_to_all(late, "bl", split_axis=0, concat_axis=0, tiled=True)

    energy = early[:, band_count * height :][:, :BF16_PARTS, :column].astype(F32).sum(axis=1)
    early = [early] + [early[:, s * height : (s + 1) * height] for s in range(1, band_count)]
    early = delay_transform(me, matrices, spread(early))

    small = jnp.concatenate(
        [energy.reshape(-1), pair_list.reshape(-1).astype(F32), group_ids.astype(F32)]
    )
    early, small = lax.optimization_barrier((early, small))
    early = spread(early)
    small = spread([small] * band_count)
    energy = sum(table[:rows] for table in small).reshape(1, rows) / (parts * times) + 1e-06
    tables = [table[rows:].astype(jnp.int32) for table in small]
    owners = [(band + band_count - s) % band_count for s in range(band_count)]
    place = jnp.concatenate(
        [
            window_places(table[: pair_list.size].reshape(-1, 2), owner, block_count, peer, band_count)
            for table, owner in zip(tables, owners)
        ]
    ).T
    slot = jnp.zeros((block_count, band_count, peer), jnp.int32)
    for s, (table, owner) in enumerate(zip(tables, owners)):
        groups = table[pair_list.size :].reshape(block_count, 1, peer)
        groups = groups + GRP_DEV * ((band_count - s) % band_count)
        slot = jnp.where(jnp.arange(band_count)[None, :, None] == owner, groups, slot)
    mix, group = pair_weights(
        place[0:1], place[1:2], energy, slot.reshape(1, rows), GRP_DEV * band_count
    )
    sums = pair_sums(band_count, sub, mix, group, early)
    sums = sums + pair_sums(band_count, sub, mix, group, [late])
    sums = sums.reshape(band_count, GRP_DEV, sub)
    return interleave(me, spread([sums[s] for s in range(band_count)]))


def solution(mesh):
    band_count = mesh.shape["band"]

    def whole(visibilities, send_order, channel_flags, group_ids, pair_list):
        full_width = visibilities.shape[3]
        matrices = jnp.asarray(class_matrices(full_width, band_count))
        window = jnp.asarray(taper_window(full_width))
        mapped = jax.shard_map(
            on_device,
            mesh=mesh,
            in_specs=(
                P(),
                P(),
                P("bl", None, None, "band"),
                P("bl", None),
                P(),
                P(("band", "bl")),
                P(("band", "bl"), None),
            ),
            out_specs=P(("band", "bl"), None),
            check_vma=False,
        )
        return mapped(
            matrices, window, visibilities, send_order, channel_flags, group_ids, pair_list
        )

    return whole
```

time: 171 us -> 144 us (0.84)
  waiting for transfers between devices: 84.5 us -> 67.8 us
  Pallas kernels: 29.7 us -> 23.2 us
  starting transfers between devices: 39.7 us -> 34.4 us
    ppermute x21 -> x18, waiting for transfers between devices: 74.7 us -> 33.2 us  [shifted(): return lax.ppermute(value, axis, pairs)]
    all_to_all x1, waiting for transfers between devices: 0.01 us -> 18.6 us  [on_device(): early = lax.all_to_all(early, 'bl', split_axis=0, concat_axis=0, tiled=True)]
    all_to_all x1, waiting for transfers between devices: 9.78 us -> 15.9 us  [on_device(): late = lax.all_to_all(late, 'bl', split_axis=0, concat_axis=0, tiled=True)]
    pallas_call x7 -> x5, Pallas kernels: 24.8 us -> 20.3 us  [the longest x1 7.23 us: taper(): pl.pallas_call(functools.partial(taper_kernel, times, parts, band_count),...]
    ppermute x21 -> x18, starting transfers between devices: 28.3 us -> 25.2 us  [shifted(): return lax.ppermute(value, axis, pairs)]
    concatenate x0 -> x2, other arithmetic: none -> 2.88 us  [the longest x1 2.87 us: on_device(): late = jnp.concatenate(late, axis=1)]
    pallas_call x1, Pallas kernels: 3.11 us -> 1.09 us  [interleave(): pl.pallas_call(interleave_kernel, out_shape=jax.ShapeDtypeStruct((groups,...]
    unnamed x20 -> x28, local copies, waits for them, and re-layouts: 10.8 us -> 11.3 us
  transfers between devices with their start and end apart: 23 -> 20, of which waited for: 14 -> 10; matrix products, arithmetic and copies ran while one was open for 2% -> 4% of each run, Pallas kernels for 9% -> 9%
where the time goes in v2:
time: 144 us; the launch traced here: 143 us
  waiting for transfers between devices  67.8 us (47%)
  starting transfers between devices  34.4 us (24%)
  Pallas kernels  23.2 us (16%)
  local copies, waits for them, and re-layouts  14.2 us (10%)
  other arithmetic  3.14 us (2%)
    ppermute x18, waiting for transfers between devices, shifted(): return lax.ppermute(value, axis, pairs)  33.2 us
    ppermute x18, starting transfers between devices, shifted(): return lax.ppermute(value, axis, pairs)  25.2 us
    all_to_all x1, waiting for transfers between devices, on_device(): early = lax.all_to_all(early, 'bl', split_axis=0, concat_axis=0, tiled=True)  18.6 us
    all_to_all x1, waiting for transfers between devices, on_device(): late = lax.all_to_all(late, 'bl', split_axis=0, concat_axis=0, tiled=True)  15.9 us
    unnamed x28, local copies, waits for them, and re-layouts  11.3 us
    pallas_call x1, Pallas kernels, taper(): pl.pallas_call(functools.partial(taper_kernel, times, parts, band_count),...  7.23 us
    pallas_call x2, Pallas kernels, delay_transform(): pl.pallas_call(delay_kernel, grid=(blocks // group,), out_shape=[jax.Shap...  6.96 us
    pallas_call x2, Pallas kernels, pair_sums(): pl.pallas_call(functools.partial(pair_kernel, count), grid=(rows // block...  6.12 us
  transfers between devices with their start and end apart: 20, of which 10 were waited for; matrix products, arithmetic and copies ran while one was open for 4% of the time, Pallas kernels for 9%

profile of v2, /device:TPU:0, one launch (start us, length us, event | category | flops | bytes accessed | tf_op | source)
XLA Modules:
  0.0 143.0 jit_solution(15358241262628099272)
XLA Ops:
  0.0 7.2 %taper_rows.1 = (bf16[8,1040,128]{2,1,0:T(8,128)(2,1)}, bf16[8,256,128]{2,1,0:T(8,128)(2,1)}, bf16[8,256,128]{2,1,0:T(8,128)(2,1)}, bf16[8,256,128]{2,1,0:T(8,128)(2,1)}, bf16[8,256,128]{2,1,0:T(8,128)(2,1)}) custom-call(s32[1]{0:T(128)} %bitcast.me_ref, s32[1,512]{1,0:T(1,128)} %order_ref.1, f32[1,1024]{1,0:T(1,128)} %constant.174.clone.window_ref, ...), custom_call_target="tpu_custom_call" | custom-call | flops 2147483648 | bytes 8388608 | tf_op jit(solution)/shard_map/taper_rows/pallas_call | solution.py:165
  7.2 3.0 %collective-permute-start.10 = (bf16[8,256,128]{2,1,0:T(8,128)(2,1)}, bf16[8,256,128]{2,1,0:T(8,128)(2,1)S(1)}, u32[]{:S(2)}, u32[]{:S(2)}) collective-permute-start(bf16[8,256,128]{2,1,0:T(8,128)(2,1)} %get-tuple-element.39), channel_id=1, source_target_pairs={{0,16},{8,24},{16,0},{24,8},{1,17},{9,25},{17,1},{25,9},{2,18},{10... | collective-permute-start | bytes 1572872 | tf_op jit(solution)/shard_map/ppermute | solution.py:29
  10.3 1.4 %collective-permute-start.11 = (bf16[8,256,128]{2,1,0:T(8,128)(2,1)}, bf16[8,256,128]{2,1,0:T(8,128)(2,1)S(1)}, u32[]{:S(2)}, u32[]{:S(2)}) collective-permute-start(bf16[8,256,128]{2,1,0:T(8,128)(2,1)} %get-tuple-element.40), channel_id=1, source_target_pairs={{0,24},{8,0},{16,8},{24,16},{1,25},{9,1},{17,9},{25,17},{2,26},{10... | collective-permute-start | bytes 1572872 | tf_op jit(solution)/shard_map/ppermute | solution.py:29
  11.7 0.6 collective-permute-start.9
  12.3 4.9 %all-to-all-start = ((bf16[8,1040,128]{2,1,0:T(8,128)(2,1)}), bf16[8,1040,128]{2,1,0:T(8,128)(2,1)S(1)}, u32[]{:S(2)}, u32[]{:S(2)}) async-start(bf16[8,1040,128]{2,1,0:T(8,128)(2,1)} %get-tuple-element.25), calls=%async_computation | async-start | bytes 4259840 | tf_op jit(solution)/shard_map/all_to_all | solution.py:386
  17.2 5.2 %collective-permute-done.10.refs_2_ = bf16[8,256,128]{2,1,0:T(8,128)(2,1)S(1)} collective-permute-done((bf16[8,256,128]{2,1,0:T(8,128)(2,1)}, bf16[8,256,128]{2,1,0:T(8,128)(2,1)S(1)}, u32[]{:S(2)}, u32[]{:S(2)}) %collective-permute-start.10) | collective-permute-done | bytes 524320 | tf_op jit(solution)/shard_map/ppermute | solution.py:29
  22.4 0.8 copy-done.1
  23.2 2.1 %collective-permute-done.11.refs_3_ = bf16[8,256,128]{2,1,0:T(8,128)(2,1)S(1)} collective-permute-done((bf16[8,256,128]{2,1,0:T(8,128)(2,1)}, bf16[8,256,128]{2,1,0:T(8,128)(2,1)S(1)}, u32[]{:S(2)}, u32[]{:S(2)}) %collective-permute-start.11) | collective-permute-done | bytes 524320 | tf_op jit(solution)/shard_map/ppermute | solution.py:29
  25.3 0.8 copy-done.3
  26.1 8.9 %collective-permute-done.9.refs_1_ = bf16[8,256,128]{2,1,0:T(8,128)(2,1)} collective-permute-done((bf16[8,256,128]{2,1,0:T(8,128)(2,1)}, bf16[8,256,128]{2,1,0:T(8,128)(2,1)}, u32[]{:S(2)}, u32[]{:S(2)}) %collective-permute-start.9) | collective-permute-done | bytes 524320 | tf_op jit(solution)/shard_map/ppermute | solution.py:29
  35.0 1.0 copy-done.2
  36.0 1.0 copy-done.4
  37.1 1.6 %copy-done.5 = bf16[4,512,512]{2,1,0:T(8,128)(2,1)S(1)} copy-done((bf16[4,512,512]{2,1,0:T(8,128)(2,1)S(1)}, bf16[4,512,512]{2,1,0:T(8,128)(2,1)}, u32[]{:S(2)}) %copy-start.5) | copy-done | bytes 2097176
  38.7 1.0 copy-done.11
  39.7 3.7 %delay_transform.3 = (bf16[8,256,128]{2,1,0:T(8,128)(2,1)S(1)}, bf16[8,256,128]{2,1,0:T(8,128)(2,1)}, bf16[8,256,128]{2,1,0:T(8,128)(2,1)}, bf16[8,256,128]{2,1,0:T(8,128)(2,1)S(1)}) custom-call(s32[1]{0:T(128)} %bitcast.me_ref, bf16[4,512,512]{2,1,0:T(8,128)(2,1)S(1)} %copy-done.5, bf16[8,256,128]{2,1,0:T(8,128)(2,1)S(1)} %copy-done.11, ...), custom_call_target="tpu_custom_call" | custom-call | flops 107374182400 | bytes 4194304 | tf_op jit(solution)/shard_map/delay_transform/pallas_call | solution.py:224
  43.4 2.0 %collective-permute-start.12 = (bf16[8,256,128]{2,1,0:T(8,128)(2,1)}, bf16[8,256,128]{2,1,0:T(8,128)(2,1)}, u32[]{:S(2)}, u32[]{:S(2)}) collective-permute-start(bf16[8,256,128]{2,1,0:T(8,128)(2,1)} %get-tuple-element.42), channel_id=1, source_target_pairs={{0,8},{8,16},{16,24},{24,0},{1,9},{9,17},{17,25},{25,1},{2,10},{10... | collective-permute-start | bytes 1572872 | tf_op jit(solution)/shard_map/ppermute | solution.py:29
  45.3 1.6 %collective-permute-start.13 = (bf16[8,256,128]{2,1,0:T(8,128)(2,1)}, bf16[8,256,128]{2,1,0:T(8,128)(2,1)}, u32[]{:S(2)}, u32[]{:S(2)}) collective-permute-start(bf16[8,256,128]{2,1,0:T(8,128)(2,1)} %get-tuple-element.43), channel_id=1, source_target_pairs={{0,16},{8,24},{16,0},{24,8},{1,17},{9,25},{17,1},{25,9},{2,18},{10... | collective-permute-start | bytes 1572872 | tf_op jit(solution)/shard_map/ppermute | solution.py:29
  46.9 1.1 collective-permute-start.14
  48.0 0.1 copy.10
  48.1 0.1 convert_element_type.48
  48.4 18.6 %all-to-all-done.refs_0_ = bf16[8,1040,128]{2,1,0:T(8,128)(2,1)S(1)} async-done(((bf16[8,1040,128]{2,1,0:T(8,128)(2,1)}), bf16[8,1040,128]{2,1,0:T(8,128)(2,1)S(1)}, u32[]{:S(2)}, u32[]{:S(2)}) %all-to-all-start) | async-done | bytes 2129952 | tf_op jit(solution)/shard_map/all_to_all | solution.py:386
  66.9 1.2 fusion.18
  68.1 2.4 %collective-permute-start = (bf16[8,256,128]{2,1,0:T(8,128)(2,1)}, bf16[8,256,128]{2,1,0:T(8,128)(2,1)}, u32[]{:S(2)}, u32[]{:S(2)}) collective-permute-start(bf16[8,256,128]{2,1,0:T(8,128)(2,1)} %get-tuple-element.47), channel_id=1, source_target_pairs={{0,8},{8,16},{16,24},{24,0},{1,9},{9,17},{17,25},{25,1},{2,10},{10... | collective-permute-start | bytes 1572872 | tf_op jit(solution)/shard_map/ppermute | solution.py:29
  70.5 0.5 collective-permute-start.1
  71.0 1.0 collective-permute-start.2
  72.0 2.9 %pad_maximum_fusion = bf16[8,1024,128]{2,1,0:T(8,128)(2,1)} fusion(bf16[8,256,128]{2,1,0:T(8,128)(2,1)} %collective-permute-done.14, bf16[8,256,128]{2,1,0:T(8,128)(2,1)} %collective-permute-done.13, bf16[8,256,128]{2,1,0:T(8,128)(2,1)} %collective-permute-done.12, bf16[8,256,128]{2,1,0:T(8,128)(2,1)S(1)} %get-tuple-element.41), kind=kLoop, calls=%fused_computation | loop fusion | flops 8388608 | bytes 4194304 | tf_op jit(solution)/shard_map/concatenate | solution.py:388
  74.9 4.4 %all-to-all-start.1 = ((bf16[8,1024,128]{2,1,0:T(8,128)(2,1)}), bf16[8,1024,128]{2,1,0:T(8,128)(2,1)}, u32[]{:S(2)}, u32[]{:S(2)}) async-start(bf16[8,1024,128]{2,1,0:T(8,128)(2,1)} %pad_maximum_fusion), calls=%async_computation.1 | async-start | bytes 4194304 | tf_op jit(solution)/shard_map/all_to_all | solution.py:389
  79.3 0.1 reshape.264
  79.4 4.9 %collective-permute-done.refs_1_ = bf16[8,256,128]{2,1,0:T(8,128)(2,1)} collective-permute-done((bf16[8,256,128]{2,1,0:T(8,128)(2,1)}, bf16[8,256,128]{2,1,0:T(8,128)(2,1)}, u32[]{:S(2)}, u32[]{:S(2)}) %collective-permute-start) | collective-permute-done | bytes 524320 | tf_op jit(solution)/shard_map/ppermute | solution.py:29
  84.2 9.8 %collective-permute-done.1.refs_2_ = bf16[8,256,128]{2,1,0:T(8,128)(2,1)} collective-permute-done((bf16[8,256,128]{2,1,0:T(8,128)(2,1)}, bf16[8,256,128]{2,1,0:T(8,128)(2,1)}, u32[]{:S(2)}, u32[]{:S(2)}) %collective-permute-start.1) | collective-permute-done | bytes 524320 | tf_op jit(solution)/shard_map/ppermute | solution.py:29
  94.1 1.6 %copy-done.6 = bf16[4,512,512]{2,1,0:T(8,128)(2,1)S(1)} copy-done((bf16[4,512,512]{2,1,0:T(8,128)(2,1)S(1)}, bf16[4,512,512]{2,1,0:T(8,128)(2,1)}, u32[]{:S(2)}) %copy-start.6) | copy-done | bytes 2097176
  95.6 3.3 %delay_transform.2 = (bf16[8,256,128]{2,1,0:T(8,128)(2,1)S(1)}, bf16[8,256,128]{2,1,0:T(8,128)(2,1)S(1)}, bf16[8,256,128]{2,1,0:T(8,128)(2,1)S(1)}, bf16[8,256,128]{2,1,0:T(8,128)(2,1)S(1)}) custom-call(s32[1]{0:T(128)} %bitcast.me_ref, bf16[4,512,512]{2,1,0:T(8,128)(2,1)S(1)} %copy-done.6, bf16[8,1040,128]{2,1,0:T(8,128)(2,1)S(1)} %all-to-all-done.refs_0_, ...), custom_call_target="tpu_custom_call" | custom-call | flops 107374182400 | bytes 4194304 | tf_op jit(solution)/shard_map/delay_transform/pallas_call | solution.py:224
  98.9 0.8 copy-done
  99.8 0.8 copy-done.7
  100.6 2.5 %collective-permute-start.5 = (f32[1152]{0:T(1024)S(1)}, f32[1152]{0:T(1024)S(1)}, u32[]{:S(2)}, u32[]{:S(2)}) collective-permute-start(f32[1152]{0:T(1024)S(1)} %pad_maximum_fusion.1), channel_id=1, source_target_pairs={{0,24},{8,0},{16,8},{24,16},{1,25},{9,1},{17,9},{25,17},{2,26},{10... | collective-permute-start | bytes 13832 | tf_op jit(solution)/shard_map/ppermute | solution.py:29
  103.1 0.5 collective-permute-start.4
  103.6 0.3 collective-permute-start.3
  103.9 0.1 broadcast_in_dim.96
  104.0 0.1 slice.178
  104.1 0.1 copy.11
  104.2 2.7 %collective-permute-start.6 = (bf16[8,256,128]{2,1,0:T(8,128)(2,1)}, bf16[8,256,128]{2,1,0:T(8,128)(2,1)S(1)}, u32[]{:S(2)}, u32[]{:S(2)}) collective-permute-start(bf16[8,256,128]{2,1,0:T(8,128)(2,1)} %copy-done), channel_id=1, source_target_pairs={{0,8},{8,16},{16,24},{24,0},{1,9},{9,17},{17,25},{25,1},{2,10},{10... | collective-permute-start | bytes 1572872 | tf_op jit(solution)/shard_map/ppermute | solution.py:29
  106.9 0.5 collective-permute-start.7
  107.4 1.0 collective-permute-start.8
  108.5 0.1 add.201
  108.6 0.1 add.204
  108.7 0.1 add.207
  108.8 0.1 select_select_fusion
  108.9 0.1 select_n.171.slot_ref
  109.0 0.1 slice.181
  109.2 0.1 slice.184
  109.4 0.1 slice.187
  109.8 1.8 %pair_weights.1 = (bf16[512,512]{1,0:T(8,128)(2,1)S(1)}, f32[64,512]{1,0:T(8,128)S(1)}) custom-call(s32[1,1024]{1,0:T(1,128)S(1)} %get-tuple-element.53.first_ref, s32[1,1024]{1,0:T(1,128)S(1)} %get-tuple-element.52.second_ref, f32[1,512]{1,0:T(1,128)S(1)} %bitcast.10, s32[1,512]{1,0:T(1,128)S(1)} %select_n.171.slot_ref), custom_call_target="tpu_custom_call" | custom-call | flops 536870912 | bytes 1048576 | tf_op jit(solution)/shard_map/pair_weights/pallas_call | solution.py:267
  111.6 0.8 copy-done.9
  112.4 15.9 %all-to-all-done.1.refs_0_ = bf16[8,1024,128]{2,1,0:T(8,128)(2,1)} async-done(((bf16[8,1024,128]{2,1,0:T(8,128)(2,1)}), bf16[8,1024,128]{2,1,0:T(8,128)(2,1)}, u32[]{:S(2)}, u32[]{:S(2)}) %all-to-all-start.1) | async-done | bytes 2097184 | tf_op jit(solution)/shard_map/all_to_all | solution.py:389
  128.3 1.0 copy-done.10
  129.3 3.8 %pair_sums.3 = f32[64,256]{1,0:T(8,128)S(1)} custom-call(bf16[512,512]{1,0:T(8,128)(2,1)S(1)} %copy-done.10, f32[64,512]{1,0:T(8,128)S(1)} %get-tuple-element.32.group_ref, bf16[8,1024,128]{2,1,0:T(8,128)(2,1)} %all-to-all-done.1.refs_0_), custom_call_target="tpu_custom_call" | custom-call | flops 1073741824 | bytes 2097152 | tf_op jit(solution)/shard_map/pair_sums/pallas_call | solution.py:314
  133.2 2.3 %pair_sums.2 = f32[64,256]{1,0:T(8,128)S(1)} custom-call(bf16[512,512]{1,0:T(8,128)(2,1)S(1)} %copy-done.10, f32[64,512]{1,0:T(8,128)S(1)} %get-tuple-element.32.group_ref, bf16[8,256,128]{2,1,0:T(8,128)(2,1)S(1)} %copy-done.8, bf16[8,256,128]{2,1,0:T(8,128)(2,1)S(1)} %collective-permute-done.6.refs_1_, ...), custom_call_target="tpu_custom_call" | custom-call | flops 1073741824 | bytes 2097152 | tf_op jit(solution)/shard_map/pair_sums/pallas_call | solution.py:314
  135.6 1.1 collective-permute-start.15
  136.7 1.5 %collective-permute-start.16 = (f32[16,256]{1,0:T(8,128)S(1)}, f32[16,256]{1,0:T(8,128)S(1)}, u32[]{:S(2)}, u32[]{:S(2)}) collective-permute-start(f32[16,256]{1,0:T(8,128)S(1)} %get-tuple-element.49), channel_id=1, source_target_pairs={{0,16},{8,24},{16,0},{24,8},{1,17},{9,25},{17,1},{25,9},{2,18},{10... | collective-permute-start | bytes 49160 | tf_op jit(solution)/shard_map/ppermute | solution.py:29
  138.2 1.4 %collective-permute-start.17 = (f32[16,256]{1,0:T(8,128)S(1)}, f32[16,256]{1,0:T(8,128)S(1)}, u32[]{:S(2)}, u32[]{:S(2)}) collective-permute-start(f32[16,256]{1,0:T(8,128)S(1)} %get-tuple-element.48), channel_id=1, source_target_pairs={{0,24},{8,0},{16,8},{24,16},{1,25},{9,1},{17,9},{25,17},{2,26},{10... | collective-permute-start | bytes 49160 | tf_op jit(solution)/shard_map/ppermute | solution.py:29
  139.6 0.6 collective-permute-done.15.refs_1_
  140.2 0.2 collective-permute-done.16.refs_2_
  140.4 1.5 %collective-permute-done.17.refs_3_ = f32[16,256]{1,0:T(8,128)S(1)} collective-permute-done((f32[16,256]{1,0:T(8,128)S(1)}, f32[16,256]{1,0:T(8,128)S(1)}, u32[]{:S(2)}, u32[]{:S(2)}) %collective-permute-start.17) | collective-permute-done | bytes 16416 | tf_op jit(solution)/shard_map/ppermute | solution.py:29
  141.9 1.1 interleave_delays.1
  (55 shorter events, 0.5 us)
Async XLA Ops:
  7.2 15.2 %collective-permute-start.10 = (bf16[8,256,128]{2,1,0:T(8,128)(2,1)}, bf16[8,256,128]{2,1,0:T(8,128)(2,1)S(1)}, u32[]{:S(2)}, u32[]{:S(2)}) collective-permute-start(bf16[8,256,128]{2,1,0:T(8,128)(2,1)} %get-tuple-element.39), channel_id=1, source_target_pairs={{0,16},{8,24},{16,0},{24,8},{1,17},{9,25},{17,1},{25,9},{2,18},{10... | collective-permute-start | bytes 1572872 | tf_op jit(solution)/shard_map/ppermute | solution.py:29
  10.3 15.1 %collective-permute-start.11 = (bf16[8,256,128]{2,1,0:T(8,128)(2,1)}, bf16[8,256,128]{2,1,0:T(8,128)(2,1)S(1)}, u32[]{:S(2)}, u32[]{:S(2)}) collective-permute-start(bf16[8,256,128]{2,1,0:T(8,128)(2,1)} %get-tuple-element.40), channel_id=1, source_target_pairs={{0,24},{8,0},{16,8},{24,16},{1,25},{9,1},{17,9},{25,17},{2,26},{10... | collective-permute-start | bytes 1572872 | tf_op jit(solution)/shard_map/ppermute | solution.py:29
  11.7 23.3 %collective-permute-start.9 = (bf16[8,256,128]{2,1,0:T(8,128)(2,1)}, bf16[8,256,128]{2,1,0:T(8,128)(2,1)}, u32[]{:S(2)}, u32[]{:S(2)}) collective-permute-start(bf16[8,256,128]{2,1,0:T(8,128)(2,1)} %get-tuple-element.38), channel_id=1, source_target_pairs={{0,8},{8,16},{16,24},{24,0},{1,9},{9,17},{17,25},{25,1},{2,10},{10... | collective-permute-start | bytes 1572872 | tf_op jit(solution)/shard_map/ppermute | solution.py:29
  12.3 54.6 %all-to-all-start = ((bf16[8,1040,128]{2,1,0:T(8,128)(2,1)}), bf16[8,1040,128]{2,1,0:T(8,128)(2,1)S(1)}, u32[]{:S(2)}, u32[]{:S(2)}) async-start(bf16[8,1040,128]{2,1,0:T(8,128)(2,1)} %get-tuple-element.25), calls=%async_computation | async-start | bytes 4259840 | tf_op jit(solution)/shard_map/all_to_all | solution.py:386
  22.4 0.8 copy-start.1
  25.3 0.8 copy-start.3
  35.0 1.0 copy-start.2
  36.0 1.0 copy-start.4
  37.1 1.6 %copy-start.5 = (bf16[4,512,512]{2,1,0:T(8,128)(2,1)S(1)}, bf16[4,512,512]{2,1,0:T(8,128)(2,1)}, u32[]{:S(2)}) copy-start(bf16[4,512,512]{2,1,0:T(8,128)(2,1)} %constant.173.clone.matrix_ref) | copy-start | bytes 6291460
  38.7 1.0 copy-start.11
  39.7 8.3 %copy-start.12 = (s32[256,2]{0,1:T(2,128)S(1)}, s32[256,2]{0,1:T(2,128)}, u32[]{:S(2)}) copy-start(s32[256,2]{0,1:T(2,128)} %param.11) | copy-start | bytes 6148
  39.7 8.6 %copy-start.13 = (s32[128]{0:T(128)S(1)}, s32[128]{0:T(128)}, u32[]{:S(2)}) copy-start(s32[128]{0:T(128)} %param.10) | copy-start | bytes 1540
  43.4 27.6 %collective-permute-start.12 = (bf16[8,256,128]{2,1,0:T(8,128)(2,1)}, bf16[8,256,128]{2,1,0:T(8,128)(2,1)}, u32[]{:S(2)}, u32[]{:S(2)}) collective-permute-start(bf16[8,256,128]{2,1,0:T(8,128)(2,1)} %get-tuple-element.42), channel_id=1, source_target_pairs={{0,8},{8,16},{16,24},{24,0},{1,9},{9,17},{17,25},{25,1},{2,10},{10... | collective-permute-start | bytes 1572872 | tf_op jit(solution)/shard_map/ppermute | solution.py:29
  45.3 26.7 %collective-permute-start.13 = (bf16[8,256,128]{2,1,0:T(8,128)(2,1)}, bf16[8,256,128]{2,1,0:T(8,128)(2,1)}, u32[]{:S(2)}, u32[]{:S(2)}) collective-permute-start(bf16[8,256,128]{2,1,0:T(8,128)(2,1)} %get-tuple-element.43), channel_id=1, source_target_pairs={{0,16},{8,24},{16,0},{24,8},{1,17},{9,25},{17,1},{25,9},{2,18},{10... | collective-permute-start | bytes 1572872 | tf_op jit(solution)/shard_map/ppermute | solution.py:29
  46.9 25.1 %collective-permute-start.14 = (bf16[8,256,128]{2,1,0:T(8,128)(2,1)S(1)}, bf16[8,256,128]{2,1,0:T(8,128)(2,1)}, u32[]{:S(2)}, u32[]{:S(2)}) collective-permute-start(bf16[8,256,128]{2,1,0:T(8,128)(2,1)S(1)} %get-tuple-element.44), channel_id=1, source_target_pairs={{0,24},{8,0},{16,8},{24,16},{1,25},{9,1},{17,9},{25,17},{2,26},{10... | collective-permute-start | bytes 1572872 | tf_op jit(solution)/shard_map/ppermute | solution.py:29
  68.1 16.1 %collective-permute-start = (bf16[8,256,128]{2,1,0:T(8,128)(2,1)}, bf16[8,256,128]{2,1,0:T(8,128)(2,1)}, u32[]{:S(2)}, u32[]{:S(2)}) collective-permute-start(bf16[8,256,128]{2,1,0:T(8,128)(2,1)} %get-tuple-element.47), channel_id=1, source_target_pairs={{0,8},{8,16},{16,24},{24,0},{1,9},{9,17},{17,25},{25,1},{2,10},{10... | collective-permute-start | bytes 1572872 | tf_op jit(solution)/shard_map/ppermute | solution.py:29
  70.5 23.5 %collective-permute-start.1 = (bf16[8,256,128]{2,1,0:T(8,128)(2,1)}, bf16[8,256,128]{2,1,0:T(8,128)(2,1)}, u32[]{:S(2)}, u32[]{:S(2)}) collective-permute-start(bf16[8,256,128]{2,1,0:T(8,128)(2,1)} %get-tuple-element.46), channel_id=1, source_target_pairs={{0,16},{8,24},{16,0},{24,8},{1,17},{9,25},{17,1},{25,9},{2,18},{10... | collective-permute-start | bytes 1572872 | tf_op jit(solution)/shard_map/ppermute | solution.py:29
  71.0 23.0 %collective-permute-start.2 = (bf16[8,256,128]{2,1,0:T(8,128)(2,1)}, bf16[8,256,128]{2,1,0:T(8,128)(2,1)}, u32[]{:S(2)}, u32[]{:S(2)}) collective-permute-start(bf16[8,256,128]{2,1,0:T(8,128)(2,1)} %get-tuple-element.45), channel_id=1, source_target_pairs={{0,24},{8,0},{16,8},{24,16},{1,25},{9,1},{17,9},{25,17},{2,26},{10... | collective-permute-start | bytes 1572872 | tf_op jit(solution)/shard_map/ppermute | solution.py:29
  74.9 53.4 %all-to-all-start.1 = ((bf16[8,1024,128]{2,1,0:T(8,128)(2,1)}), bf16[8,1024,128]{2,1,0:T(8,128)(2,1)}, u32[]{:S(2)}, u32[]{:S(2)}) async-start(bf16[8,1024,128]{2,1,0:T(8,128)(2,1)} %pad_maximum_fusion), calls=%async_computation.1 | async-start | bytes 4194304 | tf_op jit(solution)/shard_map/all_to_all | solution.py:389
  94.0 1.6 %copy-start.6 = (bf16[4,512,512]{2,1,0:T(8,128)(2,1)S(1)}, bf16[4,512,512]{2,1,0:T(8,128)(2,1)}, u32[]{:S(2)}) copy-start(bf16[4,512,512]{2,1,0:T(8,128)(2,1)} %constant.173.clone.matrix_ref) | copy-start | bytes 6291460
  98.9 0.8 copy-start
  99.8 0.8 copy-start.7
  100.6 6.9 %collective-permute-start.5 = (f32[1152]{0:T(1024)S(1)}, f32[1152]{0:T(1024)S(1)}, u32[]{:S(2)}, u32[]{:S(2)}) collective-permute-start(f32[1152]{0:T(1024)S(1)} %pad_maximum_fusion.1), channel_id=1, source_target_pairs={{0,24},{8,0},{16,8},{24,16},{1,25},{9,1},{17,9},{25,17},{2,26},{10... | collective-permute-start | bytes 13832 | tf_op jit(solution)/shard_map/ppermute | solution.py:29
  103.1 5.4 %collective-permute-start.4 = (f32[1152]{0:T(1024)S(1)}, f32[1152]{0:T(1024)S(1)}, u32[]{:S(2)}, u32[]{:S(2)}) collective-permute-start(f32[1152]{0:T(1024)S(1)} %pad_maximum_fusion.1), channel_id=1, source_target_pairs={{0,16},{8,24},{16,0},{24,8},{1,17},{9,25},{17,1},{25,9},{2,18},{10... | collective-permute-start | bytes 13832 | tf_op jit(solution)/shard_map/ppermute | solution.py:29
  103.6 5.1 %collective-permute-start.3 = (f32[1152]{0:T(1024)S(1)}, f32[1152]{0:T(1024)S(1)}, u32[]{:S(2)}, u32[]{:S(2)}) collective-permute-start(f32[1152]{0:T(1024)S(1)} %pad_maximum_fusion.1), channel_id=1, source_target_pairs={{0,8},{8,16},{16,24},{24,0},{1,9},{9,17},{17,25},{25,1},{2,10},{10... | collective-permute-start | bytes 13832 | tf_op jit(solution)/shard_map/ppermute | solution.py:29
  104.2 29.0 %collective-permute-start.6 = (bf16[8,256,128]{2,1,0:T(8,128)(2,1)}, bf16[8,256,128]{2,1,0:T(8,128)(2,1)S(1)}, u32[]{:S(2)}, u32[]{:S(2)}) collective-permute-start(bf16[8,256,128]{2,1,0:T(8,128)(2,1)} %copy-done), channel_id=1, source_target_pairs={{0,8},{8,16},{16,24},{24,0},{1,9},{9,17},{17,25},{25,1},{2,10},{10... | collective-permute-start | bytes 1572872 | tf_op jit(solution)/shard_map/ppermute | solution.py:29
  106.9 26.3 %collective-permute-start.7 = (bf16[8,256,128]{2,1,0:T(8,128)(2,1)S(1)}, bf16[8,256,128]{2,1,0:T(8,128)(2,1)S(1)}, u32[]{:S(2)}, u32[]{:S(2)}) collective-permute-start(bf16[8,256,128]{2,1,0:T(8,128)(2,1)S(1)} %get-tuple-element.35), channel_id=1, source_target_pairs={{0,16},{8,24},{16,0},{24,8},{1,17},{9,25},{17,1},{25,9},{2,18},{10... | collective-permute-start | bytes 1572872 | tf_op jit(solution)/shard_map/ppermute | solution.py:29
  107.4 25.7 %collective-permute-start.8 = (bf16[8,256,128]{2,1,0:T(8,128)(2,1)S(1)}, bf16[8,256,128]{2,1,0:T(8,128)(2,1)S(1)}, u32[]{:S(2)}, u32[]{:S(2)}) collective-permute-start(bf16[8,256,128]{2,1,0:T(8,128)(2,1)S(1)} %get-tuple-element.36), channel_id=1, source_target_pairs={{0,24},{8,0},{16,8},{24,16},{1,25},{9,1},{17,9},{25,17},{2,26},{10... | collective-permute-start | bytes 1572872 | tf_op jit(solution)/shard_map/ppermute | solution.py:29
  111.6 0.8 copy-start.9
  112.4 20.8 %copy-start.8 = (bf16[8,256,128]{2,1,0:T(8,128)(2,1)S(1)}, bf16[8,256,128]{2,1,0:T(8,128)(2,1)}, u32[]{:S(2)}) copy-start(bf16[8,256,128]{2,1,0:T(8,128)(2,1)} %copy-done.7) | copy-start | bytes 1572868
  128.3 1.0 copy-start.10
  135.6 4.7 %collective-permute-start.15 = (f32[16,256]{1,0:T(8,128)S(1)}, f32[16,256]{1,0:T(8,128)S(1)}, u32[]{:S(2)}, u32[]{:S(2)}) collective-permute-start(f32[16,256]{1,0:T(8,128)S(1)} %get-tuple-element.50), channel_id=1, source_target_pairs={{0,8},{8,16},{16,24},{24,0},{1,9},{9,17},{17,25},{25,1},{2,10},{10... | collective-permute-start | bytes 49160 | tf_op jit(solution)/shard_map/ppermute | solution.py:29
  136.7 3.7 %collective-permute-start.16 = (f32[16,256]{1,0:T(8,128)S(1)}, f32[16,256]{1,0:T(8,128)S(1)}, u32[]{:S(2)}, u32[]{:S(2)}) collective-permute-start(f32[16,256]{1,0:T(8,128)S(1)} %get-tuple-element.49), channel_id=1, source_target_pairs={{0,16},{8,24},{16,0},{24,8},{1,17},{9,25},{17,1},{25,9},{2,18},{10... | collective-permute-start | bytes 49160 | tf_op jit(solution)/shard_map/ppermute | solution.py:29
  138.2 3.7 %collective-permute-start.17 = (f32[16,256]{1,0:T(8,128)S(1)}, f32[16,256]{1,0:T(8,128)S(1)}, u32[]{:S(2)}, u32[]{:S(2)}) collective-permute-start(f32[16,256]{1,0:T(8,128)S(1)} %get-tuple-element.48), channel_id=1, source_target_pairs={{0,24},{8,0},{16,8},{24,16},{1,25},{9,1},{17,9},{25,17},{2,26},{10... | collective-permute-start | bytes 49160 | tf_op jit(solution)/shard_map/ppermute | solution.py:29

commit v3 on v2

v3 whole, which is shorter than its diff:
```python
import functools
import math

import jax
import jax.numpy as jnp
import ml_dtypes
import numpy as np
from jax import lax
from jax.experimental import pallas as pl
from jax.experimental.pallas import tpu as pltpu
from jax.sharding import PartitionSpec as P

GRP_DEV = 16
LANES = 128
LATE_COST = 10**9
EARLY_COST = 10**9
HALVES = 2
LOADS = 8
PAIR_ROWS = 2
BF16_PARTS = 3
EXTRA_ROWS = 16
HIGHEST = lax.Precision.HIGHEST
VMEM_LIMIT = 20 * 1024 * 1024
F32 = jnp.float32
BF16 = jnp.bfloat16
VMEM = pl.BlockSpec(memory_space=pltpu.VMEM)
SMEM = pl.BlockSpec(memory_space=pltpu.SMEM)
HBM = pl.BlockSpec(memory_space=pltpu.HBM)


def shifted(value, axis, steps):
    count = lax.axis_size(axis)
    pairs = [(source, (source + steps) % count) for source in range(count)]
    return lax.ppermute(value, axis, pairs)


def spread(pieces):
    return [pieces[0]] + [shifted(pieces[s], "band", s) for s in range(1, len(pieces))]


def cost(flops, bytes_accessed):
    return pl.CostEstimate(flops=flops, bytes_accessed=bytes_accessed, transcendentals=0)


def params(limit=VMEM_LIMIT):
    return pltpu.CompilerParams(vmem_limit_bytes=limit)


def class_matrices(full_width, classes):
    sub = full_width // classes
    channel = np.arange(sub)[None, :, None]
    delay = classes * np.arange(sub)[None, None, :] + np.arange(classes)[:, None, None]
    angle = (channel * delay % full_width) * (2.0 * math.pi / full_width)
    cosine, sine = np.cos(angle), np.sin(angle)
    upper = np.concatenate([cosine, -sine], axis=2)
    lower = np.concatenate([sine, cosine], axis=2)
    return np.concatenate([upper, lower], axis=1).astype(ml_dtypes.bfloat16)


def taper_window(full_width):
    angle = np.arange(full_width) * (2.0 * math.pi / full_width)
    window = (
        0.35875
        - 0.48829 * np.cos(angle)
        + 0.14128 * np.cos(2.0 * angle)
        - 0.01168 * np.cos(3.0 * angle)
    )
    return window.reshape(1, -1).astype(np.float32)


def tiles_of(ref, where, start, count, column):
    tiles = [ref[where, pl.ds((start + c) * column, column), :] for c in range(count)]
    return jnp.concatenate([t.reshape(-1, LANES) for t in tiles], axis=1)


def taper_kernel(times, parts, band_count, me_ref, order_ref, window_ref, flags_ref, vis_ref, *refs):
    early_ref, late_refs = refs[0], refs[1:-6]
    vis_buf, slab_ref, early_buf, late_buf, load_sems, sems = refs[-6:]
    slabs, rows, _ = slab_ref.shape
    chunks = load_sems.shape[0]
    height = rows // chunks
    loads = []
    for k in range(chunks):
        where = pl.ds(k * height * slabs, height * slabs)
        loads.append(
            pltpu.make_async_copy(vis_ref.at[where, :], vis_buf.at[where, :], load_sems.at[k])
        )
        loads[-1].start()
    blocks = early_buf.shape[0]
    count, halves = late_buf.shape[:2]
    column = rows // blocks
    peer = column // band_count
    tiles = slabs // times
    sub = tiles // parts * LANES
    me = me_ref[0]
    here = pl.ds(pl.multiple_of(me * sub, sub), sub)
    weight = window_ref[:, here] * flags_ref[:, here].astype(F32)
    weight = jnp.concatenate([weight] * parts, axis=1)
    order = jnp.transpose(jnp.broadcast_to(order_ref[...].astype(F32), (LANES, rows)))
    if peer % 8 == 0:
        order = order.reshape(band_count, blocks, peer, LANES).transpose(1, 0, 2, 3)
        order = order.reshape(rows, LANES)
    lane = lax.broadcasted_iota(jnp.int32, (rows, LANES), 1)
    pick = [(lane + c == order.astype(jnp.int32)).astype(BF16) for c in range(0, rows, LANES)]
    pick = jnp.concatenate(pick, axis=1)
    for k, load in enumerate(loads):
        load.wait()
        block = vis_buf[k * height * slabs : (k + 1) * height * slabs, :]
        block = jnp.transpose(block.reshape(height, slabs, LANES), (1, 0, 2))
        slab_ref[:, k * height : (k + 1) * height, :] = block
    total = jnp.zeros((rows, LANES), F32)
    copies = []
    for half in (1, 0):
        for s in range(count):
            time = half * count + lax.rem(me + s, count)
            source = [
                slab_ref[(time * (tiles // parts) + tile) * parts + part]
                for part in range(parts)
                for tile in range(tiles // parts)
            ]
            moved = jnp.dot(pick, jnp.concatenate(source, axis=1), preferred_element_type=F32)
            tapered = (moved * weight).astype(BF16)
            for c in range(tiles):
                tile = tapered[:, c * LANES : (c + 1) * LANES]
                wide = tile.astype(F32)
                total = total + wide * wide
                tile = tile.reshape(blocks, column, LANES)
                if half:
                    tile = tile.reshape(halves, blocks // halves, column, LANES)
                    late_buf[s, :, :, c * column : (c + 1) * column] = tile
                else:
                    start = (s * tiles + c) * column
                    early_buf[:, start : start + column] = tile
            if half:
                new = [
                    pltpu.make_async_copy(
                        late_buf.at[s, h], late_refs[h * count + s], sems.at[h * count + s]
                    )
                    for h in range(halves)
                ]
            else:
                where = pl.ds(s * tiles * column, tiles * column)
                new = [
                    pltpu.make_async_copy(
                        early_buf.at[:, where], early_ref.at[:, where], sems.at[halves * count + s]
                    )
                ]
            for copy in new:
                copy.start()
            copies += new
    energy = lax.dot_general(
        jnp.ones((EXTRA_ROWS, LANES), F32),
        total,
        (((1,), (1,)), ((), ())),
        precision=HIGHEST,
        preferred_element_type=F32,
    )
    row = lax.broadcasted_iota(jnp.int32, energy.shape, 0)
    rest, extra = energy, jnp.zeros_like(energy)
    for k in range(BF16_PARTS):
        part = rest.astype(BF16).astype(F32)
        extra = jnp.where(row == k, part, extra)
        rest = rest - part
    start = count * tiles * column
    for j in range(blocks):
        mine = extra[:, j * column : (j + 1) * column]
        mine = jnp.concatenate([mine, jnp.zeros((EXTRA_ROWS, LANES - column), F32)], axis=1)
        early_buf[j, start:] = mine.astype(BF16)
    where = pl.ds(start, EXTRA_ROWS)
    copy = pltpu.make_async_copy(
        early_buf.at[:, where], early_ref.at[:, where], sems.at[(halves + 1) * count]
    )
    copy.start()
    for copy in copies + [copy]:
        copy.wait()


def taper(band_count, blocks, me, order, window, flags, visibilities):
    rows, times, parts, sub = visibilities.shape
    count, lanes, tiles = times // 2, parts * sub, sub // LANES
    column = rows // blocks
    vis = visibilities.reshape(rows, times, parts, tiles, LANES).transpose(0, 1, 3, 2, 4)
    vis = vis.reshape(rows * times * tiles * parts, LANES)
    piece = (blocks // HALVES, parts * tiles * column, LANES)
    early = (blocks, count * parts * tiles * column + EXTRA_ROWS, LANES)
    return pl.pallas_call(
        functools.partial(taper_kernel, times, parts, band_count),
        out_shape=[jax.ShapeDtypeStruct(shape, BF16) for shape in [early] + [piece] * (HALVES * count)],
        in_specs=[SMEM, VMEM, VMEM, VMEM, HBM],
        out_specs=[HBM] * (1 + HALVES * count),
        scratch_shapes=[
            pltpu.VMEM(vis.shape, BF16),
            pltpu.VMEM((vis.shape[0] // rows, rows, LANES), BF16),
            pltpu.VMEM(early, BF16),
            pltpu.VMEM((count, HALVES) + piece, BF16),
            pltpu.SemaphoreType.DMA((LOADS,)),
            pltpu.SemaphoreType.DMA(((HALVES + 1) * count + 1,)),
        ],
        compiler_params=params(60 * 1024 * 1024),
        cost_estimate=cost(2 * times * rows * rows * lanes, 4 * times * rows * lanes),
        name="taper_rows",
    )(me, order, window, flags, vis)


def delay_kernel(half, me_ref, matrix_hbm, *refs):
    sources, outs = refs[:4], refs[4:8]
    x_refs, matrix_ref, mixed, out_buf, sems = refs[8:]
    blocks, height, _ = x_refs.shape[1:]
    lanes = mixed.shape[2]
    tiles = lanes // LANES
    column = height // tiles
    middle = lanes // 2
    me = me_ref[0]
    own = sources[0].at[pl.ds(half * blocks, blocks), pl.ds(0, height)]
    loads = [
        pltpu.make_async_copy(source, x_refs.at[s], sems.at[s])
        for s, source in enumerate([own] + [x.at[:, pl.ds(0, height)] for x in sources[1:]])
    ]
    loads.append(pltpu.make_async_copy(matrix_hbm, matrix_ref, sems.at[4]))
    for load in loads:
        load.start()
    for load in loads[:4]:
        load.wait()
    x = [tiles_of(x_refs.at[s], slice(None), 0, tiles, column).astype(F32) for s in range(4)]
    a, b, c, d = x[0] + x[2], x[0] - x[2], x[1] + x[3], x[1] - x[3]
    turned = jnp.concatenate([-d[:, middle:], d[:, :middle]], axis=1)
    for r, value in enumerate((a + c, b + turned, a - c, b - turned)):
        if r:
            turns = lax.rem(r * me, 4)
            real = jnp.where(turns == 0, 1.0, jnp.where(turns == 2, -1.0, 0.0)).astype(F32)
            imag = jnp.where(turns == 3, 1.0, jnp.where(turns == 1, -1.0, 0.0)).astype(F32)
            if r == 2:
                value = value * real
            else:
                other = jnp.concatenate([-value[:, middle:], value[:, :middle]], axis=1)
                value = value * real + other * imag
        mixed[r] = value.astype(BF16)
    loads[4].wait()
    stores = []
    for s in (1, 2, 3, 0):
        r = lax.rem(me + s, 4)
        out = jnp.dot(mixed[r], matrix_ref[r], preferred_element_type=F32).astype(BF16)
        for c in range(tiles):
            tile = out[:, c * LANES : (c + 1) * LANES].reshape(blocks, column, LANES)
            out_buf[s, :, c * column : (c + 1) * column] = tile
        stores.append(pltpu.make_async_copy(out_buf.at[s], outs[s], sems.at[5 + s]))
        stores[-1].start()
    for store in stores:
        store.wait()


def delay_transform(me, matrices, height, pieces, flops, half=0):
    _, lanes, _ = matrices.shape
    blocks = pieces[1].shape[0]
    piece = (blocks, height, LANES)
    rows = blocks * height * LANES // lanes
    return pl.pallas_call(
        functools.partial(delay_kernel, half),
        out_shape=[jax.ShapeDtypeStruct(piece, BF16)] * 4,
        in_specs=[SMEM] + [HBM] * 5,
        out_specs=[HBM] * 4,
        scratch_shapes=[
            pltpu.VMEM((4,) + piece, BF16),
            pltpu.VMEM(matrices.shape, BF16),
            pltpu.VMEM((4, rows, lanes), BF16),
            pltpu.VMEM((4,) + piece, BF16),
            pltpu.SemaphoreType.DMA((9,)),
        ],
        compiler_params=params(),
        cost_estimate=cost(flops, 16 * rows * lanes),
        name="delay_transform",
    )(me, matrices, *pieces)


def join_kernel(*refs):
    pieces, out_ref, buf, load_sems, store_sems = refs[:-4], *refs[-4:]
    count = len(pieces) // HALVES
    blocks, height, _ = pieces[0].shape
    loads, stores = [], []
    for k, piece in enumerate(pieces):
        loads.append(pltpu.make_async_copy(piece, buf.at[k], load_sems.at[k]))
        loads[-1].start()
    for k, load in enumerate(loads):
        load.wait()
        half, s = k // count, k % count
        where = out_ref.at[pl.ds(half * blocks, blocks), pl.ds(s * height, height)]
        stores.append(pltpu.make_async_copy(buf.at[k], where, store_sems.at[k]))
        stores[-1].start()
    for store in stores:
        store.wait()


def join(pieces):
    blocks, height, _ = pieces[0].shape
    out = (blocks * HALVES, height * (len(pieces) // HALVES), LANES)
    return pl.pallas_call(
        join_kernel,
        out_shape=jax.ShapeDtypeStruct(out, BF16),
        in_specs=[HBM] * len(pieces),
        out_specs=HBM,
        scratch_shapes=[
            pltpu.VMEM((len(pieces), blocks, height, LANES), BF16),
            pltpu.SemaphoreType.DMA((len(pieces),)),
            pltpu.SemaphoreType.DMA((len(pieces),)),
        ],
        compiler_params=params(),
        name="join_pieces",
    )(*pieces)


def pair_weights_kernel(peer, samples, height, me_ref, *refs):
    sources, mix_ref, group_ref, table_ref, sems = refs[:-4], *refs[-4:]
    band_count = len(sources)
    rows = mix_ref.shape[0]
    column = band_count * peer
    owned = rows // band_count
    me = me_ref[0]
    own = [sources[0]] + [x.at[:, pl.ds(height, EXTRA_ROWS)] for x in sources[1:]]
    loads = [pltpu.make_async_copy(x, table_ref.at[s], sems.at[s]) for s, x in enumerate(own)]
    for load in loads:
        load.start()
    for load in loads:
        load.wait()

    def line(table, start, count):
        return jnp.concatenate([table[start + k : start + k + 1] for k in range(count)], axis=1)

    energy, first, second, slot = 0.0, [], [], 0.0
    local = lax.broadcasted_iota(jnp.int32, (owned, rows), 0)
    place = lax.broadcasted_iota(jnp.int32, (owned, rows), 1)
    for s in range(band_count):
        owner = lax.rem(me + band_count - s, band_count)
        table = table_ref[s].astype(F32).reshape(-1, LANES)
        at = 0
        for _ in range(BF16_PARTS):
            energy = energy + line(table, at, rows // LANES)
            at += rows // LANES
        for out in (first, second):
            pair = line(table, at, PAIR_ROWS).astype(jnp.int32)
            at += PAIR_ROWS
            own = pair < owned
            pair = jnp.where(own, pair, pair - owned)
            source = jnp.where(own, owner, lax.rem(owner + band_count - 1, band_count))
            out.append(pair // peer * column + source * peer + pair % peer)
        groups = line(table, at, owned // LANES) + GRP_DEV * ((band_count - s) % band_count)
        here = local // peer * column + owner * peer + local % peer == place
        groups = jnp.broadcast_to(groups, (8, owned)).astype(BF16)
        slot = slot + jnp.dot(groups, here.astype(BF16), preferred_element_type=F32)
    energy = energy / samples + 1e-06
    place = lax.broadcasted_iota(jnp.int32, (rows, band_count * PAIR_ROWS * LANES), 0)
    contract_last = (((1,), (1,)), ((), ()))
    counts = lax.dot_general(
        (place == jnp.concatenate(first, axis=1)).astype(BF16),
        (place == jnp.concatenate(second, axis=1)).astype(BF16),
        contract_last,
        preferred_element_type=F32,
    )
    inverse = 1.0 / energy
    scale = inverse * jnp.sqrt(inverse)
    mix_ref[...] = (counts * scale).astype(BF16)
    partner = lax.dot_general(
        jnp.broadcast_to(inverse, (8, rows)),
        counts,
        contract_last,
        precision=HIGHEST,
        preferred_element_type=F32,
    )[0:1]
    slots = group_ref.shape[0]
    member = lax.broadcasted_iota(jnp.int32, (slots, rows), 0) == slot[0:1].astype(jnp.int32)
    denom = jnp.sum(jnp.where(member, inverse * partner, 0.0), axis=1, keepdims=True)
    group_ref[...] = jnp.where(member, scale, 0.0) / denom


def pair_weights(me, peer, samples, rows, height, tables):
    slots = GRP_DEV * len(tables)
    return pl.pallas_call(
        functools.partial(pair_weights_kernel, peer, samples, height),
        out_shape=[
            jax.ShapeDtypeStruct((rows, rows), BF16),
            jax.ShapeDtypeStruct((slots, rows), F32),
        ],
        in_specs=[SMEM] + [HBM] * len(tables),
        out_specs=[VMEM] * 2,
        scratch_shapes=[
            pltpu.VMEM((len(tables),) + tables[0].shape, BF16),
            pltpu.SemaphoreType.DMA((len(tables),)),
        ],
        compiler_params=params(),
        cost_estimate=cost(4 * rows * rows * rows, 4 * rows * rows),
        name="pair_weights",
    )(me, *tables)


def pair_kernel(by_hand, mix_ref, group_ref, before_ref, *refs):
    if by_hand:
        z_refs, out_ref, buf, sems = refs[:1], *refs[1:]
        height = buf.shape[2]
        loads = [
            pltpu.make_async_copy(z_refs[0].at[:, pl.ds(t * height, height)], buf.at[t], sems.at[t])
            for t in range(buf.shape[0])
        ]
        for load in loads:
            load.start()
        parts, count = 1, len(loads)
    else:
        z_refs, out_ref = refs[:-1], refs[-1]
        parts, count = HALVES, len(z_refs) // HALVES
    rows = mix_ref.shape[0]
    slots, half = out_ref.shape
    tiles = 2 * half // LANES
    column = rows // (parts * z_refs[0].shape[0])
    value = 0.0
    for t in range(count):
        if by_hand:
            loads[t].wait()
            window = tiles_of(buf.at[t], slice(None), 0, tiles, column)
        else:
            here = z_refs[t * parts : (t + 1) * parts]
            window = [tiles_of(ref, slice(None), 0, tiles, column) for ref in here]
            window = jnp.concatenate(window, axis=0)
        mixed = jnp.dot(mix_ref[...], window, preferred_element_type=F32)
        mixed = window.astype(F32) * mixed
        value = value + (mixed[:, :half] + mixed[:, half:])
    group = group_ref[...]
    group_high, value_high = group.astype(BF16), value.astype(BF16)
    group_low = (group - group_high.astype(F32)).astype(BF16)
    value_low = (value - value_high.astype(F32)).astype(BF16)
    both = jnp.concatenate([group_high, group_low], axis=0)
    part = jnp.dot(both, value_high, preferred_element_type=F32)
    part = part[:slots] + part[slots:]
    part = part + jnp.dot(group_high, value_low, preferred_element_type=F32)
    out_ref[...] = before_ref[...] + part


def pair_sums(mix, group, before, pieces):
    rows = mix.shape[1]
    half = before.shape[1]
    blocks, length, _ = pieces[0].shape
    by_hand = len(pieces) == 1
    scratch = []
    if by_hand:
        height = 2 * half // LANES * rows // blocks
        count = length // height
        scratch = [
            pltpu.VMEM((count, blocks, height, LANES), BF16),
            pltpu.SemaphoreType.DMA((count,)),
        ]
    else:
        count = len(pieces) // HALVES
    return pl.pallas_call(
        functools.partial(pair_kernel, by_hand),
        out_shape=jax.ShapeDtypeStruct(before.shape, F32),
        in_specs=[VMEM] * 3 + [HBM if by_hand else VMEM] * len(pieces),
        out_specs=VMEM,
        scratch_shapes=scratch,
        compiler_params=params(),
        cost_estimate=cost(4 * count * rows * rows * half, 4 * count * rows * half),
        name="pair_sums",
    )(mix, group, before, *pieces)


def interleave_kernel(me_ref, *refs):
    pieces, out_ref = refs[:-1], refs[-1]
    count = len(pieces)
    width = pieces[0].shape[1]
    me = me_ref[0]
    row = lax.broadcasted_iota(jnp.int32, (width, count * width), 0)
    column = lax.broadcasted_iota(jnp.int32, (width, count * width), 1)
    total = 0.0
    for s in range(count):
        r = lax.rem(me + count - s, count)
        pick = (column == row * count + r).astype(BF16)
        rest, parts = pieces[s][...], []
        for _ in range(BF16_PARTS):
            parts.append(rest.astype(BF16))
            rest = rest - parts[-1].astype(F32)
        parts = jnp.concatenate(parts, axis=0)
        total = total + jnp.dot(parts, pick, preferred_element_type=F32)
    groups = out_ref.shape[0]
    out_ref[...] = sum(total[k * groups : (k + 1) * groups] for k in range(BF16_PARTS))


def interleave(me, pieces):
    groups, width = pieces[0].shape
    return pl.pallas_call(
        interleave_kernel,
        out_shape=jax.ShapeDtypeStruct((groups, width * len(pieces)), F32),
        in_specs=[SMEM] + [VMEM] * len(pieces),
        out_specs=VMEM,
        compiler_params=params(),
        name="interleave_delays",
    )(me, *pieces)


def on_device(matrices, window, visibilities, send_order, channel_flags, group_ids, pair_list):
    band_count = lax.axis_size("band")
    block_count = lax.axis_size("bl")
    rows, times, parts, sub = visibilities.shape
    peer = rows // (band_count * block_count)
    column = band_count * peer
    height = parts * sub // LANES * column
    band = lax.axis_index("band").astype(jnp.int32)
    me = band.reshape(1)

    order = send_order
    if peer % 8:
        order = order.reshape(band_count, block_count, peer).transpose(1, 0, 2).reshape(1, rows)
    flags = channel_flags.reshape(1, -1)
    tables = jnp.concatenate([pair_list[:, 0], pair_list[:, 1], group_ids])
    tables = tables.astype(BF16).reshape(-1, LANES)
    early, *late = taper(band_count, block_count, me, order, window, flags, visibilities)

    early = lax.all_to_all(early, "bl", split_axis=0, concat_axis=0, tiled=True)
    late = [late[h * band_count : (h + 1) * band_count] for h in range(HALVES)]
    late = [spread(pieces) for pieces in late]
    late = [spread(delay_transform(me, matrices, height, pieces, LATE_COST)) for pieces in late]
    late = join([piece for pieces in late for piece in pieces])
    early, late = lax.optimization_barrier((early, late))
    late = lax.all_to_all(late, "bl", split_axis=0, concat_axis=0, tiled=True)

    some = block_count // HALVES
    energy = early[:, band_count * height :][:, :BF16_PARTS, :column]
    energy = energy.transpose(1, 0, 2).reshape(-1, LANES)
    table = jnp.concatenate([energy, tables], axis=0)
    table = jnp.pad(table, ((0, some * EXTRA_ROWS - table.shape[0]), (0, 0)))
    table = table.reshape(some, EXTRA_ROWS, LANES)
    pieces = [
        [
            early[h * some : (h + 1) * some, s * height : (s + 1) * height]
            for s in range(1, band_count)
        ]
        for h in range(HALVES)
    ]
    pieces[0] = [jnp.concatenate([piece, table], axis=1) for piece in pieces[0]]
    pieces = [spread([early] + pieces[h]) for h in range(HALVES)]
    early = [
        spread(delay_transform(me, matrices, height, pieces[h], EARLY_COST, h))
        for h in range(HALVES)
    ]
    mix, group = pair_weights(me, peer, parts * times, rows, height, [table] + pieces[0][1:])

    sums = jnp.zeros((GRP_DEV * band_count, sub), F32)
    by_time = [early[h][s] for s in range(band_count) for h in range(HALVES)]
    sums = pair_sums(mix, group, sums, [late])
    sums = pair_sums(mix, group, sums, by_time)
    sums = sums.reshape(band_count, GRP_DEV, sub)
    return interleave(me, spread([sums[s] for s in range(band_count)]))


def solution(mesh):
    band_count = mesh.shape["band"]

    def whole(visibilities, send_order, channel_flags, group_ids, pair_list):
        full_width = visibilities.shape[3]
        matrices = jnp.asarray(class_matrices(full_width, band_count))
        window = jnp.asarray(taper_window(full_width))
        mapped = jax.shard_map(
            on_device,
            mesh=mesh,
            in_specs=(
                P(),
                P(),
                P("bl", None, None, "band"),
                P("bl", None),
                P(),
                P(("band", "bl")),
                P(("band", "bl"), None),
            ),
            out_specs=P(("band", "bl"), None),
            check_vma=False,
        )
        return mapped(
            matrices, window, visibilities, send_order, channel_flags, group_ids, pair_list
        )

    return whole
```

time: 144 us -> 131 us (0.910)
  waiting for transfers between devices: 67.8 us -> 48.4 us
  starting transfers between devices: 34.4 us -> 51 us
  local copies, waits for them, and re-layouts: 14.2 us -> 6.48 us
  other arithmetic: 3.14 us -> 1.05 us
    all_to_all x1, waiting for transfers between devices: 18.6 us -> 0.01 us  [on_device(): early = lax.all_to_all(early, 'bl', split_axis=0, concat_axis=0, tiled=True)]
    ppermute x18 -> x27, starting transfers between devices: 25.2 us -> 39.7 us  [shifted(): return lax.ppermute(value, axis, pairs)]
    unnamed x28 -> x24, local copies, waits for them, and re-layouts: 11.3 us -> 5.26 us
    all_to_all x1, waiting for transfers between devices: 15.9 us -> 11.2 us  [on_device(): late = lax.all_to_all(late, 'bl', split_axis=0, concat_axis=0, tiled=True)]
    ppermute x18 -> x27, waiting for transfers between devices: 33.2 us -> 37.1 us  [shifted(): return lax.ppermute(value, axis, pairs)]
    concatenate x2, other arithmetic: 2.88 us -> 1.02 us  [the longest x1 1.01 us: on_device(): pieces[0] = [jnp.concatenate([piece, table], axis=1) for piece in pieces[0]]]
    all_to_all x1, starting transfers between devices: 4.87 us -> 6.47 us  [on_device(): early = lax.all_to_all(early, 'bl', split_axis=0, concat_axis=0, tiled=True)]
    pallas_call x5 -> x8, Pallas kernels: 14.9 us -> 15.2 us  [the longest x4 8.17 us: delay_transform(): pl.pallas_call(functools.partial(delay_kernel, half), out_shape=[jax.Shap...]
  transfers between devices with their start and end apart: 20 -> 29, of which waited for: 10 -> 15; matrix products, arithmetic and copies ran while one was open for 4% -> 2% of each run, Pallas kernels for 9% -> 10%
where the time goes in v3:
time: 131 us; the launch traced here: 130 us
  starting transfers between devices  51 us (39%)
  waiting for transfers between devices  48.4 us (37%)
  Pallas kernels  23 us (18%)
  local copies, waits for them, and re-layouts  6.48 us (5%)
    ppermute x27, starting transfers between devices, shifted(): return lax.ppermute(value, axis, pairs)  39.7 us
    ppermute x27, waiting for transfers between devices, shifted(): return lax.ppermute(value, axis, pairs)  37.1 us
    all_to_all x1, waiting for transfers between devices, on_device(): late = lax.all_to_all(late, 'bl', split_axis=0, concat_axis=0, tiled=True)  11.2 us
    pallas_call x4, Pallas kernels, delay_transform(): pl.pallas_call(functools.partial(delay_kernel, half), out_shape=[jax.Shap...  8.17 us
    pallas_call x1, Pallas kernels, taper(): pl.pallas_call(functools.partial(taper_kernel, times, parts, band_count),...  6.75 us
    all_to_all x1, starting transfers between devices, on_device(): early = lax.all_to_all(early, 'bl', split_axis=0, concat_axis=0, tiled=True)  6.47 us
    unnamed x24, local copies, waits for them, and re-layouts  5.26 us
    all_to_all x1, starting transfers between devices, on_device(): late = lax.all_to_all(late, 'bl', split_axis=0, concat_axis=0, tiled=True)  4.87 us
  transfers between devices with their start and end apart: 29, of which 15 were waited for; matrix products, arithmetic and copies ran while one was open for 2% of the time, Pallas kernels for 10%

profile of v3, /device:TPU:0, one launch (start us, length us, event | category | flops | bytes accessed | tf_op | source)
XLA Modules:
  0.0 130.2 jit_solution(9138224849522316576)
XLA Ops:
  0.0 6.7 %taper_rows.1 = (bf16[8,1040,128]{2,1,0:T(8,128)(2,1)}, bf16[4,256,128]{2,1,0:T(8,128)(2,1)}, bf16[4,256,128]{2,1,0:T(8,128)(2,1)}, bf16[4,256,128]{2,1,0:T(8,12...) custom-call(s32[1]{0:T(128)} %bitcast.me_ref, ...), custom_call_target="tpu_custom_call" | custom-call | flops 2147483648 | bytes 8388608 | tf_op jit(solution)/shard_map/taper_rows/pallas_call | solution.py:186
  6.8 6.5 %all-to-all-start = ((bf16[8,1040,128]{2,1,0:T(8,128)(2,1)}), bf16[8,1040,128]{2,1,0:T(8,128)(2,1)S(1)}, u32[]{:S(2)}, u32[]{:S(2)}) async-start(bf16[8,1040,128]{2,1,0:T(8,128)(2,1)} %get-tuple-element.34), calls=%async_computation | async-start | bytes 4259840 | tf_op jit(solution)/shard_map/all_to_all | solution.py:513
  13.3 1.5 %collective-permute-start.6 = (bf16[4,256,128]{2,1,0:T(8,128)(2,1)}, bf16[4,256,128]{2,1,0:T(8,128)(2,1)S(1)}, u32[]{:S(2)}, u32[]{:S(2)}) collective-permute-start(bf16[4,256,128]{2,1,0:T(8,128)(2,1)} %get-tuple-element.44), channel_id=1, source_target_pairs={{0,8},{8,16},{16,24},{24,0},{1,9},{9,17},{17,25},{25,1},{2,10},{10... | collective-permute-start | bytes 786440 | tf_op jit(solution)/shard_map/ppermute | solution.py:34
  14.8 1.5 %collective-permute-start.7 = (bf16[4,256,128]{2,1,0:T(8,128)(2,1)}, bf16[4,256,128]{2,1,0:T(8,128)(2,1)S(1)}, u32[]{:S(2)}, u32[]{:S(2)}) collective-permute-start(bf16[4,256,128]{2,1,0:T(8,128)(2,1)} %get-tuple-element.45), channel_id=1, source_target_pairs={{0,16},{8,24},{16,0},{24,8},{1,17},{9,25},{17,1},{25,9},{2,18},{10... | collective-permute-start | bytes 786440 | tf_op jit(solution)/shard_map/ppermute | solution.py:34
  16.3 1.4 %collective-permute-start.8 = (bf16[4,256,128]{2,1,0:T(8,128)(2,1)}, bf16[4,256,128]{2,1,0:T(8,128)(2,1)S(1)}, u32[]{:S(2)}, u32[]{:S(2)}) collective-permute-start(bf16[4,256,128]{2,1,0:T(8,128)(2,1)} %get-tuple-element.46), channel_id=1, source_target_pairs={{0,24},{8,0},{16,8},{24,16},{1,25},{9,1},{17,9},{25,17},{2,26},{10... | collective-permute-start | bytes 786440 | tf_op jit(solution)/shard_map/ppermute | solution.py:34
  17.7 0.6 collective-permute-start
  18.3 0.5 collective-permute-start.1
  18.8 4.7 %collective-permute-done.6.refs_1_ = bf16[4,256,128]{2,1,0:T(8,128)(2,1)S(1)} collective-permute-done((bf16[4,256,128]{2,1,0:T(8,128)(2,1)}, bf16[4,256,128]{2,1,0:T(8,128)(2,1)S(1)}, u32[]{:S(2)}, u32[]{:S(2)}) %collective-permute-start.6) | collective-permute-done | bytes 262176 | tf_op jit(solution)/shard_map/ppermute | solution.py:34
  23.5 1.5 %collective-permute-start.2 = (bf16[4,256,128]{2,1,0:T(8,128)(2,1)S(1)}, bf16[4,256,128]{2,1,0:T(8,128)(2,1)S(1)}, u32[]{:S(2)}, u32[]{:S(2)}) collective-permute-start(bf16[4,256,128]{2,1,0:T(8,128)(2,1)S(1)} %copy-done.8), channel_id=1, source_target_pairs={{0,24},{8,0},{16,8},{24,16},{1,25},{9,1},{17,9},{25,17},{2,26},{10... | collective-permute-start | bytes 786440 | tf_op jit(solution)/shard_map/ppermute | solution.py:34
  25.0 4.1 %collective-permute-done.7.refs_2_ = bf16[4,256,128]{2,1,0:T(8,128)(2,1)S(1)} collective-permute-done((bf16[4,256,128]{2,1,0:T(8,128)(2,1)}, bf16[4,256,128]{2,1,0:T(8,128)(2,1)S(1)}, u32[]{:S(2)}, u32[]{:S(2)}) %collective-permute-start.7) | collective-permute-done | bytes 262176 | tf_op jit(solution)/shard_map/ppermute | solution.py:34
  29.2 0.0 collective-permute-done.8.refs_3_
  29.2 1.6 %copy-done.1 = bf16[4,512,512]{2,1,0:T(8,128)(2,1)S(1)} copy-done((bf16[4,512,512]{2,1,0:T(8,128)(2,1)S(1)}, bf16[4,512,512]{2,1,0:T(8,128)(2,1)}, u32[]{:S(2)}) %copy-start.1) | copy-done | bytes 2097176
  30.8 2.0 %delay_transform.5 = (bf16[4,256,128]{2,1,0:T(8,128)(2,1)S(1)}, bf16[4,256,128]{2,1,0:T(8,128)(2,1)S(1)}, bf16[4,256,128]{2,1,0:T(8,128)(2,1)S(1)}, bf16[4,256,128]{2,1,0:T(8,128)(2,1)S(1)}) custom-call(s32[1]{0:T(128)} %bitcast.me_ref, bf16[4,512,512]{2,1,0:T(8,128)(2,1)S(1)} %copy-done.1, bf16[4,256,128]{2,1,0:T(8,128)(2,1)S(1)} %copy-done.6, ...), custom_call_target="tpu_custom_call" | custom-call | flops 1000000000 | bytes 2097152 | tf_op jit(solution)/shard_map/delay_transform/pallas_call | solution.py:257
  32.8 1.6 %collective-permute-start.10 = (bf16[4,256,128]{2,1,0:T(8,128)(2,1)S(1)}, bf16[4,256,128]{2,1,0:T(8,128)(2,1)S(1)}, u32[]{:S(2)}, u32[]{:S(2)}) collective-permute-start(bf16[4,256,128]{2,1,0:T(8,128)(2,1)S(1)} %get-tuple-element.49), channel_id=1, source_target_pairs={{0,16},{8,24},{16,0},{24,8},{1,17},{9,25},{17,1},{25,9},{2,18},{10... | collective-permute-start | bytes 786440 | tf_op jit(solution)/shard_map/ppermute | solution.py:34
  34.4 2.0 %collective-permute-start.11 = (bf16[4,256,128]{2,1,0:T(8,128)(2,1)S(1)}, bf16[4,256,128]{2,1,0:T(8,128)(2,1)S(1)}, u32[]{:S(2)}, u32[]{:S(2)}) collective-permute-start(bf16[4,256,128]{2,1,0:T(8,128)(2,1)S(1)} %get-tuple-element.50), channel_id=1, source_target_pairs={{0,24},{8,0},{16,8},{24,16},{1,25},{9,1},{17,9},{25,17},{2,26},{10... | collective-permute-start | bytes 786440 | tf_op jit(solution)/shard_map/ppermute | solution.py:34
  36.4 0.0 collective-permute-done.refs_1_
  36.4 0.0 collective-permute-start.9
  36.4 3.6 %collective-permute-done.1.refs_2_ = bf16[4,256,128]{2,1,0:T(8,128)(2,1)S(1)} collective-permute-done((bf16[4,256,128]{2,1,0:T(8,128)(2,1)S(1)}, bf16[4,256,128]{2,1,0:T(8,128)(2,1)S(1)}, u32[]{:S(2)}, u32[]{:S(2)}) %collective-permute-start.1) | collective-permute-done | bytes 262176 | tf_op jit(solution)/shard_map/ppermute | solution.py:34
  40.0 0.5 collective-permute-done.2.refs_3_
  40.5 2.0 %delay_transform.4 = (bf16[4,256,128]{2,1,0:T(8,128)(2,1)S(1)}, bf16[4,256,128]{2,1,0:T(8,128)(2,1)S(1)}, bf16[4,256,128]{2,1,0:T(8,128)(2,1)S(1)}, bf16[4,256,128]{2,1,0:T(8,128)(2,1)S(1)}) custom-call(s32[1]{0:T(128)} %bitcast.me_ref, bf16[4,512,512]{2,1,0:T(8,128)(2,1)S(1)} %copy-done.1, bf16[4,256,128]{2,1,0:T(8,128)(2,1)S(1)} %copy-done.5, ...), custom_call_target="tpu_custom_call" | custom-call | flops 1000000000 | bytes 2097152 | tf_op jit(solution)/shard_map/delay_transform/pallas_call | solution.py:257
  42.5 7.0 %collective-permute-start.3 = (bf16[4,256,128]{2,1,0:T(8,128)(2,1)S(1)}, bf16[4,256,128]{2,1,0:T(8,128)(2,1)S(1)}, u32[]{:S(2)}, u32[]{:S(2)}) collective-permute-start(bf16[4,256,128]{2,1,0:T(8,128)(2,1)S(1)} %get-tuple-element.40), channel_id=1, source_target_pairs={{0,8},{8,16},{16,24},{24,0},{1,9},{9,17},{17,25},{25,1},{2,10},{10... | collective-permute-start | bytes 786440 | tf_op jit(solution)/shard_map/ppermute | solution.py:34
  49.5 0.5 collective-permute-start.4
  50.1 3.0 %collective-permute-start.5 = (bf16[4,256,128]{2,1,0:T(8,128)(2,1)S(1)}, bf16[4,256,128]{2,1,0:T(8,128)(2,1)S(1)}, u32[]{:S(2)}, u32[]{:S(2)}) collective-permute-start(bf16[4,256,128]{2,1,0:T(8,128)(2,1)S(1)} %get-tuple-element.42), channel_id=1, source_target_pairs={{0,24},{8,0},{16,8},{24,16},{1,25},{9,1},{17,9},{25,17},{2,26},{10... | collective-permute-start | bytes 786440 | tf_op jit(solution)/shard_map/ppermute | solution.py:34
  53.1 0.0 collective-permute-done.11.refs_7_
  53.1 4.2 %collective-permute-done.3.refs_1_ = bf16[4,256,128]{2,1,0:T(8,128)(2,1)S(1)} collective-permute-done((bf16[4,256,128]{2,1,0:T(8,128)(2,1)S(1)}, bf16[4,256,128]{2,1,0:T(8,128)(2,1)S(1)}, u32[]{:S(2)}, u32[]{:S(2)}) %collective-permute-start.3) | collective-permute-done | bytes 262176 | tf_op jit(solution)/shard_map/ppermute | solution.py:34
  57.3 5.1 %collective-permute-done.4.refs_2_ = bf16[4,256,128]{2,1,0:T(8,128)(2,1)S(1)} collective-permute-done((bf16[4,256,128]{2,1,0:T(8,128)(2,1)S(1)}, bf16[4,256,128]{2,1,0:T(8,128)(2,1)S(1)}, u32[]{:S(2)}, u32[]{:S(2)}) %collective-permute-start.4) | collective-permute-done | bytes 262176 | tf_op jit(solution)/shard_map/ppermute | solution.py:34
  62.4 0.2 collective-permute-done.5.refs_3_
  62.6 0.5 join_pieces.1
  63.1 1.3 %copy-done = bf16[8,1024,128]{2,1,0:T(8,128)(2,1)} copy-done((bf16[8,1024,128]{2,1,0:T(8,128)(2,1)}, bf16[8,1024,128]{2,1,0:T(8,128)(2,1)S(1)}, u32[]{:S(2)}) %copy-start) | copy-done | bytes 2097176
  64.4 4.9 %all-to-all-start.1 = ((bf16[8,1024,128]{2,1,0:T(8,128)(2,1)}), bf16[8,1024,128]{2,1,0:T(8,128)(2,1)}, u32[]{:S(2)}, u32[]{:S(2)}) async-start(bf16[8,1024,128]{2,1,0:T(8,128)(2,1)} %copy-done), calls=%async_computation.1 | async-start | bytes 4194304 | tf_op jit(solution)/shard_map/all_to_all | solution.py:519
  69.4 1.1 fusion.3
  70.5 1.6 %collective-permute-start.15 = (bf16[4,256,128]{2,1,0:T(8,128)(2,1)}, bf16[4,256,128]{2,1,0:T(8,128)(2,1)S(1)}, u32[]{:S(2)}, u32[]{:S(2)}) collective-permute-start(bf16[4,256,128]{2,1,0:T(8,128)(2,1)} %get-tuple-element.67), channel_id=1, source_target_pairs={{0,8},{8,16},{16,24},{24,0},{1,9},{9,17},{17,25},{25,1},{2,10},{10... | collective-permute-start | bytes 786440 | tf_op jit(solution)/shard_map/ppermute | solution.py:34
  72.1 0.5 collective-permute-start.16
  72.6 2.1 %collective-permute-start.17 = (bf16[4,256,128]{2,1,0:T(8,128)(2,1)}, bf16[4,256,128]{2,1,0:T(8,128)(2,1)S(1)}, u32[]{:S(2)}, u32[]{:S(2)}) collective-permute-start(bf16[4,256,128]{2,1,0:T(8,128)(2,1)} %get-tuple-element.65), channel_id=1, source_target_pairs={{0,24},{8,0},{16,8},{24,16},{1,25},{9,1},{17,9},{25,17},{2,26},{10... | collective-permute-start | bytes 786440 | tf_op jit(solution)/shard_map/ppermute | solution.py:34
  74.7 0.1 reshape.34
  74.8 1.0 pad_maximum_fusion
  75.8 0.1 collective-permute-start.12
  75.9 1.4 %collective-permute-start.13 = (bf16[4,272,128]{2,1,0:T(8,128)(2,1)S(1)}, bf16[4,272,128]{2,1,0:T(8,128)(2,1)S(1)}, u32[]{:S(2)}, u32[]{:S(2)}) collective-permute-start(bf16[4,272,128]{2,1,0:T(8,128)(2,1)S(1)} %get-tuple-element.76), channel_id=1, source_target_pairs={{0,16},{8,24},{16,0},{24,8},{1,17},{9,25},{17,1},{25,9},{2,18},{10... | collective-permute-start | bytes 835592 | tf_op jit(solution)/shard_map/ppermute | solution.py:34
  77.3 3.4 %collective-permute-done.15.refs_1_ = bf16[4,256,128]{2,1,0:T(8,128)(2,1)S(1)} collective-permute-done((bf16[4,256,128]{2,1,0:T(8,128)(2,1)}, bf16[4,256,128]{2,1,0:T(8,128)(2,1)S(1)}, u32[]{:S(2)}, u32[]{:S(2)}) %collective-permute-start.15) | collective-permute-done | bytes 262176 | tf_op jit(solution)/shard_map/ppermute | solution.py:34
  80.7 0.6 collective-permute-start.14
  81.3 5.0 %collective-permute-done.16.refs_2_ = bf16[4,256,128]{2,1,0:T(8,128)(2,1)S(1)} collective-permute-done((bf16[4,256,128]{2,1,0:T(8,128)(2,1)}, bf16[4,256,128]{2,1,0:T(8,128)(2,1)S(1)}, u32[]{:S(2)}, u32[]{:S(2)}) %collective-permute-start.16) | collective-permute-done | bytes 262176 | tf_op jit(solution)/shard_map/ppermute | solution.py:34
  86.4 1.6 %copy-done.2 = bf16[4,512,512]{2,1,0:T(8,128)(2,1)S(1)} copy-done((bf16[4,512,512]{2,1,0:T(8,128)(2,1)S(1)}, bf16[4,512,512]{2,1,0:T(8,128)(2,1)}, u32[]{:S(2)}) %copy-start.2) | copy-done | bytes 2097176
  88.0 2.1 %delay_transform.7 = (bf16[4,256,128]{2,1,0:T(8,128)(2,1)S(1)}, bf16[4,256,128]{2,1,0:T(8,128)(2,1)S(1)}, bf16[4,256,128]{2,1,0:T(8,128)(2,1)}, bf16[4,256,128]{2,1,0:T(8,128)(2,1)S(1)}) custom-call(s32[1]{0:T(128)} %bitcast.me_ref, bf16[4,512,512]{2,1,0:T(8,128)(2,1)S(1)} %copy-done.2, bf16[8,1040,128]{2,1,0:T(8,128)(2,1)S(1)} %all-to-all-done.refs_0_, ...), custom_call_target="tpu_custom_call" | custom-call | flops 1000000000 | bytes 2097152 | tf_op jit(solution)/shard_map/delay_transform/pallas_call | solution.py:257
  90.1 1.9 %collective-permute-start.19 = (bf16[4,256,128]{2,1,0:T(8,128)(2,1)S(1)}, bf16[4,256,128]{2,1,0:T(8,128)(2,1)S(1)}, u32[]{:S(2)}, u32[]{:S(2)}) collective-permute-start(bf16[4,256,128]{2,1,0:T(8,128)(2,1)S(1)} %get-tuple-element.58), channel_id=1, source_target_pairs={{0,8},{8,16},{16,24},{24,0},{1,9},{9,17},{17,25},{25,1},{2,10},{10... | collective-permute-start | bytes 786440 | tf_op jit(solution)/shard_map/ppermute | solution.py:34
  92.0 0.7 collective-permute-start.21
  92.7 1.7 %collective-permute-start.23 = (bf16[4,256,128]{2,1,0:T(8,128)(2,1)S(1)}, bf16[4,256,128]{2,1,0:T(8,128)(2,1)S(1)}, u32[]{:S(2)}, u32[]{:S(2)}) collective-permute-start(bf16[4,256,128]{2,1,0:T(8,128)(2,1)S(1)} %get-tuple-element.62), channel_id=1, source_target_pairs={{0,24},{8,0},{16,8},{24,16},{1,25},{9,1},{17,9},{25,17},{2,26},{10... | collective-permute-start | bytes 786440 | tf_op jit(solution)/shard_map/ppermute | solution.py:34
  94.4 3.9 %collective-permute-done.13.refs_2_ = bf16[4,272,128]{2,1,0:T(8,128)(2,1)S(1)} collective-permute-done((bf16[4,272,128]{2,1,0:T(8,128)(2,1)S(1)}, bf16[4,272,128]{2,1,0:T(8,128)(2,1)S(1)}, u32[]{:S(2)}, u32[]{:S(2)}) %collective-permute-start.13) | collective-permute-done | bytes 278560 | tf_op jit(solution)/shard_map/ppermute | solution.py:34
  98.3 2.0 %delay_transform.6 = (bf16[4,256,128]{2,1,0:T(8,128)(2,1)S(1)}, bf16[4,256,128]{2,1,0:T(8,128)(2,1)}, bf16[4,256,128]{2,1,0:T(8,128)(2,1)}, bf16[4,256,128]{2,1,0:T(8,128)(2,1)}) custom-call(s32[1]{0:T(128)} %bitcast.me_ref, bf16[4,512,512]{2,1,0:T(8,128)(2,1)S(1)} %copy-done.2, bf16[8,1040,128]{2,1,0:T(8,128)(2,1)S(1)} %all-to-all-done.refs_0_, ...), custom_call_target="tpu_custom_call" | custom-call | flops 1000000000 | bytes 2097152 | tf_op jit(solution)/shard_map/delay_transform/pallas_call | solution.py:257
  100.3 0.7 copy-done.3
  101.0 1.9 %collective-permute-start.18 = (bf16[4,256,128]{2,1,0:T(8,128)(2,1)}, bf16[4,256,128]{2,1,0:T(8,128)(2,1)S(1)}, u32[]{:S(2)}, u32[]{:S(2)}) collective-permute-start(bf16[4,256,128]{2,1,0:T(8,128)(2,1)} %get-tuple-element.57), channel_id=1, source_target_pairs={{0,8},{8,16},{16,24},{24,0},{1,9},{9,17},{17,25},{25,1},{2,10},{10... | collective-permute-start | bytes 786440 | tf_op jit(solution)/shard_map/ppermute | solution.py:34
  102.9 0.3 collective-permute-start.20
  103.3 0.7 collective-permute-done.19.refs_3_
  104.0 1.3 %collective-permute-start.22 = (bf16[4,256,128]{2,1,0:T(8,128)(2,1)}, bf16[4,256,128]{2,1,0:T(8,128)(2,1)S(1)}, u32[]{:S(2)}, u32[]{:S(2)}) collective-permute-start(bf16[4,256,128]{2,1,0:T(8,128)(2,1)} %get-tuple-element.61), channel_id=1, source_target_pairs={{0,24},{8,0},{16,8},{24,16},{1,25},{9,1},{17,9},{25,17},{2,26},{10... | collective-permute-start | bytes 786440 | tf_op jit(solution)/shard_map/ppermute | solution.py:34
  105.3 1.9 %pair_weights.1 = (bf16[512,512]{1,0:T(8,128)(2,1)S(1)}, f32[64,512]{1,0:T(8,128)S(1)}) custom-call(s32[1]{0:T(128)} %bitcast.me_ref, bf16[4,16,128]{2,1,0:T(8,128)(2,1)S(1)} %bitcast.13, bf16[4,272,128]{2,1,0:T(8,128)(2,1)S(1)} %collective-permute-done.12.refs_1_, bf16[4,272,128]{2,1,0:T(8,128)(2,1)S(1)} %collective-permute-done.13.refs_2_, ...), custom_call_target="tpu_custom_call" | custom-call | flops 536870912 | bytes 1048576 | tf_op jit(solution)/shard_map/pair_weights/pallas_call | solution.py:376
  107.2 11.2 %all-to-all-done.1.refs_0_ = bf16[8,1024,128]{2,1,0:T(8,128)(2,1)} async-done(((bf16[8,1024,128]{2,1,0:T(8,128)(2,1)}), bf16[8,1024,128]{2,1,0:T(8,128)(2,1)}, u32[]{:S(2)}, u32[]{:S(2)}) %all-to-all-start.1) | async-done | bytes 2097184 | tf_op jit(solution)/shard_map/all_to_all | solution.py:519
  118.5 3.1 %pair_sums.2.before_ref = f32[64,256]{1,0:T(8,128)S(1)} custom-call(bf16[512,512]{1,0:T(8,128)(2,1)S(1)} %get-tuple-element.52.mix_ref, f32[64,512]{1,0:T(8,128)S(1)} %get-tuple-element.53.group_ref, f32[64,256]{1,0:T(8,128)S(1)} %broadcast_in_dim.3.before_ref, bf16[8,1024,128]{2,1,0:T(8,128)(2,1)} %all-to-all-done.1.refs_0_), custom_call_target="tpu_custom_call" | custom-call | flops 1073741824 | bytes 2097152 | tf_op jit(solution)/shard_map/pair_sums/pallas_call | solution.py:450
  121.7 1.5 %pair_sums.3 = f32[64,256]{1,0:T(8,128)S(1)} custom-call(bf16[512,512]{1,0:T(8,128)(2,1)S(1)} %get-tuple-element.52.mix_ref, f32[64,512]{1,0:T(8,128)S(1)} %get-tuple-element.53.group_ref, f32[64,256]{1,0:T(8,128)S(1)} %pair_sums.2.before_ref, bf16[4,256,128]{2,1,0:T(8,128)(2,1)S(1)} %copy-done.4, bf16[4,256,128]{2,1,0:T(8,128)(2,1)S(1)} %get-tuple-element.56.refs_1_, ...), custom_call_target="tpu_custom_call" | custom-call | flops 1073741824 | bytes 2097152 | tf_op jit(solution)/shard_map/pair_sums/pallas_call | solution.py:450
  123.2 1.7 %collective-permute-start.24 = (f32[16,256]{1,0:T(8,128)S(1)}, f32[16,256]{1,0:T(8,128)S(1)}, u32[]{:S(2)}, u32[]{:S(2)}) collective-permute-start(f32[16,256]{1,0:T(8,128)S(1)} %get-tuple-element.73), channel_id=1, source_target_pairs={{0,8},{8,16},{16,24},{24,0},{1,9},{9,17},{17,25},{25,1},{2,10},{10... | collective-permute-start | bytes 49160 | tf_op jit(solution)/shard_map/ppermute | solution.py:34
  124.9 0.5 collective-permute-start.25
  125.4 2.1 %collective-permute-start.26 = (f32[16,256]{1,0:T(8,128)S(1)}, f32[16,256]{1,0:T(8,128)S(1)}, u32[]{:S(2)}, u32[]{:S(2)}) collective-permute-start(f32[16,256]{1,0:T(8,128)S(1)} %get-tuple-element.71), channel_id=1, source_target_pairs={{0,24},{8,0},{16,8},{24,16},{1,25},{9,1},{17,9},{25,17},{2,26},{10... | collective-permute-start | bytes 49160 | tf_op jit(solution)/shard_map/ppermute | solution.py:34
  127.5 0.4 collective-permute-done.24.refs_1_
  127.9 0.7 collective-permute-done.25.refs_2_
  128.6 0.5 collective-permute-done.26.refs_3_
  129.1 1.1 interleave_delays.1
  (40 shorter events, 0.1 us)
Async XLA Ops:
  6.8 11.0 %copy-start.10 = (bf16[4,256,128]{2,1,0:T(8,128)(2,1)S(1)}, bf16[4,256,128]{2,1,0:T(8,128)(2,1)}, u32[]{:S(2)}) copy-start(bf16[4,256,128]{2,1,0:T(8,128)(2,1)} %get-tuple-element.36) | copy-start | bytes 786436
  6.8 11.6 %copy-start.9 = (bf16[4,256,128]{2,1,0:T(8,128)(2,1)S(1)}, bf16[4,256,128]{2,1,0:T(8,128)(2,1)}, u32[]{:S(2)}) copy-start(bf16[4,256,128]{2,1,0:T(8,128)(2,1)} %get-tuple-element.37) | copy-start | bytes 786436
  6.8 16.8 %copy-start.8 = (bf16[4,256,128]{2,1,0:T(8,128)(2,1)S(1)}, bf16[4,256,128]{2,1,0:T(8,128)(2,1)}, u32[]{:S(2)}) copy-start(bf16[4,256,128]{2,1,0:T(8,128)(2,1)} %get-tuple-element.38) | copy-start | bytes 786436
  6.8 22.4 %copy-start.6 = (bf16[4,256,128]{2,1,0:T(8,128)(2,1)S(1)}, bf16[4,256,128]{2,1,0:T(8,128)(2,1)}, u32[]{:S(2)}) copy-start(bf16[4,256,128]{2,1,0:T(8,128)(2,1)} %get-tuple-element.43.refs_0_) | copy-start | bytes 786436
  6.8 33.7 %copy-start.5 = (bf16[4,256,128]{2,1,0:T(8,128)(2,1)S(1)}, bf16[4,256,128]{2,1,0:T(8,128)(2,1)}, u32[]{:S(2)}) copy-start(bf16[4,256,128]{2,1,0:T(8,128)(2,1)} %get-tuple-element.35.refs_0_) | copy-start | bytes 786436
  6.8 57.6 %all-to-all-start = ((bf16[8,1040,128]{2,1,0:T(8,128)(2,1)}), bf16[8,1040,128]{2,1,0:T(8,128)(2,1)S(1)}, u32[]{:S(2)}, u32[]{:S(2)}) async-start(bf16[8,1040,128]{2,1,0:T(8,128)(2,1)} %get-tuple-element.34), calls=%async_computation | async-start | bytes 4259840 | tf_op jit(solution)/shard_map/all_to_all | solution.py:513
  13.3 10.3 %collective-permute-start.6 = (bf16[4,256,128]{2,1,0:T(8,128)(2,1)}, bf16[4,256,128]{2,1,0:T(8,128)(2,1)S(1)}, u32[]{:S(2)}, u32[]{:S(2)}) collective-permute-start(bf16[4,256,128]{2,1,0:T(8,128)(2,1)} %get-tuple-element.44), channel_id=1, source_target_pairs={{0,8},{8,16},{16,24},{24,0},{1,9},{9,17},{17,25},{25,1},{2,10},{10... | collective-permute-start | bytes 786440 | tf_op jit(solution)/shard_map/ppermute | solution.py:34
  14.8 14.4 %collective-permute-start.7 = (bf16[4,256,128]{2,1,0:T(8,128)(2,1)}, bf16[4,256,128]{2,1,0:T(8,128)(2,1)S(1)}, u32[]{:S(2)}, u32[]{:S(2)}) collective-permute-start(bf16[4,256,128]{2,1,0:T(8,128)(2,1)} %get-tuple-element.45), channel_id=1, source_target_pairs={{0,16},{8,24},{16,0},{24,8},{1,17},{9,25},{17,1},{25,9},{2,18},{10... | collective-permute-start | bytes 786440 | tf_op jit(solution)/shard_map/ppermute | solution.py:34
  16.3 12.9 %collective-permute-start.8 = (bf16[4,256,128]{2,1,0:T(8,128)(2,1)}, bf16[4,256,128]{2,1,0:T(8,128)(2,1)S(1)}, u32[]{:S(2)}, u32[]{:S(2)}) collective-permute-start(bf16[4,256,128]{2,1,0:T(8,128)(2,1)} %get-tuple-element.46), channel_id=1, source_target_pairs={{0,24},{8,0},{16,8},{24,16},{1,25},{9,1},{17,9},{25,17},{2,26},{10... | collective-permute-start | bytes 786440 | tf_op jit(solution)/shard_map/ppermute | solution.py:34
  17.7 18.7 %collective-permute-start = (bf16[4,256,128]{2,1,0:T(8,128)(2,1)S(1)}, bf16[4,256,128]{2,1,0:T(8,128)(2,1)S(1)}, u32[]{:S(2)}, u32[]{:S(2)}) collective-permute-start(bf16[4,256,128]{2,1,0:T(8,128)(2,1)S(1)} %copy-done.10), channel_id=1, source_target_pairs={{0,8},{8,16},{16,24},{24,0},{1,9},{9,17},{17,25},{25,1},{2,10},{10... | collective-permute-start | bytes 786440 | tf_op jit(solution)/shard_map/ppermute | solution.py:34
  18.3 21.7 %collective-permute-start.1 = (bf16[4,256,128]{2,1,0:T(8,128)(2,1)S(1)}, bf16[4,256,128]{2,1,0:T(8,128)(2,1)S(1)}, u32[]{:S(2)}, u32[]{:S(2)}) collective-permute-start(bf16[4,256,128]{2,1,0:T(8,128)(2,1)S(1)} %copy-done.9), channel_id=1, source_target_pairs={{0,16},{8,24},{16,0},{24,8},{1,17},{9,25},{17,1},{25,9},{2,18},{10... | collective-permute-start | bytes 786440 | tf_op jit(solution)/shard_map/ppermute | solution.py:34
  23.5 16.9 %collective-permute-start.2 = (bf16[4,256,128]{2,1,0:T(8,128)(2,1)S(1)}, bf16[4,256,128]{2,1,0:T(8,128)(2,1)S(1)}, u32[]{:S(2)}, u32[]{:S(2)}) collective-permute-start(bf16[4,256,128]{2,1,0:T(8,128)(2,1)S(1)} %copy-done.8), channel_id=1, source_target_pairs={{0,24},{8,0},{16,8},{24,16},{1,25},{9,1},{17,9},{25,17},{2,26},{10... | collective-permute-start | bytes 786440 | tf_op jit(solution)/shard_map/ppermute | solution.py:34
  29.2 1.6 %copy-start.1 = (bf16[4,512,512]{2,1,0:T(8,128)(2,1)S(1)}, bf16[4,512,512]{2,1,0:T(8,128)(2,1)}, u32[]{:S(2)}) copy-start(bf16[4,512,512]{2,1,0:T(8,128)(2,1)} %constant.14.clone.matrix_hbm) | copy-start | bytes 6291460
  32.8 17.2 %collective-permute-start.10 = (bf16[4,256,128]{2,1,0:T(8,128)(2,1)S(1)}, bf16[4,256,128]{2,1,0:T(8,128)(2,1)S(1)}, u32[]{:S(2)}, u32[]{:S(2)}) collective-permute-start(bf16[4,256,128]{2,1,0:T(8,128)(2,1)S(1)} %get-tuple-element.49), channel_id=1, source_target_pairs={{0,16},{8,24},{16,0},{24,8},{1,17},{9,25},{17,1},{25,9},{2,18},{10... | collective-permute-start | bytes 786440 | tf_op jit(solution)/shard_map/ppermute | solution.py:34
  34.4 18.7 %collective-permute-start.11 = (bf16[4,256,128]{2,1,0:T(8,128)(2,1)S(1)}, bf16[4,256,128]{2,1,0:T(8,128)(2,1)S(1)}, u32[]{:S(2)}, u32[]{:S(2)}) collective-permute-start(bf16[4,256,128]{2,1,0:T(8,128)(2,1)S(1)} %get-tuple-element.50), channel_id=1, source_target_pairs={{0,24},{8,0},{16,8},{24,16},{1,25},{9,1},{17,9},{25,17},{2,26},{10... | collective-permute-start | bytes 786440 | tf_op jit(solution)/shard_map/ppermute | solution.py:34
  36.4 16.7 %collective-permute-start.9 = (bf16[4,256,128]{2,1,0:T(8,128)(2,1)S(1)}, bf16[4,256,128]{2,1,0:T(8,128)(2,1)S(1)}, u32[]{:S(2)}, u32[]{:S(2)}) collective-permute-start(bf16[4,256,128]{2,1,0:T(8,128)(2,1)S(1)} %get-tuple-element.48), channel_id=1, source_target_pairs={{0,8},{8,16},{16,24},{24,0},{1,9},{9,17},{17,25},{25,1},{2,10},{10... | collective-permute-start | bytes 786440 | tf_op jit(solution)/shard_map/ppermute | solution.py:34
  42.5 14.8 %collective-permute-start.3 = (bf16[4,256,128]{2,1,0:T(8,128)(2,1)S(1)}, bf16[4,256,128]{2,1,0:T(8,128)(2,1)S(1)}, u32[]{:S(2)}, u32[]{:S(2)}) collective-permute-start(bf16[4,256,128]{2,1,0:T(8,128)(2,1)S(1)} %get-tuple-element.40), channel_id=1, source_target_pairs={{0,8},{8,16},{16,24},{24,0},{1,9},{9,17},{17,25},{25,1},{2,10},{10... | collective-permute-start | bytes 786440 | tf_op jit(solution)/shard_map/ppermute | solution.py:34
  49.5 12.9 %collective-permute-start.4 = (bf16[4,256,128]{2,1,0:T(8,128)(2,1)S(1)}, bf16[4,256,128]{2,1,0:T(8,128)(2,1)S(1)}, u32[]{:S(2)}, u32[]{:S(2)}) collective-permute-start(bf16[4,256,128]{2,1,0:T(8,128)(2,1)S(1)} %get-tuple-element.41), channel_id=1, source_target_pairs={{0,16},{8,24},{16,0},{24,8},{1,17},{9,25},{17,1},{25,9},{2,18},{10... | collective-permute-start | bytes 786440 | tf_op jit(solution)/shard_map/ppermute | solution.py:34
  50.1 12.5 %collective-permute-start.5 = (bf16[4,256,128]{2,1,0:T(8,128)(2,1)S(1)}, bf16[4,256,128]{2,1,0:T(8,128)(2,1)S(1)}, u32[]{:S(2)}, u32[]{:S(2)}) collective-permute-start(bf16[4,256,128]{2,1,0:T(8,128)(2,1)S(1)} %get-tuple-element.42), channel_id=1, source_target_pairs={{0,24},{8,0},{16,8},{24,16},{1,25},{9,1},{17,9},{25,17},{2,26},{10... | collective-permute-start | bytes 786440 | tf_op jit(solution)/shard_map/ppermute | solution.py:34
  63.1 1.3 %copy-start = (bf16[8,1024,128]{2,1,0:T(8,128)(2,1)}, bf16[8,1024,128]{2,1,0:T(8,128)(2,1)S(1)}, u32[]{:S(2)}) copy-start(bf16[8,1024,128]{2,1,0:T(8,128)(2,1)S(1)} %join_pieces.1) | copy-start | bytes 6291460
  64.4 4.9 %copy-start.7 = (s32[256,2]{0,1:T(2,128)S(1)}, s32[256,2]{0,1:T(2,128)}, u32[]{:S(2)}) copy-start(s32[256,2]{0,1:T(2,128)} %param.11) | copy-start | bytes 6148
  64.4 4.9 %copy-start.11 = (s32[128]{0:T(128)S(1)}, s32[128]{0:T(128)}, u32[]{:S(2)}) copy-start(s32[128]{0:T(128)} %param.10) | copy-start | bytes 1540
  64.4 54.0 %all-to-all-start.1 = ((bf16[8,1024,128]{2,1,0:T(8,128)(2,1)}), bf16[8,1024,128]{2,1,0:T(8,128)(2,1)}, u32[]{:S(2)}, u32[]{:S(2)}) async-start(bf16[8,1024,128]{2,1,0:T(8,128)(2,1)} %copy-done), calls=%async_computation.1 | async-start | bytes 4194304 | tf_op jit(solution)/shard_map/all_to_all | solution.py:519
  70.5 10.3 %collective-permute-start.15 = (bf16[4,256,128]{2,1,0:T(8,128)(2,1)}, bf16[4,256,128]{2,1,0:T(8,128)(2,1)S(1)}, u32[]{:S(2)}, u32[]{:S(2)}) collective-permute-start(bf16[4,256,128]{2,1,0:T(8,128)(2,1)} %get-tuple-element.67), channel_id=1, source_target_pairs={{0,8},{8,16},{16,24},{24,0},{1,9},{9,17},{17,25},{25,1},{2,10},{10... | collective-permute-start | bytes 786440 | tf_op jit(solution)/shard_map/ppermute | solution.py:34
  72.1 14.3 %collective-permute-start.16 = (bf16[4,256,128]{2,1,0:T(8,128)(2,1)}, bf16[4,256,128]{2,1,0:T(8,128)(2,1)S(1)}, u32[]{:S(2)}, u32[]{:S(2)}) collective-permute-start(bf16[4,256,128]{2,1,0:T(8,128)(2,1)} %get-tuple-element.66), channel_id=1, source_target_pairs={{0,16},{8,24},{16,0},{24,8},{1,17},{9,25},{17,1},{25,9},{2,18},{10... | collective-permute-start | bytes 786440 | tf_op jit(solution)/shard_map/ppermute | solution.py:34
  72.6 13.8 %collective-permute-start.17 = (bf16[4,256,128]{2,1,0:T(8,128)(2,1)}, bf16[4,256,128]{2,1,0:T(8,128)(2,1)S(1)}, u32[]{:S(2)}, u32[]{:S(2)}) collective-permute-start(bf16[4,256,128]{2,1,0:T(8,128)(2,1)} %get-tuple-element.65), channel_id=1, source_target_pairs={{0,24},{8,0},{16,8},{24,16},{1,25},{9,1},{17,9},{25,17},{2,26},{10... | collective-permute-start | bytes 786440 | tf_op jit(solution)/shard_map/ppermute | solution.py:34
  75.8 16.8 %collective-permute-start.12 = (bf16[4,272,128]{2,1,0:T(8,128)(2,1)S(1)}, bf16[4,272,128]{2,1,0:T(8,128)(2,1)S(1)}, u32[]{:S(2)}, u32[]{:S(2)}) collective-permute-start(bf16[4,272,128]{2,1,0:T(8,128)(2,1)S(1)} %get-tuple-element.77), channel_id=1, source_target_pairs={{0,8},{8,16},{16,24},{24,0},{1,9},{9,17},{17,25},{25,1},{2,10},{10... | collective-permute-start | bytes 835592 | tf_op jit(solution)/shard_map/ppermute | solution.py:34
  75.9 22.4 %collective-permute-start.13 = (bf16[4,272,128]{2,1,0:T(8,128)(2,1)S(1)}, bf16[4,272,128]{2,1,0:T(8,128)(2,1)S(1)}, u32[]{:S(2)}, u32[]{:S(2)}) collective-permute-start(bf16[4,272,128]{2,1,0:T(8,128)(2,1)S(1)} %get-tuple-element.76), channel_id=1, source_target_pairs={{0,16},{8,24},{16,0},{24,8},{1,17},{9,25},{17,1},{25,9},{2,18},{10... | collective-permute-start | bytes 835592 | tf_op jit(solution)/shard_map/ppermute | solution.py:34
  80.7 17.6 %collective-permute-start.14 = (bf16[4,272,128]{2,1,0:T(8,128)(2,1)S(1)}, bf16[4,272,128]{2,1,0:T(8,128)(2,1)S(1)}, u32[]{:S(2)}, u32[]{:S(2)}) collective-permute-start(bf16[4,272,128]{2,1,0:T(8,128)(2,1)S(1)} %get-tuple-element.75), channel_id=1, source_target_pairs={{0,24},{8,0},{16,8},{24,16},{1,25},{9,1},{17,9},{25,17},{2,26},{10... | collective-permute-start | bytes 835592 | tf_op jit(solution)/shard_map/ppermute | solution.py:34
  86.4 1.6 %copy-start.2 = (bf16[4,512,512]{2,1,0:T(8,128)(2,1)S(1)}, bf16[4,512,512]{2,1,0:T(8,128)(2,1)}, u32[]{:S(2)}) copy-start(bf16[4,512,512]{2,1,0:T(8,128)(2,1)} %constant.14.clone.matrix_hbm) | copy-start | bytes 6291460
  90.1 13.9 %collective-permute-start.19 = (bf16[4,256,128]{2,1,0:T(8,128)(2,1)S(1)}, bf16[4,256,128]{2,1,0:T(8,128)(2,1)S(1)}, u32[]{:S(2)}, u32[]{:S(2)}) collective-permute-start(bf16[4,256,128]{2,1,0:T(8,128)(2,1)S(1)} %get-tuple-element.58), channel_id=1, source_target_pairs={{0,8},{8,16},{16,24},{24,0},{1,9},{9,17},{17,25},{25,1},{2,10},{10... | collective-permute-start | bytes 786440 | tf_op jit(solution)/shard_map/ppermute | solution.py:34
  92.0 29.6 %collective-permute-start.21 = (bf16[4,256,128]{2,1,0:T(8,128)(2,1)}, bf16[4,256,128]{2,1,0:T(8,128)(2,1)S(1)}, u32[]{:S(2)}, u32[]{:S(2)}) collective-permute-start(bf16[4,256,128]{2,1,0:T(8,128)(2,1)} %get-tuple-element.60), channel_id=1, source_target_pairs={{0,16},{8,24},{16,0},{24,8},{1,17},{9,25},{17,1},{25,9},{2,18},{10... | collective-permute-start | bytes 786440 | tf_op jit(solution)/shard_map/ppermute | solution.py:34
  92.7 28.9 %collective-permute-start.23 = (bf16[4,256,128]{2,1,0:T(8,128)(2,1)S(1)}, bf16[4,256,128]{2,1,0:T(8,128)(2,1)S(1)}, u32[]{:S(2)}, u32[]{:S(2)}) collective-permute-start(bf16[4,256,128]{2,1,0:T(8,128)(2,1)S(1)} %get-tuple-element.62), channel_id=1, source_target_pairs={{0,24},{8,0},{16,8},{24,16},{1,25},{9,1},{17,9},{25,17},{2,26},{10... | collective-permute-start | bytes 786440 | tf_op jit(solution)/shard_map/ppermute | solution.py:34
  100.3 0.7 copy-start.3
  101.0 20.6 %collective-permute-start.18 = (bf16[4,256,128]{2,1,0:T(8,128)(2,1)}, bf16[4,256,128]{2,1,0:T(8,128)(2,1)S(1)}, u32[]{:S(2)}, u32[]{:S(2)}) collective-permute-start(bf16[4,256,128]{2,1,0:T(8,128)(2,1)} %get-tuple-element.57), channel_id=1, source_target_pairs={{0,8},{8,16},{16,24},{24,0},{1,9},{9,17},{17,25},{25,1},{2,10},{10... | collective-permute-start | bytes 786440 | tf_op jit(solution)/shard_map/ppermute | solution.py:34
  102.9 18.7 %collective-permute-start.20 = (bf16[4,256,128]{2,1,0:T(8,128)(2,1)}, bf16[4,256,128]{2,1,0:T(8,128)(2,1)S(1)}, u32[]{:S(2)}, u32[]{:S(2)}) collective-permute-start(bf16[4,256,128]{2,1,0:T(8,128)(2,1)} %get-tuple-element.59), channel_id=1, source_target_pairs={{0,16},{8,24},{16,0},{24,8},{1,17},{9,25},{17,1},{25,9},{2,18},{10... | collective-permute-start | bytes 786440 | tf_op jit(solution)/shard_map/ppermute | solution.py:34
  104.0 17.7 %collective-permute-start.22 = (bf16[4,256,128]{2,1,0:T(8,128)(2,1)}, bf16[4,256,128]{2,1,0:T(8,128)(2,1)S(1)}, u32[]{:S(2)}, u32[]{:S(2)}) collective-permute-start(bf16[4,256,128]{2,1,0:T(8,128)(2,1)} %get-tuple-element.61), channel_id=1, source_target_pairs={{0,24},{8,0},{16,8},{24,16},{1,25},{9,1},{17,9},{25,17},{2,26},{10... | collective-permute-start | bytes 786440 | tf_op jit(solution)/shard_map/ppermute | solution.py:34
  107.2 14.4 %copy-start.4 = (bf16[4,256,128]{2,1,0:T(8,128)(2,1)S(1)}, bf16[4,256,128]{2,1,0:T(8,128)(2,1)}, u32[]{:S(2)}) copy-start(bf16[4,256,128]{2,1,0:T(8,128)(2,1)} %copy-done.3) | copy-start | bytes 786436
  123.2 4.7 %collective-permute-start.24 = (f32[16,256]{1,0:T(8,128)S(1)}, f32[16,256]{1,0:T(8,128)S(1)}, u32[]{:S(2)}, u32[]{:S(2)}) collective-permute-start(f32[16,256]{1,0:T(8,128)S(1)} %get-tuple-element.73), channel_id=1, source_target_pairs={{0,8},{8,16},{16,24},{24,0},{1,9},{9,17},{17,25},{25,1},{2,10},{10... | collective-permute-start | bytes 49160 | tf_op jit(solution)/shard_map/ppermute | solution.py:34
  124.9 3.7 %collective-permute-start.25 = (f32[16,256]{1,0:T(8,128)S(1)}, f32[16,256]{1,0:T(8,128)S(1)}, u32[]{:S(2)}, u32[]{:S(2)}) collective-permute-start(f32[16,256]{1,0:T(8,128)S(1)} %get-tuple-element.72), channel_id=1, source_target_pairs={{0,16},{8,24},{16,0},{24,8},{1,17},{9,25},{17,1},{25,9},{2,18},{10... | collective-permute-start | bytes 49160 | tf_op jit(solution)/shard_map/ppermute | solution.py:34
  125.4 3.7 %collective-permute-start.26 = (f32[16,256]{1,0:T(8,128)S(1)}, f32[16,256]{1,0:T(8,128)S(1)}, u32[]{:S(2)}, u32[]{:S(2)}) collective-permute-start(f32[16,256]{1,0:T(8,128)S(1)} %get-tuple-element.71), channel_id=1, source_target_pairs={{0,24},{8,0},{16,8},{24,16},{1,25},{9,1},{17,9},{25,17},{2,26},{10... | collective-permute-start | bytes 49160 | tf_op jit(solution)/shard_map/ppermute | solution.py:34

commit v4 on v3

--- a/solution.py
+++ b/solution.py
@@ -120,10 +120,11 @@
             ]
             moved = jnp.dot(pick, jnp.concatenate(source, axis=1), preferred_element_type=F32)
             tapered = (moved * weight).astype(BF16)
+            squares = 0.0
             for c in range(tiles):
                 tile = tapered[:, c * LANES : (c + 1) * LANES]
                 wide = tile.astype(F32)
-                total = total + wide * wide
+                squares = squares + wide * wide
                 tile = tile.reshape(blocks, column, LANES)
                 if half:
                     tile = tile.reshape(halves, blocks // halves, column, LANES)
@@ -131,6 +132,7 @@
                 else:
                     start = (s * tiles + c) * column
                     early_buf[:, start : start + column] = tile
+            total = total + squares
             if half:
                 new = [
                     pltpu.make_async_copy(

time: 131 us -> 131 us (level)
  no operation moved by 1% of the time
where the time goes in v4:
time: 131 us; the launch traced here: 130 us
  starting transfers between devices  51 us (39%)
  waiting for transfers between devices  48.4 us (37%)
  Pallas kernels  23.1 us (18%)
  local copies, waits for them, and re-layouts  6.48 us (5%)
    ppermute x27, starting transfers between devices, shifted(): return lax.ppermute(value, axis, pairs)  39.7 us
    ppermute x27, waiting for transfers between devices, shifted(): return lax.ppermute(value, axis, pairs)  37.1 us
    all_to_all x1, waiting for transfers between devices, on_device(): late = lax.all_to_all(late, 'bl', split_axis=0, concat_axis=0, tiled=True)  11.2 us
    pallas_call x4, Pallas kernels, delay_transform(): pl.pallas_call(functools.partial(delay_kernel, half), out_shape=[jax.Shap...  8.17 us
    pallas_call x1, Pallas kernels, taper(): pl.pallas_call(functools.partial(taper_kernel, times, parts, band_count),...  6.77 us
    all_to_all x1, starting transfers between devices, on_device(): early = lax.all_to_all(early, 'bl', split_axis=0, concat_axis=0, tiled=True)  6.47 us
    unnamed x24, local copies, waits for them, and re-layouts  5.26 us
    all_to_all x1, starting transfers between devices, on_device(): late = lax.all_to_all(late, 'bl', split_axis=0, concat_axis=0, tiled=True)  4.87 us
  transfers between devices with their start and end apart: 29, of which 15 were waited for; matrix products, arithmetic and copies ran while one was open for 2% of the time, Pallas kernels for 10%

profile of v4, /device:TPU:0, one launch (start us, length us, event | category | flops | bytes accessed | tf_op | source)
XLA Modules:
  0.0 130.3 jit_solution(3315107873699498241)
XLA Ops:
  0.0 6.8 %taper_rows.1 = (bf16[8,1040,128]{2,1,0:T(8,128)(2,1)}, bf16[4,256,128]{2,1,0:T(8,128)(2,1)}, bf16[4,256,128]{2,1,0:T(8,128)(2,1)}, bf16[4,256,128]{2,1,0:T(8,12...) custom-call(s32[1]{0:T(128)} %bitcast.me_ref, ...), custom_call_target="tpu_custom_call" | custom-call | flops 2147483648 | bytes 8388608 | tf_op jit(solution)/shard_map/taper_rows/pallas_call | solution.py:188
  6.8 6.5 %all-to-all-start = ((bf16[8,1040,128]{2,1,0:T(8,128)(2,1)}), bf16[8,1040,128]{2,1,0:T(8,128)(2,1)S(1)}, u32[]{:S(2)}, u32[]{:S(2)}) async-start(bf16[8,1040,128]{2,1,0:T(8,128)(2,1)} %get-tuple-element.34), calls=%async_computation | async-start | bytes 4259840 | tf_op jit(solution)/shard_map/all_to_all | solution.py:515
  13.3 1.5 %collective-permute-start.6 = (bf16[4,256,128]{2,1,0:T(8,128)(2,1)}, bf16[4,256,128]{2,1,0:T(8,128)(2,1)S(1)}, u32[]{:S(2)}, u32[]{:S(2)}) collective-permute-start(bf16[4,256,128]{2,1,0:T(8,128)(2,1)} %get-tuple-element.44), channel_id=1, source_target_pairs={{0,8},{8,16},{16,24},{24,0},{1,9},{9,17},{17,25},{25,1},{2,10},{10... | collective-permute-start | bytes 786440 | tf_op jit(solution)/shard_map/ppermute | solution.py:34
  14.8 1.5 %collective-permute-start.7 = (bf16[4,256,128]{2,1,0:T(8,128)(2,1)}, bf16[4,256,128]{2,1,0:T(8,128)(2,1)S(1)}, u32[]{:S(2)}, u32[]{:S(2)}) collective-permute-start(bf16[4,256,128]{2,1,0:T(8,128)(2,1)} %get-tuple-element.45), channel_id=1, source_target_pairs={{0,16},{8,24},{16,0},{24,8},{1,17},{9,25},{17,1},{25,9},{2,18},{10... | collective-permute-start | bytes 786440 | tf_op jit(solution)/shard_map/ppermute | solution.py:34
  16.3 1.4 %collective-permute-start.8 = (bf16[4,256,128]{2,1,0:T(8,128)(2,1)}, bf16[4,256,128]{2,1,0:T(8,128)(2,1)S(1)}, u32[]{:S(2)}, u32[]{:S(2)}) collective-permute-start(bf16[4,256,128]{2,1,0:T(8,128)(2,1)} %get-tuple-element.46), channel_id=1, source_target_pairs={{0,24},{8,0},{16,8},{24,16},{1,25},{9,1},{17,9},{25,17},{2,26},{10... | collective-permute-start | bytes 786440 | tf_op jit(solution)/shard_map/ppermute | solution.py:34
  17.8 0.6 collective-permute-start
  18.4 0.5 collective-permute-start.1
  18.8 4.7 %collective-permute-done.6.refs_1_ = bf16[4,256,128]{2,1,0:T(8,128)(2,1)S(1)} collective-permute-done((bf16[4,256,128]{2,1,0:T(8,128)(2,1)}, bf16[4,256,128]{2,1,0:T(8,128)(2,1)S(1)}, u32[]{:S(2)}, u32[]{:S(2)}) %collective-permute-start.6) | collective-permute-done | bytes 262176 | tf_op jit(solution)/shard_map/ppermute | solution.py:34
  23.6 1.5 %collective-permute-start.2 = (bf16[4,256,128]{2,1,0:T(8,128)(2,1)S(1)}, bf16[4,256,128]{2,1,0:T(8,128)(2,1)S(1)}, u32[]{:S(2)}, u32[]{:S(2)}) collective-permute-start(bf16[4,256,128]{2,1,0:T(8,128)(2,1)S(1)} %copy-done.8), channel_id=1, source_target_pairs={{0,24},{8,0},{16,8},{24,16},{1,25},{9,1},{17,9},{25,17},{2,26},{10... | collective-permute-start | bytes 786440 | tf_op jit(solution)/shard_map/ppermute | solution.py:34
  25.1 4.1 %collective-permute-done.7.refs_2_ = bf16[4,256,128]{2,1,0:T(8,128)(2,1)S(1)} collective-permute-done((bf16[4,256,128]{2,1,0:T(8,128)(2,1)}, bf16[4,256,128]{2,1,0:T(8,128)(2,1)S(1)}, u32[]{:S(2)}, u32[]{:S(2)}) %collective-permute-start.7) | collective-permute-done | bytes 262176 | tf_op jit(solution)/shard_map/ppermute | solution.py:34
  29.2 0.0 collective-permute-done.8.refs_3_
  29.2 1.6 %copy-done.1 = bf16[4,512,512]{2,1,0:T(8,128)(2,1)S(1)} copy-done((bf16[4,512,512]{2,1,0:T(8,128)(2,1)S(1)}, bf16[4,512,512]{2,1,0:T(8,128)(2,1)}, u32[]{:S(2)}) %copy-start.1) | copy-done | bytes 2097176
  30.8 2.0 %delay_transform.5 = (bf16[4,256,128]{2,1,0:T(8,128)(2,1)S(1)}, bf16[4,256,128]{2,1,0:T(8,128)(2,1)S(1)}, bf16[4,256,128]{2,1,0:T(8,128)(2,1)S(1)}, bf16[4,256,128]{2,1,0:T(8,128)(2,1)S(1)}) custom-call(s32[1]{0:T(128)} %bitcast.me_ref, bf16[4,512,512]{2,1,0:T(8,128)(2,1)S(1)} %copy-done.1, bf16[4,256,128]{2,1,0:T(8,128)(2,1)S(1)} %copy-done.6, ...), custom_call_target="tpu_custom_call" | custom-call | flops 1000000000 | bytes 2097152 | tf_op jit(solution)/shard_map/delay_transform/pallas_call | solution.py:259
  32.9 1.6 %collective-permute-start.10 = (bf16[4,256,128]{2,1,0:T(8,128)(2,1)S(1)}, bf16[4,256,128]{2,1,0:T(8,128)(2,1)S(1)}, u32[]{:S(2)}, u32[]{:S(2)}) collective-permute-start(bf16[4,256,128]{2,1,0:T(8,128)(2,1)S(1)} %get-tuple-element.49), channel_id=1, source_target_pairs={{0,16},{8,24},{16,0},{24,8},{1,17},{9,25},{17,1},{25,9},{2,18},{10... | collective-permute-start | bytes 786440 | tf_op jit(solution)/shard_map/ppermute | solution.py:34
  34.4 2.0 %collective-permute-start.11 = (bf16[4,256,128]{2,1,0:T(8,128)(2,1)S(1)}, bf16[4,256,128]{2,1,0:T(8,128)(2,1)S(1)}, u32[]{:S(2)}, u32[]{:S(2)}) collective-permute-start(bf16[4,256,128]{2,1,0:T(8,128)(2,1)S(1)} %get-tuple-element.50), channel_id=1, source_target_pairs={{0,24},{8,0},{16,8},{24,16},{1,25},{9,1},{17,9},{25,17},{2,26},{10... | collective-permute-start | bytes 786440 | tf_op jit(solution)/shard_map/ppermute | solution.py:34
  36.4 0.0 collective-permute-start.9
  36.5 3.6 %collective-permute-done.1.refs_2_ = bf16[4,256,128]{2,1,0:T(8,128)(2,1)S(1)} collective-permute-done((bf16[4,256,128]{2,1,0:T(8,128)(2,1)S(1)}, bf16[4,256,128]{2,1,0:T(8,128)(2,1)S(1)}, u32[]{:S(2)}, u32[]{:S(2)}) %collective-permute-start.1) | collective-permute-done | bytes 262176 | tf_op jit(solution)/shard_map/ppermute | solution.py:34
  40.1 0.5 collective-permute-done.2.refs_3_
  40.5 2.0 %delay_transform.4 = (bf16[4,256,128]{2,1,0:T(8,128)(2,1)S(1)}, bf16[4,256,128]{2,1,0:T(8,128)(2,1)S(1)}, bf16[4,256,128]{2,1,0:T(8,128)(2,1)S(1)}, bf16[4,256,128]{2,1,0:T(8,128)(2,1)S(1)}) custom-call(s32[1]{0:T(128)} %bitcast.me_ref, bf16[4,512,512]{2,1,0:T(8,128)(2,1)S(1)} %copy-done.1, bf16[4,256,128]{2,1,0:T(8,128)(2,1)S(1)} %copy-done.5, ...), custom_call_target="tpu_custom_call" | custom-call | flops 1000000000 | bytes 2097152 | tf_op jit(solution)/shard_map/delay_transform/pallas_call | solution.py:259
  42.5 7.0 %collective-permute-start.3 = (bf16[4,256,128]{2,1,0:T(8,128)(2,1)S(1)}, bf16[4,256,128]{2,1,0:T(8,128)(2,1)S(1)}, u32[]{:S(2)}, u32[]{:S(2)}) collective-permute-start(bf16[4,256,128]{2,1,0:T(8,128)(2,1)S(1)} %get-tuple-element.40), channel_id=1, source_target_pairs={{0,8},{8,16},{16,24},{24,0},{1,9},{9,17},{17,25},{25,1},{2,10},{10... | collective-permute-start | bytes 786440 | tf_op jit(solution)/shard_map/ppermute | solution.py:34
  49.5 0.6 collective-permute-start.4
  50.1 3.0 %collective-permute-start.5 = (bf16[4,256,128]{2,1,0:T(8,128)(2,1)S(1)}, bf16[4,256,128]{2,1,0:T(8,128)(2,1)S(1)}, u32[]{:S(2)}, u32[]{:S(2)}) collective-permute-start(bf16[4,256,128]{2,1,0:T(8,128)(2,1)S(1)} %get-tuple-element.42), channel_id=1, source_target_pairs={{0,24},{8,0},{16,8},{24,16},{1,25},{9,1},{17,9},{25,17},{2,26},{10... | collective-permute-start | bytes 786440 | tf_op jit(solution)/shard_map/ppermute | solution.py:34
  53.1 4.2 %collective-permute-done.3.refs_1_ = bf16[4,256,128]{2,1,0:T(8,128)(2,1)S(1)} collective-permute-done((bf16[4,256,128]{2,1,0:T(8,128)(2,1)S(1)}, bf16[4,256,128]{2,1,0:T(8,128)(2,1)S(1)}, u32[]{:S(2)}, u32[]{:S(2)}) %collective-permute-start.3) | collective-permute-done | bytes 262176 | tf_op jit(solution)/shard_map/ppermute | solution.py:34
  57.4 5.1 %collective-permute-done.4.refs_2_ = bf16[4,256,128]{2,1,0:T(8,128)(2,1)S(1)} collective-permute-done((bf16[4,256,128]{2,1,0:T(8,128)(2,1)S(1)}, bf16[4,256,128]{2,1,0:T(8,128)(2,1)S(1)}, u32[]{:S(2)}, u32[]{:S(2)}) %collective-permute-start.4) | collective-permute-done | bytes 262176 | tf_op jit(solution)/shard_map/ppermute | solution.py:34
  62.5 0.2 collective-permute-done.5.refs_3_
  62.6 0.5 join_pieces.1
  63.1 1.3 %copy-done = bf16[8,1024,128]{2,1,0:T(8,128)(2,1)} copy-done((bf16[8,1024,128]{2,1,0:T(8,128)(2,1)}, bf16[8,1024,128]{2,1,0:T(8,128)(2,1)S(1)}, u32[]{:S(2)}) %copy-start) | copy-done | bytes 2097176
  64.4 0.0 all-to-all-done.refs_0_
  64.5 4.9 %all-to-all-start.1 = ((bf16[8,1024,128]{2,1,0:T(8,128)(2,1)}), bf16[8,1024,128]{2,1,0:T(8,128)(2,1)}, u32[]{:S(2)}, u32[]{:S(2)}) async-start(bf16[8,1024,128]{2,1,0:T(8,128)(2,1)} %copy-done), calls=%async_computation.1 | async-start | bytes 4194304 | tf_op jit(solution)/shard_map/all_to_all | solution.py:521
  69.4 1.1 fusion.3
  70.5 1.6 %collective-permute-start.15 = (bf16[4,256,128]{2,1,0:T(8,128)(2,1)}, bf16[4,256,128]{2,1,0:T(8,128)(2,1)S(1)}, u32[]{:S(2)}, u32[]{:S(2)}) collective-permute-start(bf16[4,256,128]{2,1,0:T(8,128)(2,1)} %get-tuple-element.67), channel_id=1, source_target_pairs={{0,8},{8,16},{16,24},{24,0},{1,9},{9,17},{17,25},{25,1},{2,10},{10... | collective-permute-start | bytes 786440 | tf_op jit(solution)/shard_map/ppermute | solution.py:34
  72.1 0.5 collective-permute-start.16
  72.6 2.1 %collective-permute-start.17 = (bf16[4,256,128]{2,1,0:T(8,128)(2,1)}, bf16[4,256,128]{2,1,0:T(8,128)(2,1)S(1)}, u32[]{:S(2)}, u32[]{:S(2)}) collective-permute-start(bf16[4,256,128]{2,1,0:T(8,128)(2,1)} %get-tuple-element.65), channel_id=1, source_target_pairs={{0,24},{8,0},{16,8},{24,16},{1,25},{9,1},{17,9},{25,17},{2,26},{10... | collective-permute-start | bytes 786440 | tf_op jit(solution)/shard_map/ppermute | solution.py:34
  74.8 0.1 reshape.34
  74.9 1.0 pad_maximum_fusion
  75.9 0.1 collective-permute-start.12
  75.9 1.4 %collective-permute-start.13 = (bf16[4,272,128]{2,1,0:T(8,128)(2,1)S(1)}, bf16[4,272,128]{2,1,0:T(8,128)(2,1)S(1)}, u32[]{:S(2)}, u32[]{:S(2)}) collective-permute-start(bf16[4,272,128]{2,1,0:T(8,128)(2,1)S(1)} %get-tuple-element.76), channel_id=1, source_target_pairs={{0,16},{8,24},{16,0},{24,8},{1,17},{9,25},{17,1},{25,9},{2,18},{10... | collective-permute-start | bytes 835592 | tf_op jit(solution)/shard_map/ppermute | solution.py:34
  77.3 3.4 %collective-permute-done.15.refs_1_ = bf16[4,256,128]{2,1,0:T(8,128)(2,1)S(1)} collective-permute-done((bf16[4,256,128]{2,1,0:T(8,128)(2,1)}, bf16[4,256,128]{2,1,0:T(8,128)(2,1)S(1)}, u32[]{:S(2)}, u32[]{:S(2)}) %collective-permute-start.15) | collective-permute-done | bytes 262176 | tf_op jit(solution)/shard_map/ppermute | solution.py:34
  80.7 0.6 collective-permute-start.14
  81.4 5.0 %collective-permute-done.16.refs_2_ = bf16[4,256,128]{2,1,0:T(8,128)(2,1)S(1)} collective-permute-done((bf16[4,256,128]{2,1,0:T(8,128)(2,1)}, bf16[4,256,128]{2,1,0:T(8,128)(2,1)S(1)}, u32[]{:S(2)}, u32[]{:S(2)}) %collective-permute-start.16) | collective-permute-done | bytes 262176 | tf_op jit(solution)/shard_map/ppermute | solution.py:34
  86.4 0.0 collective-permute-done.17.refs_3_
  86.4 1.6 %copy-done.2 = bf16[4,512,512]{2,1,0:T(8,128)(2,1)S(1)} copy-done((bf16[4,512,512]{2,1,0:T(8,128)(2,1)S(1)}, bf16[4,512,512]{2,1,0:T(8,128)(2,1)}, u32[]{:S(2)}) %copy-start.2) | copy-done | bytes 2097176
  88.0 2.1 %delay_transform.7 = (bf16[4,256,128]{2,1,0:T(8,128)(2,1)S(1)}, bf16[4,256,128]{2,1,0:T(8,128)(2,1)S(1)}, bf16[4,256,128]{2,1,0:T(8,128)(2,1)}, bf16[4,256,128]{2,1,0:T(8,128)(2,1)S(1)}) custom-call(s32[1]{0:T(128)} %bitcast.me_ref, bf16[4,512,512]{2,1,0:T(8,128)(2,1)S(1)} %copy-done.2, bf16[8,1040,128]{2,1,0:T(8,128)(2,1)S(1)} %all-to-all-done.refs_0_, ...), custom_call_target="tpu_custom_call" | custom-call | flops 1000000000 | bytes 2097152 | tf_op jit(solution)/shard_map/delay_transform/pallas_call | solution.py:259
  90.1 1.9 %collective-permute-start.19 = (bf16[4,256,128]{2,1,0:T(8,128)(2,1)S(1)}, bf16[4,256,128]{2,1,0:T(8,128)(2,1)S(1)}, u32[]{:S(2)}, u32[]{:S(2)}) collective-permute-start(bf16[4,256,128]{2,1,0:T(8,128)(2,1)S(1)} %get-tuple-element.58), channel_id=1, source_target_pairs={{0,8},{8,16},{16,24},{24,0},{1,9},{9,17},{17,25},{25,1},{2,10},{10... | collective-permute-start | bytes 786440 | tf_op jit(solution)/shard_map/ppermute | solution.py:34
  92.0 0.7 collective-permute-start.21
  92.7 1.7 %collective-permute-start.23 = (bf16[4,256,128]{2,1,0:T(8,128)(2,1)S(1)}, bf16[4,256,128]{2,1,0:T(8,128)(2,1)S(1)}, u32[]{:S(2)}, u32[]{:S(2)}) collective-permute-start(bf16[4,256,128]{2,1,0:T(8,128)(2,1)S(1)} %get-tuple-element.62), channel_id=1, source_target_pairs={{0,24},{8,0},{16,8},{24,16},{1,25},{9,1},{17,9},{25,17},{2,26},{10... | collective-permute-start | bytes 786440 | tf_op jit(solution)/shard_map/ppermute | solution.py:34
  94.4 3.9 %collective-permute-done.13.refs_2_ = bf16[4,272,128]{2,1,0:T(8,128)(2,1)S(1)} collective-permute-done((bf16[4,272,128]{2,1,0:T(8,128)(2,1)S(1)}, bf16[4,272,128]{2,1,0:T(8,128)(2,1)S(1)}, u32[]{:S(2)}, u32[]{:S(2)}) %collective-permute-start.13) | collective-permute-done | bytes 278560 | tf_op jit(solution)/shard_map/ppermute | solution.py:34
  98.3 2.0 %delay_transform.6 = (bf16[4,256,128]{2,1,0:T(8,128)(2,1)S(1)}, bf16[4,256,128]{2,1,0:T(8,128)(2,1)}, bf16[4,256,128]{2,1,0:T(8,128)(2,1)}, bf16[4,256,128]{2,1,0:T(8,128)(2,1)}) custom-call(s32[1]{0:T(128)} %bitcast.me_ref, bf16[4,512,512]{2,1,0:T(8,128)(2,1)S(1)} %copy-done.2, bf16[8,1040,128]{2,1,0:T(8,128)(2,1)S(1)} %all-to-all-done.refs_0_, ...), custom_call_target="tpu_custom_call" | custom-call | flops 1000000000 | bytes 2097152 | tf_op jit(solution)/shard_map/delay_transform/pallas_call | solution.py:259
  100.4 0.7 copy-done.3
  101.1 1.9 %collective-permute-start.18 = (bf16[4,256,128]{2,1,0:T(8,128)(2,1)}, bf16[4,256,128]{2,1,0:T(8,128)(2,1)S(1)}, u32[]{:S(2)}, u32[]{:S(2)}) collective-permute-start(bf16[4,256,128]{2,1,0:T(8,128)(2,1)} %get-tuple-element.57), channel_id=1, source_target_pairs={{0,8},{8,16},{16,24},{24,0},{1,9},{9,17},{17,25},{25,1},{2,10},{10... | collective-permute-start | bytes 786440 | tf_op jit(solution)/shard_map/ppermute | solution.py:34
  103.0 0.3 collective-permute-start.20
  103.3 0.7 collective-permute-done.19.refs_3_
  104.0 1.3 %collective-permute-start.22 = (bf16[4,256,128]{2,1,0:T(8,128)(2,1)}, bf16[4,256,128]{2,1,0:T(8,128)(2,1)S(1)}, u32[]{:S(2)}, u32[]{:S(2)}) collective-permute-start(bf16[4,256,128]{2,1,0:T(8,128)(2,1)} %get-tuple-element.61), channel_id=1, source_target_pairs={{0,24},{8,0},{16,8},{24,16},{1,25},{9,1},{17,9},{25,17},{2,26},{10... | collective-permute-start | bytes 786440 | tf_op jit(solution)/shard_map/ppermute | solution.py:34
  105.3 1.9 %pair_weights.1 = (bf16[512,512]{1,0:T(8,128)(2,1)S(1)}, f32[64,512]{1,0:T(8,128)S(1)}) custom-call(s32[1]{0:T(128)} %bitcast.me_ref, bf16[4,16,128]{2,1,0:T(8,128)(2,1)S(1)} %bitcast.13, bf16[4,272,128]{2,1,0:T(8,128)(2,1)S(1)} %collective-permute-done.12.refs_1_, bf16[4,272,128]{2,1,0:T(8,128)(2,1)S(1)} %collective-permute-done.13.refs_2_, ...), custom_call_target="tpu_custom_call" | custom-call | flops 536870912 | bytes 1048576 | tf_op jit(solution)/shard_map/pair_weights/pallas_call | solution.py:378
  107.3 11.2 %all-to-all-done.1.refs_0_ = bf16[8,1024,128]{2,1,0:T(8,128)(2,1)} async-done(((bf16[8,1024,128]{2,1,0:T(8,128)(2,1)}), bf16[8,1024,128]{2,1,0:T(8,128)(2,1)}, u32[]{:S(2)}, u32[]{:S(2)}) %all-to-all-start.1) | async-done | bytes 2097184 | tf_op jit(solution)/shard_map/all_to_all | solution.py:521
  118.5 3.1 %pair_sums.2.before_ref = f32[64,256]{1,0:T(8,128)S(1)} custom-call(bf16[512,512]{1,0:T(8,128)(2,1)S(1)} %get-tuple-element.52.mix_ref, f32[64,512]{1,0:T(8,128)S(1)} %get-tuple-element.53.group_ref, f32[64,256]{1,0:T(8,128)S(1)} %broadcast_in_dim.3.before_ref, bf16[8,1024,128]{2,1,0:T(8,128)(2,1)} %all-to-all-done.1.refs_0_), custom_call_target="tpu_custom_call" | custom-call | flops 1073741824 | bytes 2097152 | tf_op jit(solution)/shard_map/pair_sums/pallas_call | solution.py:452
  121.7 1.5 %pair_sums.3 = f32[64,256]{1,0:T(8,128)S(1)} custom-call(bf16[512,512]{1,0:T(8,128)(2,1)S(1)} %get-tuple-element.52.mix_ref, f32[64,512]{1,0:T(8,128)S(1)} %get-tuple-element.53.group_ref, f32[64,256]{1,0:T(8,128)S(1)} %pair_sums.2.before_ref, bf16[4,256,128]{2,1,0:T(8,128)(2,1)S(1)} %copy-done.4, bf16[4,256,128]{2,1,0:T(8,128)(2,1)S(1)} %get-tuple-element.56.refs_1_, ...), custom_call_target="tpu_custom_call" | custom-call | flops 1073741824 | bytes 2097152 | tf_op jit(solution)/shard_map/pair_sums/pallas_call | solution.py:452
  123.2 1.7 %collective-permute-start.24 = (f32[16,256]{1,0:T(8,128)S(1)}, f32[16,256]{1,0:T(8,128)S(1)}, u32[]{:S(2)}, u32[]{:S(2)}) collective-permute-start(f32[16,256]{1,0:T(8,128)S(1)} %get-tuple-element.73), channel_id=1, source_target_pairs={{0,8},{8,16},{16,24},{24,0},{1,9},{9,17},{17,25},{25,1},{2,10},{10... | collective-permute-start | bytes 49160 | tf_op jit(solution)/shard_map/ppermute | solution.py:34
  124.9 0.5 collective-permute-start.25
  125.4 2.1 %collective-permute-start.26 = (f32[16,256]{1,0:T(8,128)S(1)}, f32[16,256]{1,0:T(8,128)S(1)}, u32[]{:S(2)}, u32[]{:S(2)}) collective-permute-start(f32[16,256]{1,0:T(8,128)S(1)} %get-tuple-element.71), channel_id=1, source_target_pairs={{0,24},{8,0},{16,8},{24,16},{1,25},{9,1},{17,9},{25,17},{2,26},{10... | collective-permute-start | bytes 49160 | tf_op jit(solution)/shard_map/ppermute | solution.py:34
  127.6 0.4 collective-permute-done.24.refs_1_
  127.9 0.7 collective-permute-done.25.refs_2_
  128.7 0.5 collective-permute-done.26.refs_3_
  129.2 1.1 interleave_delays.1
  (40 shorter events, 0.1 us)
Async XLA Ops:
  6.8 11.0 %copy-start.10 = (bf16[4,256,128]{2,1,0:T(8,128)(2,1)S(1)}, bf16[4,256,128]{2,1,0:T(8,128)(2,1)}, u32[]{:S(2)}) copy-start(bf16[4,256,128]{2,1,0:T(8,128)(2,1)} %get-tuple-element.36) | copy-start | bytes 786436
  6.8 11.6 %copy-start.9 = (bf16[4,256,128]{2,1,0:T(8,128)(2,1)S(1)}, bf16[4,256,128]{2,1,0:T(8,128)(2,1)}, u32[]{:S(2)}) copy-start(bf16[4,256,128]{2,1,0:T(8,128)(2,1)} %get-tuple-element.37) | copy-start | bytes 786436
  6.8 16.8 %copy-start.8 = (bf16[4,256,128]{2,1,0:T(8,128)(2,1)S(1)}, bf16[4,256,128]{2,1,0:T(8,128)(2,1)}, u32[]{:S(2)}) copy-start(bf16[4,256,128]{2,1,0:T(8,128)(2,1)} %get-tuple-element.38) | copy-start | bytes 786436
  6.8 22.4 %copy-start.6 = (bf16[4,256,128]{2,1,0:T(8,128)(2,1)S(1)}, bf16[4,256,128]{2,1,0:T(8,128)(2,1)}, u32[]{:S(2)}) copy-start(bf16[4,256,128]{2,1,0:T(8,128)(2,1)} %get-tuple-element.43.refs_0_) | copy-start | bytes 786436
  6.8 33.7 %copy-start.5 = (bf16[4,256,128]{2,1,0:T(8,128)(2,1)S(1)}, bf16[4,256,128]{2,1,0:T(8,128)(2,1)}, u32[]{:S(2)}) copy-start(bf16[4,256,128]{2,1,0:T(8,128)(2,1)} %get-tuple-element.35.refs_0_) | copy-start | bytes 786436
  6.8 57.6 %all-to-all-start = ((bf16[8,1040,128]{2,1,0:T(8,128)(2,1)}), bf16[8,1040,128]{2,1,0:T(8,128)(2,1)S(1)}, u32[]{:S(2)}, u32[]{:S(2)}) async-start(bf16[8,1040,128]{2,1,0:T(8,128)(2,1)} %get-tuple-element.34), calls=%async_computation | async-start | bytes 4259840 | tf_op jit(solution)/shard_map/all_to_all | solution.py:515
  13.3 10.3 %collective-permute-start.6 = (bf16[4,256,128]{2,1,0:T(8,128)(2,1)}, bf16[4,256,128]{2,1,0:T(8,128)(2,1)S(1)}, u32[]{:S(2)}, u32[]{:S(2)}) collective-permute-start(bf16[4,256,128]{2,1,0:T(8,128)(2,1)} %get-tuple-element.44), channel_id=1, source_target_pairs={{0,8},{8,16},{16,24},{24,0},{1,9},{9,17},{17,25},{25,1},{2,10},{10... | collective-permute-start | bytes 786440 | tf_op jit(solution)/shard_map/ppermute | solution.py:34
  14.8 14.4 %collective-permute-start.7 = (bf16[4,256,128]{2,1,0:T(8,128)(2,1)}, bf16[4,256,128]{2,1,0:T(8,128)(2,1)S(1)}, u32[]{:S(2)}, u32[]{:S(2)}) collective-permute-start(bf16[4,256,128]{2,1,0:T(8,128)(2,1)} %get-tuple-element.45), channel_id=1, source_target_pairs={{0,16},{8,24},{16,0},{24,8},{1,17},{9,25},{17,1},{25,9},{2,18},{10... | collective-permute-start | bytes 786440 | tf_op jit(solution)/shard_map/ppermute | solution.py:34
  16.3 12.9 %collective-permute-start.8 = (bf16[4,256,128]{2,1,0:T(8,128)(2,1)}, bf16[4,256,128]{2,1,0:T(8,128)(2,1)S(1)}, u32[]{:S(2)}, u32[]{:S(2)}) collective-permute-start(bf16[4,256,128]{2,1,0:T(8,128)(2,1)} %get-tuple-element.46), channel_id=1, source_target_pairs={{0,24},{8,0},{16,8},{24,16},{1,25},{9,1},{17,9},{25,17},{2,26},{10... | collective-permute-start | bytes 786440 | tf_op jit(solution)/shard_map/ppermute | solution.py:34
  17.8 18.7 %collective-permute-start = (bf16[4,256,128]{2,1,0:T(8,128)(2,1)S(1)}, bf16[4,256,128]{2,1,0:T(8,128)(2,1)S(1)}, u32[]{:S(2)}, u32[]{:S(2)}) collective-permute-start(bf16[4,256,128]{2,1,0:T(8,128)(2,1)S(1)} %copy-done.10), channel_id=1, source_target_pairs={{0,8},{8,16},{16,24},{24,0},{1,9},{9,17},{17,25},{25,1},{2,10},{10... | collective-permute-start | bytes 786440 | tf_op jit(solution)/shard_map/ppermute | solution.py:34
  18.4 21.7 %collective-permute-start.1 = (bf16[4,256,128]{2,1,0:T(8,128)(2,1)S(1)}, bf16[4,256,128]{2,1,0:T(8,128)(2,1)S(1)}, u32[]{:S(2)}, u32[]{:S(2)}) collective-permute-start(bf16[4,256,128]{2,1,0:T(8,128)(2,1)S(1)} %copy-done.9), channel_id=1, source_target_pairs={{0,16},{8,24},{16,0},{24,8},{1,17},{9,25},{17,1},{25,9},{2,18},{10... | collective-permute-start | bytes 786440 | tf_op jit(solution)/shard_map/ppermute | solution.py:34
  23.6 16.9 %collective-permute-start.2 = (bf16[4,256,128]{2,1,0:T(8,128)(2,1)S(1)}, bf16[4,256,128]{2,1,0:T(8,128)(2,1)S(1)}, u32[]{:S(2)}, u32[]{:S(2)}) collective-permute-start(bf16[4,256,128]{2,1,0:T(8,128)(2,1)S(1)} %copy-done.8), channel_id=1, source_target_pairs={{0,24},{8,0},{16,8},{24,16},{1,25},{9,1},{17,9},{25,17},{2,26},{10... | collective-permute-start | bytes 786440 | tf_op jit(solution)/shard_map/ppermute | solution.py:34
  29.2 1.6 %copy-start.1 = (bf16[4,512,512]{2,1,0:T(8,128)(2,1)S(1)}, bf16[4,512,512]{2,1,0:T(8,128)(2,1)}, u32[]{:S(2)}) copy-start(bf16[4,512,512]{2,1,0:T(8,128)(2,1)} %constant.14.clone.matrix_hbm) | copy-start | bytes 6291460
  32.9 17.2 %collective-permute-start.10 = (bf16[4,256,128]{2,1,0:T(8,128)(2,1)S(1)}, bf16[4,256,128]{2,1,0:T(8,128)(2,1)S(1)}, u32[]{:S(2)}, u32[]{:S(2)}) collective-permute-start(bf16[4,256,128]{2,1,0:T(8,128)(2,1)S(1)} %get-tuple-element.49), channel_id=1, source_target_pairs={{0,16},{8,24},{16,0},{24,8},{1,17},{9,25},{17,1},{25,9},{2,18},{10... | collective-permute-start | bytes 786440 | tf_op jit(solution)/shard_map/ppermute | solution.py:34
  34.4 18.7 %collective-permute-start.11 = (bf16[4,256,128]{2,1,0:T(8,128)(2,1)S(1)}, bf16[4,256,128]{2,1,0:T(8,128)(2,1)S(1)}, u32[]{:S(2)}, u32[]{:S(2)}) collective-permute-start(bf16[4,256,128]{2,1,0:T(8,128)(2,1)S(1)} %get-tuple-element.50), channel_id=1, source_target_pairs={{0,24},{8,0},{16,8},{24,16},{1,25},{9,1},{17,9},{25,17},{2,26},{10... | collective-permute-start | bytes 786440 | tf_op jit(solution)/shard_map/ppermute | solution.py:34
  36.4 16.7 %collective-permute-start.9 = (bf16[4,256,128]{2,1,0:T(8,128)(2,1)S(1)}, bf16[4,256,128]{2,1,0:T(8,128)(2,1)S(1)}, u32[]{:S(2)}, u32[]{:S(2)}) collective-permute-start(bf16[4,256,128]{2,1,0:T(8,128)(2,1)S(1)} %get-tuple-element.48), channel_id=1, source_target_pairs={{0,8},{8,16},{16,24},{24,0},{1,9},{9,17},{17,25},{25,1},{2,10},{10... | collective-permute-start | bytes 786440 | tf_op jit(solution)/shard_map/ppermute | solution.py:34
  42.5 14.8 %collective-permute-start.3 = (bf16[4,256,128]{2,1,0:T(8,128)(2,1)S(1)}, bf16[4,256,128]{2,1,0:T(8,128)(2,1)S(1)}, u32[]{:S(2)}, u32[]{:S(2)}) collective-permute-start(bf16[4,256,128]{2,1,0:T(8,128)(2,1)S(1)} %get-tuple-element.40), channel_id=1, source_target_pairs={{0,8},{8,16},{16,24},{24,0},{1,9},{9,17},{17,25},{25,1},{2,10},{10... | collective-permute-start | bytes 786440 | tf_op jit(solution)/shard_map/ppermute | solution.py:34
  49.5 12.9 %collective-permute-start.4 = (bf16[4,256,128]{2,1,0:T(8,128)(2,1)S(1)}, bf16[4,256,128]{2,1,0:T(8,128)(2,1)S(1)}, u32[]{:S(2)}, u32[]{:S(2)}) collective-permute-start(bf16[4,256,128]{2,1,0:T(8,128)(2,1)S(1)} %get-tuple-element.41), channel_id=1, source_target_pairs={{0,16},{8,24},{16,0},{24,8},{1,17},{9,25},{17,1},{25,9},{2,18},{10... | collective-permute-start | bytes 786440 | tf_op jit(solution)/shard_map/ppermute | solution.py:34
  50.1 12.6 %collective-permute-start.5 = (bf16[4,256,128]{2,1,0:T(8,128)(2,1)S(1)}, bf16[4,256,128]{2,1,0:T(8,128)(2,1)S(1)}, u32[]{:S(2)}, u32[]{:S(2)}) collective-permute-start(bf16[4,256,128]{2,1,0:T(8,128)(2,1)S(1)} %get-tuple-element.42), channel_id=1, source_target_pairs={{0,24},{8,0},{16,8},{24,16},{1,25},{9,1},{17,9},{25,17},{2,26},{10... | collective-permute-start | bytes 786440 | tf_op jit(solution)/shard_map/ppermute | solution.py:34
  63.1 1.3 %copy-start = (bf16[8,1024,128]{2,1,0:T(8,128)(2,1)}, bf16[8,1024,128]{2,1,0:T(8,128)(2,1)S(1)}, u32[]{:S(2)}) copy-start(bf16[8,1024,128]{2,1,0:T(8,128)(2,1)S(1)} %join_pieces.1) | copy-start | bytes 6291460
  64.4 4.9 %copy-start.7 = (s32[256,2]{0,1:T(2,128)S(1)}, s32[256,2]{0,1:T(2,128)}, u32[]{:S(2)}) copy-start(s32[256,2]{0,1:T(2,128)} %param.11) | copy-start | bytes 6148
  64.4 4.9 %copy-start.11 = (s32[128]{0:T(128)S(1)}, s32[128]{0:T(128)}, u32[]{:S(2)}) copy-start(s32[128]{0:T(128)} %param.10) | copy-start | bytes 1540
  64.5 54.0 %all-to-all-start.1 = ((bf16[8,1024,128]{2,1,0:T(8,128)(2,1)}), bf16[8,1024,128]{2,1,0:T(8,128)(2,1)}, u32[]{:S(2)}, u32[]{:S(2)}) async-start(bf16[8,1024,128]{2,1,0:T(8,128)(2,1)} %copy-done), calls=%async_computation.1 | async-start | bytes 4194304 | tf_op jit(solution)/shard_map/all_to_all | solution.py:521
  70.5 10.3 %collective-permute-start.15 = (bf16[4,256,128]{2,1,0:T(8,128)(2,1)}, bf16[4,256,128]{2,1,0:T(8,128)(2,1)S(1)}, u32[]{:S(2)}, u32[]{:S(2)}) collective-permute-start(bf16[4,256,128]{2,1,0:T(8,128)(2,1)} %get-tuple-element.67), channel_id=1, source_target_pairs={{0,8},{8,16},{16,24},{24,0},{1,9},{9,17},{17,25},{25,1},{2,10},{10... | collective-permute-start | bytes 786440 | tf_op jit(solution)/shard_map/ppermute | solution.py:34
  72.1 14.3 %collective-permute-start.16 = (bf16[4,256,128]{2,1,0:T(8,128)(2,1)}, bf16[4,256,128]{2,1,0:T(8,128)(2,1)S(1)}, u32[]{:S(2)}, u32[]{:S(2)}) collective-permute-start(bf16[4,256,128]{2,1,0:T(8,128)(2,1)} %get-tuple-element.66), channel_id=1, source_target_pairs={{0,16},{8,24},{16,0},{24,8},{1,17},{9,25},{17,1},{25,9},{2,18},{10... | collective-permute-start | bytes 786440 | tf_op jit(solution)/shard_map/ppermute | solution.py:34
  72.6 13.8 %collective-permute-start.17 = (bf16[4,256,128]{2,1,0:T(8,128)(2,1)}, bf16[4,256,128]{2,1,0:T(8,128)(2,1)S(1)}, u32[]{:S(2)}, u32[]{:S(2)}) collective-permute-start(bf16[4,256,128]{2,1,0:T(8,128)(2,1)} %get-tuple-element.65), channel_id=1, source_target_pairs={{0,24},{8,0},{16,8},{24,16},{1,25},{9,1},{17,9},{25,17},{2,26},{10... | collective-permute-start | bytes 786440 | tf_op jit(solution)/shard_map/ppermute | solution.py:34
  75.9 16.8 %collective-permute-start.12 = (bf16[4,272,128]{2,1,0:T(8,128)(2,1)S(1)}, bf16[4,272,128]{2,1,0:T(8,128)(2,1)S(1)}, u32[]{:S(2)}, u32[]{:S(2)}) collective-permute-start(bf16[4,272,128]{2,1,0:T(8,128)(2,1)S(1)} %get-tuple-element.77), channel_id=1, source_target_pairs={{0,8},{8,16},{16,24},{24,0},{1,9},{9,17},{17,25},{25,1},{2,10},{10... | collective-permute-start | bytes 835592 | tf_op jit(solution)/shard_map/ppermute | solution.py:34
  75.9 22.4 %collective-permute-start.13 = (bf16[4,272,128]{2,1,0:T(8,128)(2,1)S(1)}, bf16[4,272,128]{2,1,0:T(8,128)(2,1)S(1)}, u32[]{:S(2)}, u32[]{:S(2)}) collective-permute-start(bf16[4,272,128]{2,1,0:T(8,128)(2,1)S(1)} %get-tuple-element.76), channel_id=1, source_target_pairs={{0,16},{8,24},{16,0},{24,8},{1,17},{9,25},{17,1},{25,9},{2,18},{10... | collective-permute-start | bytes 835592 | tf_op jit(solution)/shard_map/ppermute | solution.py:34
  80.7 17.6 %collective-permute-start.14 = (bf16[4,272,128]{2,1,0:T(8,128)(2,1)S(1)}, bf16[4,272,128]{2,1,0:T(8,128)(2,1)S(1)}, u32[]{:S(2)}, u32[]{:S(2)}) collective-permute-start(bf16[4,272,128]{2,1,0:T(8,128)(2,1)S(1)} %get-tuple-element.75), channel_id=1, source_target_pairs={{0,24},{8,0},{16,8},{24,16},{1,25},{9,1},{17,9},{25,17},{2,26},{10... | collective-permute-start | bytes 835592 | tf_op jit(solution)/shard_map/ppermute | solution.py:34
  86.4 1.6 %copy-start.2 = (bf16[4,512,512]{2,1,0:T(8,128)(2,1)S(1)}, bf16[4,512,512]{2,1,0:T(8,128)(2,1)}, u32[]{:S(2)}) copy-start(bf16[4,512,512]{2,1,0:T(8,128)(2,1)} %constant.14.clone.matrix_hbm) | copy-start | bytes 6291460
  90.1 13.9 %collective-permute-start.19 = (bf16[4,256,128]{2,1,0:T(8,128)(2,1)S(1)}, bf16[4,256,128]{2,1,0:T(8,128)(2,1)S(1)}, u32[]{:S(2)}, u32[]{:S(2)}) collective-permute-start(bf16[4,256,128]{2,1,0:T(8,128)(2,1)S(1)} %get-tuple-element.58), channel_id=1, source_target_pairs={{0,8},{8,16},{16,24},{24,0},{1,9},{9,17},{17,25},{25,1},{2,10},{10... | collective-permute-start | bytes 786440 | tf_op jit(solution)/shard_map/ppermute | solution.py:34
  92.0 29.6 %collective-permute-start.21 = (bf16[4,256,128]{2,1,0:T(8,128)(2,1)}, bf16[4,256,128]{2,1,0:T(8,128)(2,1)S(1)}, u32[]{:S(2)}, u32[]{:S(2)}) collective-permute-start(bf16[4,256,128]{2,1,0:T(8,128)(2,1)} %get-tuple-element.60), channel_id=1, source_target_pairs={{0,16},{8,24},{16,0},{24,8},{1,17},{9,25},{17,1},{25,9},{2,18},{10... | collective-permute-start | bytes 786440 | tf_op jit(solution)/shard_map/ppermute | solution.py:34
  92.7 28.9 %collective-permute-start.23 = (bf16[4,256,128]{2,1,0:T(8,128)(2,1)S(1)}, bf16[4,256,128]{2,1,0:T(8,128)(2,1)S(1)}, u32[]{:S(2)}, u32[]{:S(2)}) collective-permute-start(bf16[4,256,128]{2,1,0:T(8,128)(2,1)S(1)} %get-tuple-element.62), channel_id=1, source_target_pairs={{0,24},{8,0},{16,8},{24,16},{1,25},{9,1},{17,9},{25,17},{2,26},{10... | collective-permute-start | bytes 786440 | tf_op jit(solution)/shard_map/ppermute | solution.py:34
  100.3 0.7 copy-start.3
  101.1 20.6 %collective-permute-start.18 = (bf16[4,256,128]{2,1,0:T(8,128)(2,1)}, bf16[4,256,128]{2,1,0:T(8,128)(2,1)S(1)}, u32[]{:S(2)}, u32[]{:S(2)}) collective-permute-start(bf16[4,256,128]{2,1,0:T(8,128)(2,1)} %get-tuple-element.57), channel_id=1, source_target_pairs={{0,8},{8,16},{16,24},{24,0},{1,9},{9,17},{17,25},{25,1},{2,10},{10... | collective-permute-start | bytes 786440 | tf_op jit(solution)/shard_map/ppermute | solution.py:34
  103.0 18.7 %collective-permute-start.20 = (bf16[4,256,128]{2,1,0:T(8,128)(2,1)}, bf16[4,256,128]{2,1,0:T(8,128)(2,1)S(1)}, u32[]{:S(2)}, u32[]{:S(2)}) collective-permute-start(bf16[4,256,128]{2,1,0:T(8,128)(2,1)} %get-tuple-element.59), channel_id=1, source_target_pairs={{0,16},{8,24},{16,0},{24,8},{1,17},{9,25},{17,1},{25,9},{2,18},{10... | collective-permute-start | bytes 786440 | tf_op jit(solution)/shard_map/ppermute | solution.py:34
  104.0 17.7 %collective-permute-start.22 = (bf16[4,256,128]{2,1,0:T(8,128)(2,1)}, bf16[4,256,128]{2,1,0:T(8,128)(2,1)S(1)}, u32[]{:S(2)}, u32[]{:S(2)}) collective-permute-start(bf16[4,256,128]{2,1,0:T(8,128)(2,1)} %get-tuple-element.61), channel_id=1, source_target_pairs={{0,24},{8,0},{16,8},{24,16},{1,25},{9,1},{17,9},{25,17},{2,26},{10... | collective-permute-start | bytes 786440 | tf_op jit(solution)/shard_map/ppermute | solution.py:34
  107.2 14.4 %copy-start.4 = (bf16[4,256,128]{2,1,0:T(8,128)(2,1)S(1)}, bf16[4,256,128]{2,1,0:T(8,128)(2,1)}, u32[]{:S(2)}) copy-start(bf16[4,256,128]{2,1,0:T(8,128)(2,1)} %copy-done.3) | copy-start | bytes 786436
  123.2 4.7 %collective-permute-start.24 = (f32[16,256]{1,0:T(8,128)S(1)}, f32[16,256]{1,0:T(8,128)S(1)}, u32[]{:S(2)}, u32[]{:S(2)}) collective-permute-start(f32[16,256]{1,0:T(8,128)S(1)} %get-tuple-element.73), channel_id=1, source_target_pairs={{0,8},{8,16},{16,24},{24,0},{1,9},{9,17},{17,25},{25,1},{2,10},{10... | collective-permute-start | bytes 49160 | tf_op jit(solution)/shard_map/ppermute | solution.py:34
  124.9 3.7 %collective-permute-start.25 = (f32[16,256]{1,0:T(8,128)S(1)}, f32[16,256]{1,0:T(8,128)S(1)}, u32[]{:S(2)}, u32[]{:S(2)}) collective-permute-start(f32[16,256]{1,0:T(8,128)S(1)} %get-tuple-element.72), channel_id=1, source_target_pairs={{0,16},{8,24},{16,0},{24,8},{1,17},{9,25},{17,1},{25,9},{2,18},{10... | collective-permute-start | bytes 49160 | tf_op jit(solution)/shard_map/ppermute | solution.py:34
  125.4 3.7 %collective-permute-start.26 = (f32[16,256]{1,0:T(8,128)S(1)}, f32[16,256]{1,0:T(8,128)S(1)}, u32[]{:S(2)}, u32[]{:S(2)}) collective-permute-start(f32[16,256]{1,0:T(8,128)S(1)} %get-tuple-element.71), channel_id=1, source_target_pairs={{0,24},{8,0},{16,8},{24,16},{1,25},{9,1},{17,9},{25,17},{2,26},{10... | collective-permute-start | bytes 49160 | tf_op jit(solution)/shard_map/ppermute | solution.py:34

commit v5 on v3

--- a/solution.py
+++ b/solution.py
@@ -15,7 +15,7 @@
 LATE_COST = 10**9
 EARLY_COST = 10**9
 HALVES = 2
-LOADS = 8
+LOADS = 16
 PAIR_ROWS = 2
 BF16_PARTS = 3
 EXTRA_ROWS = 16

time: 131 us -> 131 us (level)
  no operation moved by 1% of the time
where the time goes in v5:
time: 131 us; the launch traced here: 130 us
  starting transfers between devices  51 us (39%)
  waiting for transfers between devices  48.4 us (37%)
  Pallas kernels  23 us (18%)
  local copies, waits for them, and re-layouts  6.48 us (5%)
    ppermute x27, starting transfers between devices, shifted(): return lax.ppermute(value, axis, pairs)  39.7 us
    ppermute x27, waiting for transfers between devices, shifted(): return lax.ppermute(value, axis, pairs)  37.1 us
    all_to_all x1, waiting for transfers between devices, on_device(): late = lax.all_to_all(late, 'bl', split_axis=0, concat_axis=0, tiled=True)  11.2 us
    pallas_call x4, Pallas kernels, delay_transform(): pl.pallas_call(functools.partial(delay_kernel, half), out_shape=[jax.Shap...  8.17 us
    pallas_call x1, Pallas kernels, taper(): pl.pallas_call(functools.partial(taper_kernel, times, parts, band_count),...  6.7 us
    all_to_all x1, starting transfers between devices, on_device(): early = lax.all_to_all(early, 'bl', split_axis=0, concat_axis=0, tiled=True)  6.47 us
    unnamed x24, local copies, waits for them, and re-layouts  5.26 us
    all_to_all x1, starting transfers between devices, on_device(): late = lax.all_to_all(late, 'bl', split_axis=0, concat_axis=0, tiled=True)  4.87 us
  transfers between devices with their start and end apart: 29, of which 15 were waited for; matrix products, arithmetic and copies ran while one was open for 2% of the time, Pallas kernels for 10%

profile of v5, /device:TPU:0, one launch (start us, length us, event | category | flops | bytes accessed | tf_op | source)
XLA Modules:
  0.0 130.2 jit_solution(2219748019592310080)
XLA Ops:
  0.0 6.7 %taper_rows.1 = (bf16[8,1040,128]{2,1,0:T(8,128)(2,1)}, bf16[4,256,128]{2,1,0:T(8,128)(2,1)}, bf16[4,256,128]{2,1,0:T(8,128)(2,1)}, bf16[4,256,128]{2,1,0:T(8,12...) custom-call(s32[1]{0:T(128)} %bitcast.me_ref, ...), custom_call_target="tpu_custom_call" | custom-call | flops 2147483648 | bytes 8388608 | tf_op jit(solution)/shard_map/taper_rows/pallas_call | solution.py:186
  6.8 6.5 %all-to-all-start = ((bf16[8,1040,128]{2,1,0:T(8,128)(2,1)}), bf16[8,1040,128]{2,1,0:T(8,128)(2,1)S(1)}, u32[]{:S(2)}, u32[]{:S(2)}) async-start(bf16[8,1040,128]{2,1,0:T(8,128)(2,1)} %get-tuple-element.34), calls=%async_computation | async-start | bytes 4259840 | tf_op jit(solution)/shard_map/all_to_all | solution.py:513
  13.2 1.5 %collective-permute-start.6 = (bf16[4,256,128]{2,1,0:T(8,128)(2,1)}, bf16[4,256,128]{2,1,0:T(8,128)(2,1)S(1)}, u32[]{:S(2)}, u32[]{:S(2)}) collective-permute-start(bf16[4,256,128]{2,1,0:T(8,128)(2,1)} %get-tuple-element.44), channel_id=1, source_target_pairs={{0,8},{8,16},{16,24},{24,0},{1,9},{9,17},{17,25},{25,1},{2,10},{10... | collective-permute-start | bytes 786440 | tf_op jit(solution)/shard_map/ppermute | solution.py:34
  14.7 1.5 %collective-permute-start.7 = (bf16[4,256,128]{2,1,0:T(8,128)(2,1)}, bf16[4,256,128]{2,1,0:T(8,128)(2,1)S(1)}, u32[]{:S(2)}, u32[]{:S(2)}) collective-permute-start(bf16[4,256,128]{2,1,0:T(8,128)(2,1)} %get-tuple-element.45), channel_id=1, source_target_pairs={{0,16},{8,24},{16,0},{24,8},{1,17},{9,25},{17,1},{25,9},{2,18},{10... | collective-permute-start | bytes 786440 | tf_op jit(solution)/shard_map/ppermute | solution.py:34
  16.2 1.4 %collective-permute-start.8 = (bf16[4,256,128]{2,1,0:T(8,128)(2,1)}, bf16[4,256,128]{2,1,0:T(8,128)(2,1)S(1)}, u32[]{:S(2)}, u32[]{:S(2)}) collective-permute-start(bf16[4,256,128]{2,1,0:T(8,128)(2,1)} %get-tuple-element.46), channel_id=1, source_target_pairs={{0,24},{8,0},{16,8},{24,16},{1,25},{9,1},{17,9},{25,17},{2,26},{10... | collective-permute-start | bytes 786440 | tf_op jit(solution)/shard_map/ppermute | solution.py:34
  17.7 0.6 collective-permute-start
  18.3 0.5 collective-permute-start.1
  18.8 4.7 %collective-permute-done.6.refs_1_ = bf16[4,256,128]{2,1,0:T(8,128)(2,1)S(1)} collective-permute-done((bf16[4,256,128]{2,1,0:T(8,128)(2,1)}, bf16[4,256,128]{2,1,0:T(8,128)(2,1)S(1)}, u32[]{:S(2)}, u32[]{:S(2)}) %collective-permute-start.6) | collective-permute-done | bytes 262176 | tf_op jit(solution)/shard_map/ppermute | solution.py:34
  23.5 1.5 %collective-permute-start.2 = (bf16[4,256,128]{2,1,0:T(8,128)(2,1)S(1)}, bf16[4,256,128]{2,1,0:T(8,128)(2,1)S(1)}, u32[]{:S(2)}, u32[]{:S(2)}) collective-permute-start(bf16[4,256,128]{2,1,0:T(8,128)(2,1)S(1)} %copy-done.8), channel_id=1, source_target_pairs={{0,24},{8,0},{16,8},{24,16},{1,25},{9,1},{17,9},{25,17},{2,26},{10... | collective-permute-start | bytes 786440 | tf_op jit(solution)/shard_map/ppermute | solution.py:34
  25.0 4.1 %collective-permute-done.7.refs_2_ = bf16[4,256,128]{2,1,0:T(8,128)(2,1)S(1)} collective-permute-done((bf16[4,256,128]{2,1,0:T(8,128)(2,1)}, bf16[4,256,128]{2,1,0:T(8,128)(2,1)S(1)}, u32[]{:S(2)}, u32[]{:S(2)}) %collective-permute-start.7) | collective-permute-done | bytes 262176 | tf_op jit(solution)/shard_map/ppermute | solution.py:34
  29.1 0.0 collective-permute-done.8.refs_3_
  29.2 1.6 %copy-done.1 = bf16[4,512,512]{2,1,0:T(8,128)(2,1)S(1)} copy-done((bf16[4,512,512]{2,1,0:T(8,128)(2,1)S(1)}, bf16[4,512,512]{2,1,0:T(8,128)(2,1)}, u32[]{:S(2)}) %copy-start.1) | copy-done | bytes 2097176
  30.7 2.0 %delay_transform.5 = (bf16[4,256,128]{2,1,0:T(8,128)(2,1)S(1)}, bf16[4,256,128]{2,1,0:T(8,128)(2,1)S(1)}, bf16[4,256,128]{2,1,0:T(8,128)(2,1)S(1)}, bf16[4,256,128]{2,1,0:T(8,128)(2,1)S(1)}) custom-call(s32[1]{0:T(128)} %bitcast.me_ref, bf16[4,512,512]{2,1,0:T(8,128)(2,1)S(1)} %copy-done.1, bf16[4,256,128]{2,1,0:T(8,128)(2,1)S(1)} %copy-done.6, ...), custom_call_target="tpu_custom_call" | custom-call | flops 1000000000 | bytes 2097152 | tf_op jit(solution)/shard_map/delay_transform/pallas_call | solution.py:257
  32.8 1.6 %collective-permute-start.10 = (bf16[4,256,128]{2,1,0:T(8,128)(2,1)S(1)}, bf16[4,256,128]{2,1,0:T(8,128)(2,1)S(1)}, u32[]{:S(2)}, u32[]{:S(2)}) collective-permute-start(bf16[4,256,128]{2,1,0:T(8,128)(2,1)S(1)} %get-tuple-element.49), channel_id=1, source_target_pairs={{0,16},{8,24},{16,0},{24,8},{1,17},{9,25},{17,1},{25,9},{2,18},{10... | collective-permute-start | bytes 786440 | tf_op jit(solution)/shard_map/ppermute | solution.py:34
  34.3 2.0 %collective-permute-start.11 = (bf16[4,256,128]{2,1,0:T(8,128)(2,1)S(1)}, bf16[4,256,128]{2,1,0:T(8,128)(2,1)S(1)}, u32[]{:S(2)}, u32[]{:S(2)}) collective-permute-start(bf16[4,256,128]{2,1,0:T(8,128)(2,1)S(1)} %get-tuple-element.50), channel_id=1, source_target_pairs={{0,24},{8,0},{16,8},{24,16},{1,25},{9,1},{17,9},{25,17},{2,26},{10... | collective-permute-start | bytes 786440 | tf_op jit(solution)/shard_map/ppermute | solution.py:34
  36.3 0.0 collective-permute-start.9
  36.4 3.6 %collective-permute-done.1.refs_2_ = bf16[4,256,128]{2,1,0:T(8,128)(2,1)S(1)} collective-permute-done((bf16[4,256,128]{2,1,0:T(8,128)(2,1)S(1)}, bf16[4,256,128]{2,1,0:T(8,128)(2,1)S(1)}, u32[]{:S(2)}, u32[]{:S(2)}) %collective-permute-start.1) | collective-permute-done | bytes 262176 | tf_op jit(solution)/shard_map/ppermute | solution.py:34
  40.0 0.5 collective-permute-done.2.refs_3_
  40.4 2.0 %delay_transform.4 = (bf16[4,256,128]{2,1,0:T(8,128)(2,1)S(1)}, bf16[4,256,128]{2,1,0:T(8,128)(2,1)S(1)}, bf16[4,256,128]{2,1,0:T(8,128)(2,1)S(1)}, bf16[4,256,128]{2,1,0:T(8,128)(2,1)S(1)}) custom-call(s32[1]{0:T(128)} %bitcast.me_ref, bf16[4,512,512]{2,1,0:T(8,128)(2,1)S(1)} %copy-done.1, bf16[4,256,128]{2,1,0:T(8,128)(2,1)S(1)} %copy-done.5, ...), custom_call_target="tpu_custom_call" | custom-call | flops 1000000000 | bytes 2097152 | tf_op jit(solution)/shard_map/delay_transform/pallas_call | solution.py:257
  42.5 7.0 %collective-permute-start.3 = (bf16[4,256,128]{2,1,0:T(8,128)(2,1)S(1)}, bf16[4,256,128]{2,1,0:T(8,128)(2,1)S(1)}, u32[]{:S(2)}, u32[]{:S(2)}) collective-permute-start(bf16[4,256,128]{2,1,0:T(8,128)(2,1)S(1)} %get-tuple-element.40), channel_id=1, source_target_pairs={{0,8},{8,16},{16,24},{24,0},{1,9},{9,17},{17,25},{25,1},{2,10},{10... | collective-permute-start | bytes 786440 | tf_op jit(solution)/shard_map/ppermute | solution.py:34
  49.5 0.5 collective-permute-start.4
  50.0 0.0 collective-permute-done.10.refs_6_
  50.0 3.0 %collective-permute-start.5 = (bf16[4,256,128]{2,1,0:T(8,128)(2,1)S(1)}, bf16[4,256,128]{2,1,0:T(8,128)(2,1)S(1)}, u32[]{:S(2)}, u32[]{:S(2)}) collective-permute-start(bf16[4,256,128]{2,1,0:T(8,128)(2,1)S(1)} %get-tuple-element.42), channel_id=1, source_target_pairs={{0,24},{8,0},{16,8},{24,16},{1,25},{9,1},{17,9},{25,17},{2,26},{10... | collective-permute-start | bytes 786440 | tf_op jit(solution)/shard_map/ppermute | solution.py:34
  53.0 4.2 %collective-permute-done.3.refs_1_ = bf16[4,256,128]{2,1,0:T(8,128)(2,1)S(1)} collective-permute-done((bf16[4,256,128]{2,1,0:T(8,128)(2,1)S(1)}, bf16[4,256,128]{2,1,0:T(8,128)(2,1)S(1)}, u32[]{:S(2)}, u32[]{:S(2)}) %collective-permute-start.3) | collective-permute-done | bytes 262176 | tf_op jit(solution)/shard_map/ppermute | solution.py:34
  57.3 5.1 %collective-permute-done.4.refs_2_ = bf16[4,256,128]{2,1,0:T(8,128)(2,1)S(1)} collective-permute-done((bf16[4,256,128]{2,1,0:T(8,128)(2,1)S(1)}, bf16[4,256,128]{2,1,0:T(8,128)(2,1)S(1)}, u32[]{:S(2)}, u32[]{:S(2)}) %collective-permute-start.4) | collective-permute-done | bytes 262176 | tf_op jit(solution)/shard_map/ppermute | solution.py:34
  62.4 0.2 collective-permute-done.5.refs_3_
  62.6 0.5 join_pieces.1
  63.0 1.3 %copy-done = bf16[8,1024,128]{2,1,0:T(8,128)(2,1)} copy-done((bf16[8,1024,128]{2,1,0:T(8,128)(2,1)}, bf16[8,1024,128]{2,1,0:T(8,128)(2,1)S(1)}, u32[]{:S(2)}) %copy-start) | copy-done | bytes 2097176
  64.4 0.0 all-to-all-done.refs_0_
  64.4 4.9 %all-to-all-start.1 = ((bf16[8,1024,128]{2,1,0:T(8,128)(2,1)}), bf16[8,1024,128]{2,1,0:T(8,128)(2,1)}, u32[]{:S(2)}, u32[]{:S(2)}) async-start(bf16[8,1024,128]{2,1,0:T(8,128)(2,1)} %copy-done), calls=%async_computation.1 | async-start | bytes 4194304 | tf_op jit(solution)/shard_map/all_to_all | solution.py:519
  69.3 1.1 fusion.3
  70.4 1.6 %collective-permute-start.15 = (bf16[4,256,128]{2,1,0:T(8,128)(2,1)}, bf16[4,256,128]{2,1,0:T(8,128)(2,1)S(1)}, u32[]{:S(2)}, u32[]{:S(2)}) collective-permute-start(bf16[4,256,128]{2,1,0:T(8,128)(2,1)} %get-tuple-element.67), channel_id=1, source_target_pairs={{0,8},{8,16},{16,24},{24,0},{1,9},{9,17},{17,25},{25,1},{2,10},{10... | collective-permute-start | bytes 786440 | tf_op jit(solution)/shard_map/ppermute | solution.py:34
  72.0 0.5 collective-permute-start.16
  72.5 2.1 %collective-permute-start.17 = (bf16[4,256,128]{2,1,0:T(8,128)(2,1)}, bf16[4,256,128]{2,1,0:T(8,128)(2,1)S(1)}, u32[]{:S(2)}, u32[]{:S(2)}) collective-permute-start(bf16[4,256,128]{2,1,0:T(8,128)(2,1)} %get-tuple-element.65), channel_id=1, source_target_pairs={{0,24},{8,0},{16,8},{24,16},{1,25},{9,1},{17,9},{25,17},{2,26},{10... | collective-permute-start | bytes 786440 | tf_op jit(solution)/shard_map/ppermute | solution.py:34
  74.7 0.1 reshape.34
  74.8 1.0 pad_maximum_fusion
  75.8 0.1 collective-permute-start.12
  75.9 1.4 %collective-permute-start.13 = (bf16[4,272,128]{2,1,0:T(8,128)(2,1)S(1)}, bf16[4,272,128]{2,1,0:T(8,128)(2,1)S(1)}, u32[]{:S(2)}, u32[]{:S(2)}) collective-permute-start(bf16[4,272,128]{2,1,0:T(8,128)(2,1)S(1)} %get-tuple-element.76), channel_id=1, source_target_pairs={{0,16},{8,24},{16,0},{24,8},{1,17},{9,25},{17,1},{25,9},{2,18},{10... | collective-permute-start | bytes 835592 | tf_op jit(solution)/shard_map/ppermute | solution.py:34
  77.3 3.4 %collective-permute-done.15.refs_1_ = bf16[4,256,128]{2,1,0:T(8,128)(2,1)S(1)} collective-permute-done((bf16[4,256,128]{2,1,0:T(8,128)(2,1)}, bf16[4,256,128]{2,1,0:T(8,128)(2,1)S(1)}, u32[]{:S(2)}, u32[]{:S(2)}) %collective-permute-start.15) | collective-permute-done | bytes 262176 | tf_op jit(solution)/shard_map/ppermute | solution.py:34
  80.7 0.6 collective-permute-start.14
  81.3 5.0 %collective-permute-done.16.refs_2_ = bf16[4,256,128]{2,1,0:T(8,128)(2,1)S(1)} collective-permute-done((bf16[4,256,128]{2,1,0:T(8,128)(2,1)}, bf16[4,256,128]{2,1,0:T(8,128)(2,1)S(1)}, u32[]{:S(2)}, u32[]{:S(2)}) %collective-permute-start.16) | collective-permute-done | bytes 262176 | tf_op jit(solution)/shard_map/ppermute | solution.py:34
  86.3 1.6 %copy-done.2 = bf16[4,512,512]{2,1,0:T(8,128)(2,1)S(1)} copy-done((bf16[4,512,512]{2,1,0:T(8,128)(2,1)S(1)}, bf16[4,512,512]{2,1,0:T(8,128)(2,1)}, u32[]{:S(2)}) %copy-start.2) | copy-done | bytes 2097176
  87.9 2.1 %delay_transform.7 = (bf16[4,256,128]{2,1,0:T(8,128)(2,1)S(1)}, bf16[4,256,128]{2,1,0:T(8,128)(2,1)S(1)}, bf16[4,256,128]{2,1,0:T(8,128)(2,1)}, bf16[4,256,128]{2,1,0:T(8,128)(2,1)S(1)}) custom-call(s32[1]{0:T(128)} %bitcast.me_ref, bf16[4,512,512]{2,1,0:T(8,128)(2,1)S(1)} %copy-done.2, bf16[8,1040,128]{2,1,0:T(8,128)(2,1)S(1)} %all-to-all-done.refs_0_, ...), custom_call_target="tpu_custom_call" | custom-call | flops 1000000000 | bytes 2097152 | tf_op jit(solution)/shard_map/delay_transform/pallas_call | solution.py:257
  90.0 1.9 %collective-permute-start.19 = (bf16[4,256,128]{2,1,0:T(8,128)(2,1)S(1)}, bf16[4,256,128]{2,1,0:T(8,128)(2,1)S(1)}, u32[]{:S(2)}, u32[]{:S(2)}) collective-permute-start(bf16[4,256,128]{2,1,0:T(8,128)(2,1)S(1)} %get-tuple-element.58), channel_id=1, source_target_pairs={{0,8},{8,16},{16,24},{24,0},{1,9},{9,17},{17,25},{25,1},{2,10},{10... | collective-permute-start | bytes 786440 | tf_op jit(solution)/shard_map/ppermute | solution.py:34
  91.9 0.7 collective-permute-start.21
  92.6 1.7 %collective-permute-start.23 = (bf16[4,256,128]{2,1,0:T(8,128)(2,1)S(1)}, bf16[4,256,128]{2,1,0:T(8,128)(2,1)S(1)}, u32[]{:S(2)}, u32[]{:S(2)}) collective-permute-start(bf16[4,256,128]{2,1,0:T(8,128)(2,1)S(1)} %get-tuple-element.62), channel_id=1, source_target_pairs={{0,24},{8,0},{16,8},{24,16},{1,25},{9,1},{17,9},{25,17},{2,26},{10... | collective-permute-start | bytes 786440 | tf_op jit(solution)/shard_map/ppermute | solution.py:34
  94.3 3.9 %collective-permute-done.13.refs_2_ = bf16[4,272,128]{2,1,0:T(8,128)(2,1)S(1)} collective-permute-done((bf16[4,272,128]{2,1,0:T(8,128)(2,1)S(1)}, bf16[4,272,128]{2,1,0:T(8,128)(2,1)S(1)}, u32[]{:S(2)}, u32[]{:S(2)}) %collective-permute-start.13) | collective-permute-done | bytes 278560 | tf_op jit(solution)/shard_map/ppermute | solution.py:34
  98.2 2.0 %delay_transform.6 = (bf16[4,256,128]{2,1,0:T(8,128)(2,1)S(1)}, bf16[4,256,128]{2,1,0:T(8,128)(2,1)}, bf16[4,256,128]{2,1,0:T(8,128)(2,1)}, bf16[4,256,128]{2,1,0:T(8,128)(2,1)}) custom-call(s32[1]{0:T(128)} %bitcast.me_ref, bf16[4,512,512]{2,1,0:T(8,128)(2,1)S(1)} %copy-done.2, bf16[8,1040,128]{2,1,0:T(8,128)(2,1)S(1)} %all-to-all-done.refs_0_, ...), custom_call_target="tpu_custom_call" | custom-call | flops 1000000000 | bytes 2097152 | tf_op jit(solution)/shard_map/delay_transform/pallas_call | solution.py:257
  100.3 0.7 copy-done.3
  101.0 1.9 %collective-permute-start.18 = (bf16[4,256,128]{2,1,0:T(8,128)(2,1)}, bf16[4,256,128]{2,1,0:T(8,128)(2,1)S(1)}, u32[]{:S(2)}, u32[]{:S(2)}) collective-permute-start(bf16[4,256,128]{2,1,0:T(8,128)(2,1)} %get-tuple-element.57), channel_id=1, source_target_pairs={{0,8},{8,16},{16,24},{24,0},{1,9},{9,17},{17,25},{25,1},{2,10},{10... | collective-permute-start | bytes 786440 | tf_op jit(solution)/shard_map/ppermute | solution.py:34
  102.9 0.3 collective-permute-start.20
  103.2 0.7 collective-permute-done.19.refs_3_
  103.9 1.3 %collective-permute-start.22 = (bf16[4,256,128]{2,1,0:T(8,128)(2,1)}, bf16[4,256,128]{2,1,0:T(8,128)(2,1)S(1)}, u32[]{:S(2)}, u32[]{:S(2)}) collective-permute-start(bf16[4,256,128]{2,1,0:T(8,128)(2,1)} %get-tuple-element.61), channel_id=1, source_target_pairs={{0,24},{8,0},{16,8},{24,16},{1,25},{9,1},{17,9},{25,17},{2,26},{10... | collective-permute-start | bytes 786440 | tf_op jit(solution)/shard_map/ppermute | solution.py:34
  105.2 1.9 %pair_weights.1 = (bf16[512,512]{1,0:T(8,128)(2,1)S(1)}, f32[64,512]{1,0:T(8,128)S(1)}) custom-call(s32[1]{0:T(128)} %bitcast.me_ref, bf16[4,16,128]{2,1,0:T(8,128)(2,1)S(1)} %bitcast.13, bf16[4,272,128]{2,1,0:T(8,128)(2,1)S(1)} %collective-permute-done.12.refs_1_, bf16[4,272,128]{2,1,0:T(8,128)(2,1)S(1)} %collective-permute-done.13.refs_2_, ...), custom_call_target="tpu_custom_call" | custom-call | flops 536870912 | bytes 1048576 | tf_op jit(solution)/shard_map/pair_weights/pallas_call | solution.py:376
  107.2 11.2 %all-to-all-done.1.refs_0_ = bf16[8,1024,128]{2,1,0:T(8,128)(2,1)} async-done(((bf16[8,1024,128]{2,1,0:T(8,128)(2,1)}), bf16[8,1024,128]{2,1,0:T(8,128)(2,1)}, u32[]{:S(2)}, u32[]{:S(2)}) %all-to-all-start.1) | async-done | bytes 2097184 | tf_op jit(solution)/shard_map/all_to_all | solution.py:519
  118.4 3.1 %pair_sums.2.before_ref = f32[64,256]{1,0:T(8,128)S(1)} custom-call(bf16[512,512]{1,0:T(8,128)(2,1)S(1)} %get-tuple-element.52.mix_ref, f32[64,512]{1,0:T(8,128)S(1)} %get-tuple-element.53.group_ref, f32[64,256]{1,0:T(8,128)S(1)} %broadcast_in_dim.3.before_ref, bf16[8,1024,128]{2,1,0:T(8,128)(2,1)} %all-to-all-done.1.refs_0_), custom_call_target="tpu_custom_call" | custom-call | flops 1073741824 | bytes 2097152 | tf_op jit(solution)/shard_map/pair_sums/pallas_call | solution.py:450
  121.6 1.5 %pair_sums.3 = f32[64,256]{1,0:T(8,128)S(1)} custom-call(bf16[512,512]{1,0:T(8,128)(2,1)S(1)} %get-tuple-element.52.mix_ref, f32[64,512]{1,0:T(8,128)S(1)} %get-tuple-element.53.group_ref, f32[64,256]{1,0:T(8,128)S(1)} %pair_sums.2.before_ref, bf16[4,256,128]{2,1,0:T(8,128)(2,1)S(1)} %copy-done.4, bf16[4,256,128]{2,1,0:T(8,128)(2,1)S(1)} %get-tuple-element.56.refs_1_, ...), custom_call_target="tpu_custom_call" | custom-call | flops 1073741824 | bytes 2097152 | tf_op jit(solution)/shard_map/pair_sums/pallas_call | solution.py:450
  123.2 1.7 %collective-permute-start.24 = (f32[16,256]{1,0:T(8,128)S(1)}, f32[16,256]{1,0:T(8,128)S(1)}, u32[]{:S(2)}, u32[]{:S(2)}) collective-permute-start(f32[16,256]{1,0:T(8,128)S(1)} %get-tuple-element.73), channel_id=1, source_target_pairs={{0,8},{8,16},{16,24},{24,0},{1,9},{9,17},{17,25},{25,1},{2,10},{10... | collective-permute-start | bytes 49160 | tf_op jit(solution)/shard_map/ppermute | solution.py:34
  124.8 0.5 collective-permute-start.25
  125.4 2.1 %collective-permute-start.26 = (f32[16,256]{1,0:T(8,128)S(1)}, f32[16,256]{1,0:T(8,128)S(1)}, u32[]{:S(2)}, u32[]{:S(2)}) collective-permute-start(f32[16,256]{1,0:T(8,128)S(1)} %get-tuple-element.71), channel_id=1, source_target_pairs={{0,24},{8,0},{16,8},{24,16},{1,25},{9,1},{17,9},{25,17},{2,26},{10... | collective-permute-start | bytes 49160 | tf_op jit(solution)/shard_map/ppermute | solution.py:34
  127.5 0.4 collective-permute-done.24.refs_1_
  127.9 0.7 collective-permute-done.25.refs_2_
  128.6 0.5 collective-permute-done.26.refs_3_
  129.1 1.1 interleave_delays.1
  (40 shorter events, 0.1 us)
Async XLA Ops:
  6.7 11.0 %copy-start.10 = (bf16[4,256,128]{2,1,0:T(8,128)(2,1)S(1)}, bf16[4,256,128]{2,1,0:T(8,128)(2,1)}, u32[]{:S(2)}) copy-start(bf16[4,256,128]{2,1,0:T(8,128)(2,1)} %get-tuple-element.36) | copy-start | bytes 786436
  6.7 11.6 %copy-start.9 = (bf16[4,256,128]{2,1,0:T(8,128)(2,1)S(1)}, bf16[4,256,128]{2,1,0:T(8,128)(2,1)}, u32[]{:S(2)}) copy-start(bf16[4,256,128]{2,1,0:T(8,128)(2,1)} %get-tuple-element.37) | copy-start | bytes 786436
  6.7 16.8 %copy-start.8 = (bf16[4,256,128]{2,1,0:T(8,128)(2,1)S(1)}, bf16[4,256,128]{2,1,0:T(8,128)(2,1)}, u32[]{:S(2)}) copy-start(bf16[4,256,128]{2,1,0:T(8,128)(2,1)} %get-tuple-element.38) | copy-start | bytes 786436
  6.7 22.4 %copy-start.6 = (bf16[4,256,128]{2,1,0:T(8,128)(2,1)S(1)}, bf16[4,256,128]{2,1,0:T(8,128)(2,1)}, u32[]{:S(2)}) copy-start(bf16[4,256,128]{2,1,0:T(8,128)(2,1)} %get-tuple-element.43.refs_0_) | copy-start | bytes 786436
  6.7 33.7 %copy-start.5 = (bf16[4,256,128]{2,1,0:T(8,128)(2,1)S(1)}, bf16[4,256,128]{2,1,0:T(8,128)(2,1)}, u32[]{:S(2)}) copy-start(bf16[4,256,128]{2,1,0:T(8,128)(2,1)} %get-tuple-element.35.refs_0_) | copy-start | bytes 786436
  6.8 57.6 %all-to-all-start = ((bf16[8,1040,128]{2,1,0:T(8,128)(2,1)}), bf16[8,1040,128]{2,1,0:T(8,128)(2,1)S(1)}, u32[]{:S(2)}, u32[]{:S(2)}) async-start(bf16[8,1040,128]{2,1,0:T(8,128)(2,1)} %get-tuple-element.34), calls=%async_computation | async-start | bytes 4259840 | tf_op jit(solution)/shard_map/all_to_all | solution.py:513
  13.2 10.3 %collective-permute-start.6 = (bf16[4,256,128]{2,1,0:T(8,128)(2,1)}, bf16[4,256,128]{2,1,0:T(8,128)(2,1)S(1)}, u32[]{:S(2)}, u32[]{:S(2)}) collective-permute-start(bf16[4,256,128]{2,1,0:T(8,128)(2,1)} %get-tuple-element.44), channel_id=1, source_target_pairs={{0,8},{8,16},{16,24},{24,0},{1,9},{9,17},{17,25},{25,1},{2,10},{10... | collective-permute-start | bytes 786440 | tf_op jit(solution)/shard_map/ppermute | solution.py:34
  14.7 14.4 %collective-permute-start.7 = (bf16[4,256,128]{2,1,0:T(8,128)(2,1)}, bf16[4,256,128]{2,1,0:T(8,128)(2,1)S(1)}, u32[]{:S(2)}, u32[]{:S(2)}) collective-permute-start(bf16[4,256,128]{2,1,0:T(8,128)(2,1)} %get-tuple-element.45), channel_id=1, source_target_pairs={{0,16},{8,24},{16,0},{24,8},{1,17},{9,25},{17,1},{25,9},{2,18},{10... | collective-permute-start | bytes 786440 | tf_op jit(solution)/shard_map/ppermute | solution.py:34
  16.2 12.9 %collective-permute-start.8 = (bf16[4,256,128]{2,1,0:T(8,128)(2,1)}, bf16[4,256,128]{2,1,0:T(8,128)(2,1)S(1)}, u32[]{:S(2)}, u32[]{:S(2)}) collective-permute-start(bf16[4,256,128]{2,1,0:T(8,128)(2,1)} %get-tuple-element.46), channel_id=1, source_target_pairs={{0,24},{8,0},{16,8},{24,16},{1,25},{9,1},{17,9},{25,17},{2,26},{10... | collective-permute-start | bytes 786440 | tf_op jit(solution)/shard_map/ppermute | solution.py:34
  17.7 18.7 %collective-permute-start = (bf16[4,256,128]{2,1,0:T(8,128)(2,1)S(1)}, bf16[4,256,128]{2,1,0:T(8,128)(2,1)S(1)}, u32[]{:S(2)}, u32[]{:S(2)}) collective-permute-start(bf16[4,256,128]{2,1,0:T(8,128)(2,1)S(1)} %copy-done.10), channel_id=1, source_target_pairs={{0,8},{8,16},{16,24},{24,0},{1,9},{9,17},{17,25},{25,1},{2,10},{10... | collective-permute-start | bytes 786440 | tf_op jit(solution)/shard_map/ppermute | solution.py:34
  18.3 21.7 %collective-permute-start.1 = (bf16[4,256,128]{2,1,0:T(8,128)(2,1)S(1)}, bf16[4,256,128]{2,1,0:T(8,128)(2,1)S(1)}, u32[]{:S(2)}, u32[]{:S(2)}) collective-permute-start(bf16[4,256,128]{2,1,0:T(8,128)(2,1)S(1)} %copy-done.9), channel_id=1, source_target_pairs={{0,16},{8,24},{16,0},{24,8},{1,17},{9,25},{17,1},{25,9},{2,18},{10... | collective-permute-start | bytes 786440 | tf_op jit(solution)/shard_map/ppermute | solution.py:34
  23.5 16.9 %collective-permute-start.2 = (bf16[4,256,128]{2,1,0:T(8,128)(2,1)S(1)}, bf16[4,256,128]{2,1,0:T(8,128)(2,1)S(1)}, u32[]{:S(2)}, u32[]{:S(2)}) collective-permute-start(bf16[4,256,128]{2,1,0:T(8,128)(2,1)S(1)} %copy-done.8), channel_id=1, source_target_pairs={{0,24},{8,0},{16,8},{24,16},{1,25},{9,1},{17,9},{25,17},{2,26},{10... | collective-permute-start | bytes 786440 | tf_op jit(solution)/shard_map/ppermute | solution.py:34
  29.2 1.6 %copy-start.1 = (bf16[4,512,512]{2,1,0:T(8,128)(2,1)S(1)}, bf16[4,512,512]{2,1,0:T(8,128)(2,1)}, u32[]{:S(2)}) copy-start(bf16[4,512,512]{2,1,0:T(8,128)(2,1)} %constant.14.clone.matrix_hbm) | copy-start | bytes 6291460
  32.8 17.2 %collective-permute-start.10 = (bf16[4,256,128]{2,1,0:T(8,128)(2,1)S(1)}, bf16[4,256,128]{2,1,0:T(8,128)(2,1)S(1)}, u32[]{:S(2)}, u32[]{:S(2)}) collective-permute-start(bf16[4,256,128]{2,1,0:T(8,128)(2,1)S(1)} %get-tuple-element.49), channel_id=1, source_target_pairs={{0,16},{8,24},{16,0},{24,8},{1,17},{9,25},{17,1},{25,9},{2,18},{10... | collective-permute-start | bytes 786440 | tf_op jit(solution)/shard_map/ppermute | solution.py:34
  34.3 18.7 %collective-permute-start.11 = (bf16[4,256,128]{2,1,0:T(8,128)(2,1)S(1)}, bf16[4,256,128]{2,1,0:T(8,128)(2,1)S(1)}, u32[]{:S(2)}, u32[]{:S(2)}) collective-permute-start(bf16[4,256,128]{2,1,0:T(8,128)(2,1)S(1)} %get-tuple-element.50), channel_id=1, source_target_pairs={{0,24},{8,0},{16,8},{24,16},{1,25},{9,1},{17,9},{25,17},{2,26},{10... | collective-permute-start | bytes 786440 | tf_op jit(solution)/shard_map/ppermute | solution.py:34
  36.3 16.7 %collective-permute-start.9 = (bf16[4,256,128]{2,1,0:T(8,128)(2,1)S(1)}, bf16[4,256,128]{2,1,0:T(8,128)(2,1)S(1)}, u32[]{:S(2)}, u32[]{:S(2)}) collective-permute-start(bf16[4,256,128]{2,1,0:T(8,128)(2,1)S(1)} %get-tuple-element.48), channel_id=1, source_target_pairs={{0,8},{8,16},{16,24},{24,0},{1,9},{9,17},{17,25},{25,1},{2,10},{10... | collective-permute-start | bytes 786440 | tf_op jit(solution)/shard_map/ppermute | solution.py:34
  42.5 14.8 %collective-permute-start.3 = (bf16[4,256,128]{2,1,0:T(8,128)(2,1)S(1)}, bf16[4,256,128]{2,1,0:T(8,128)(2,1)S(1)}, u32[]{:S(2)}, u32[]{:S(2)}) collective-permute-start(bf16[4,256,128]{2,1,0:T(8,128)(2,1)S(1)} %get-tuple-element.40), channel_id=1, source_target_pairs={{0,8},{8,16},{16,24},{24,0},{1,9},{9,17},{17,25},{25,1},{2,10},{10... | collective-permute-start | bytes 786440 | tf_op jit(solution)/shard_map/ppermute | solution.py:34
  49.5 12.9 %collective-permute-start.4 = (bf16[4,256,128]{2,1,0:T(8,128)(2,1)S(1)}, bf16[4,256,128]{2,1,0:T(8,128)(2,1)S(1)}, u32[]{:S(2)}, u32[]{:S(2)}) collective-permute-start(bf16[4,256,128]{2,1,0:T(8,128)(2,1)S(1)} %get-tuple-element.41), channel_id=1, source_target_pairs={{0,16},{8,24},{16,0},{24,8},{1,17},{9,25},{17,1},{25,9},{2,18},{10... | collective-permute-start | bytes 786440 | tf_op jit(solution)/shard_map/ppermute | solution.py:34
  50.0 12.5 %collective-permute-start.5 = (bf16[4,256,128]{2,1,0:T(8,128)(2,1)S(1)}, bf16[4,256,128]{2,1,0:T(8,128)(2,1)S(1)}, u32[]{:S(2)}, u32[]{:S(2)}) collective-permute-start(bf16[4,256,128]{2,1,0:T(8,128)(2,1)S(1)} %get-tuple-element.42), channel_id=1, source_target_pairs={{0,24},{8,0},{16,8},{24,16},{1,25},{9,1},{17,9},{25,17},{2,26},{10... | collective-permute-start | bytes 786440 | tf_op jit(solution)/shard_map/ppermute | solution.py:34
  63.0 1.3 %copy-start = (bf16[8,1024,128]{2,1,0:T(8,128)(2,1)}, bf16[8,1024,128]{2,1,0:T(8,128)(2,1)S(1)}, u32[]{:S(2)}) copy-start(bf16[8,1024,128]{2,1,0:T(8,128)(2,1)S(1)} %join_pieces.1) | copy-start | bytes 6291460
  64.4 4.9 %copy-start.7 = (s32[256,2]{0,1:T(2,128)S(1)}, s32[256,2]{0,1:T(2,128)}, u32[]{:S(2)}) copy-start(s32[256,2]{0,1:T(2,128)} %param.11) | copy-start | bytes 6148
  64.4 4.9 %copy-start.11 = (s32[128]{0:T(128)S(1)}, s32[128]{0:T(128)}, u32[]{:S(2)}) copy-start(s32[128]{0:T(128)} %param.10) | copy-start | bytes 1540
  64.4 54.0 %all-to-all-start.1 = ((bf16[8,1024,128]{2,1,0:T(8,128)(2,1)}), bf16[8,1024,128]{2,1,0:T(8,128)(2,1)}, u32[]{:S(2)}, u32[]{:S(2)}) async-start(bf16[8,1024,128]{2,1,0:T(8,128)(2,1)} %copy-done), calls=%async_computation.1 | async-start | bytes 4194304 | tf_op jit(solution)/shard_map/all_to_all | solution.py:519
  70.4 10.3 %collective-permute-start.15 = (bf16[4,256,128]{2,1,0:T(8,128)(2,1)}, bf16[4,256,128]{2,1,0:T(8,128)(2,1)S(1)}, u32[]{:S(2)}, u32[]{:S(2)}) collective-permute-start(bf16[4,256,128]{2,1,0:T(8,128)(2,1)} %get-tuple-element.67), channel_id=1, source_target_pairs={{0,8},{8,16},{16,24},{24,0},{1,9},{9,17},{17,25},{25,1},{2,10},{10... | collective-permute-start | bytes 786440 | tf_op jit(solution)/shard_map/ppermute | solution.py:34
  72.0 14.3 %collective-permute-start.16 = (bf16[4,256,128]{2,1,0:T(8,128)(2,1)}, bf16[4,256,128]{2,1,0:T(8,128)(2,1)S(1)}, u32[]{:S(2)}, u32[]{:S(2)}) collective-permute-start(bf16[4,256,128]{2,1,0:T(8,128)(2,1)} %get-tuple-element.66), channel_id=1, source_target_pairs={{0,16},{8,24},{16,0},{24,8},{1,17},{9,25},{17,1},{25,9},{2,18},{10... | collective-permute-start | bytes 786440 | tf_op jit(solution)/shard_map/ppermute | solution.py:34
  72.5 13.8 %collective-permute-start.17 = (bf16[4,256,128]{2,1,0:T(8,128)(2,1)}, bf16[4,256,128]{2,1,0:T(8,128)(2,1)S(1)}, u32[]{:S(2)}, u32[]{:S(2)}) collective-permute-start(bf16[4,256,128]{2,1,0:T(8,128)(2,1)} %get-tuple-element.65), channel_id=1, source_target_pairs={{0,24},{8,0},{16,8},{24,16},{1,25},{9,1},{17,9},{25,17},{2,26},{10... | collective-permute-start | bytes 786440 | tf_op jit(solution)/shard_map/ppermute | solution.py:34
  75.8 16.8 %collective-permute-start.12 = (bf16[4,272,128]{2,1,0:T(8,128)(2,1)S(1)}, bf16[4,272,128]{2,1,0:T(8,128)(2,1)S(1)}, u32[]{:S(2)}, u32[]{:S(2)}) collective-permute-start(bf16[4,272,128]{2,1,0:T(8,128)(2,1)S(1)} %get-tuple-element.77), channel_id=1, source_target_pairs={{0,8},{8,16},{16,24},{24,0},{1,9},{9,17},{17,25},{25,1},{2,10},{10... | collective-permute-start | bytes 835592 | tf_op jit(solution)/shard_map/ppermute | solution.py:34
  75.9 22.4 %collective-permute-start.13 = (bf16[4,272,128]{2,1,0:T(8,128)(2,1)S(1)}, bf16[4,272,128]{2,1,0:T(8,128)(2,1)S(1)}, u32[]{:S(2)}, u32[]{:S(2)}) collective-permute-start(bf16[4,272,128]{2,1,0:T(8,128)(2,1)S(1)} %get-tuple-element.76), channel_id=1, source_target_pairs={{0,16},{8,24},{16,0},{24,8},{1,17},{9,25},{17,1},{25,9},{2,18},{10... | collective-permute-start | bytes 835592 | tf_op jit(solution)/shard_map/ppermute | solution.py:34
  80.7 17.6 %collective-permute-start.14 = (bf16[4,272,128]{2,1,0:T(8,128)(2,1)S(1)}, bf16[4,272,128]{2,1,0:T(8,128)(2,1)S(1)}, u32[]{:S(2)}, u32[]{:S(2)}) collective-permute-start(bf16[4,272,128]{2,1,0:T(8,128)(2,1)S(1)} %get-tuple-element.75), channel_id=1, source_target_pairs={{0,24},{8,0},{16,8},{24,16},{1,25},{9,1},{17,9},{25,17},{2,26},{10... | collective-permute-start | bytes 835592 | tf_op jit(solution)/shard_map/ppermute | solution.py:34
  86.3 1.6 %copy-start.2 = (bf16[4,512,512]{2,1,0:T(8,128)(2,1)S(1)}, bf16[4,512,512]{2,1,0:T(8,128)(2,1)}, u32[]{:S(2)}) copy-start(bf16[4,512,512]{2,1,0:T(8,128)(2,1)} %constant.14.clone.matrix_hbm) | copy-start | bytes 6291460
  90.0 13.9 %collective-permute-start.19 = (bf16[4,256,128]{2,1,0:T(8,128)(2,1)S(1)}, bf16[4,256,128]{2,1,0:T(8,128)(2,1)S(1)}, u32[]{:S(2)}, u32[]{:S(2)}) collective-permute-start(bf16[4,256,128]{2,1,0:T(8,128)(2,1)S(1)} %get-tuple-element.58), channel_id=1, source_target_pairs={{0,8},{8,16},{16,24},{24,0},{1,9},{9,17},{17,25},{25,1},{2,10},{10... | collective-permute-start | bytes 786440 | tf_op jit(solution)/shard_map/ppermute | solution.py:34
  91.9 29.6 %collective-permute-start.21 = (bf16[4,256,128]{2,1,0:T(8,128)(2,1)}, bf16[4,256,128]{2,1,0:T(8,128)(2,1)S(1)}, u32[]{:S(2)}, u32[]{:S(2)}) collective-permute-start(bf16[4,256,128]{2,1,0:T(8,128)(2,1)} %get-tuple-element.60), channel_id=1, source_target_pairs={{0,16},{8,24},{16,0},{24,8},{1,17},{9,25},{17,1},{25,9},{2,18},{10... | collective-permute-start | bytes 786440 | tf_op jit(solution)/shard_map/ppermute | solution.py:34
  92.6 28.9 %collective-permute-start.23 = (bf16[4,256,128]{2,1,0:T(8,128)(2,1)S(1)}, bf16[4,256,128]{2,1,0:T(8,128)(2,1)S(1)}, u32[]{:S(2)}, u32[]{:S(2)}) collective-permute-start(bf16[4,256,128]{2,1,0:T(8,128)(2,1)S(1)} %get-tuple-element.62), channel_id=1, source_target_pairs={{0,24},{8,0},{16,8},{24,16},{1,25},{9,1},{17,9},{25,17},{2,26},{10... | collective-permute-start | bytes 786440 | tf_op jit(solution)/shard_map/ppermute | solution.py:34
  100.3 0.7 copy-start.3
  101.0 20.6 %collective-permute-start.18 = (bf16[4,256,128]{2,1,0:T(8,128)(2,1)}, bf16[4,256,128]{2,1,0:T(8,128)(2,1)S(1)}, u32[]{:S(2)}, u32[]{:S(2)}) collective-permute-start(bf16[4,256,128]{2,1,0:T(8,128)(2,1)} %get-tuple-element.57), channel_id=1, source_target_pairs={{0,8},{8,16},{16,24},{24,0},{1,9},{9,17},{17,25},{25,1},{2,10},{10... | collective-permute-start | bytes 786440 | tf_op jit(solution)/shard_map/ppermute | solution.py:34
  102.9 18.7 %collective-permute-start.20 = (bf16[4,256,128]{2,1,0:T(8,128)(2,1)}, bf16[4,256,128]{2,1,0:T(8,128)(2,1)S(1)}, u32[]{:S(2)}, u32[]{:S(2)}) collective-permute-start(bf16[4,256,128]{2,1,0:T(8,128)(2,1)} %get-tuple-element.59), channel_id=1, source_target_pairs={{0,16},{8,24},{16,0},{24,8},{1,17},{9,25},{17,1},{25,9},{2,18},{10... | collective-permute-start | bytes 786440 | tf_op jit(solution)/shard_map/ppermute | solution.py:34
  103.9 17.7 %collective-permute-start.22 = (bf16[4,256,128]{2,1,0:T(8,128)(2,1)}, bf16[4,256,128]{2,1,0:T(8,128)(2,1)S(1)}, u32[]{:S(2)}, u32[]{:S(2)}) collective-permute-start(bf16[4,256,128]{2,1,0:T(8,128)(2,1)} %get-tuple-element.61), channel_id=1, source_target_pairs={{0,24},{8,0},{16,8},{24,16},{1,25},{9,1},{17,9},{25,17},{2,26},{10... | collective-permute-start | bytes 786440 | tf_op jit(solution)/shard_map/ppermute | solution.py:34
  107.2 14.4 %copy-start.4 = (bf16[4,256,128]{2,1,0:T(8,128)(2,1)S(1)}, bf16[4,256,128]{2,1,0:T(8,128)(2,1)}, u32[]{:S(2)}) copy-start(bf16[4,256,128]{2,1,0:T(8,128)(2,1)} %copy-done.3) | copy-start | bytes 786436
  123.2 4.7 %collective-permute-start.24 = (f32[16,256]{1,0:T(8,128)S(1)}, f32[16,256]{1,0:T(8,128)S(1)}, u32[]{:S(2)}, u32[]{:S(2)}) collective-permute-start(f32[16,256]{1,0:T(8,128)S(1)} %get-tuple-element.73), channel_id=1, source_target_pairs={{0,8},{8,16},{16,24},{24,0},{1,9},{9,17},{17,25},{25,1},{2,10},{10... | collective-permute-start | bytes 49160 | tf_op jit(solution)/shard_map/ppermute | solution.py:34
  124.8 3.7 %collective-permute-start.25 = (f32[16,256]{1,0:T(8,128)S(1)}, f32[16,256]{1,0:T(8,128)S(1)}, u32[]{:S(2)}, u32[]{:S(2)}) collective-permute-start(f32[16,256]{1,0:T(8,128)S(1)} %get-tuple-element.72), channel_id=1, source_target_pairs={{0,16},{8,24},{16,0},{24,8},{1,17},{9,25},{17,1},{25,9},{2,18},{10... | collective-permute-start | bytes 49160 | tf_op jit(solution)/shard_map/ppermute | solution.py:34
  125.4 3.7 %collective-permute-start.26 = (f32[16,256]{1,0:T(8,128)S(1)}, f32[16,256]{1,0:T(8,128)S(1)}, u32[]{:S(2)}, u32[]{:S(2)}) collective-permute-start(f32[16,256]{1,0:T(8,128)S(1)} %get-tuple-element.71), channel_id=1, source_target_pairs={{0,24},{8,0},{16,8},{24,16},{1,25},{9,1},{17,9},{25,17},{2,26},{10... | collective-permute-start | bytes 49160 | tf_op jit(solution)/shard_map/ppermute | solution.py:34
